TPU v7x, 512 devices: a whole 4x8x8 slice. The times are simulated.
512 devices in a mesh: dp: 64 (over z, y_lo, core), tensor: 8 (over y_hi, x).
Axes of the slice: x: 4, y: 8 (y_hi: 2, y_lo: 4; y = y_hi * 4 + y_lo), z: 8, core: 2. Of those that a mesh axis runs over, the one named last changes fastest.
Arguments:
- hidden_acts: bfloat16 [26624, 28672], P('dp', 'tensor'), may hold values from -6 to 6
- out_grads: bfloat16 [26624, 8192], P('dp', 'tensor'), may hold values from -6 to 6
- left_factors: bfloat16 [64, 28672, 128], P('dp', 'tensor'), may hold values from -0.03125 to 0.03125
- right_factors: bfloat16 [64, 8192, 128], P('dp', 'tensor'), may hold values from -0.0625 to 0.0625
- doc_tokens: int32 [64, 8], P('dp'), may hold values from 1 to 104, 416 in all within a row
- owners: int32 [2], replicated, may hold values from 0 to 63
Outputs:
- scores: float32 [512, 8], P('dp')
Inputs may be any that keep to these rules, and one draw needn't show every extreme that they name: `doc_tokens`: each dp index's counts sum to 416; the largest of each row is 104.
All inputs are finite; a program needn't handle non-finite values.
Results may differ from a plain program's by a relative error of at most 0.0003.
Values may be sent and summed in bfloat16 or wider, within the bound.
No kernel may reach another device: no remote copies, remote signals or barrier semaphores. Data moves between devices by JAX's collectives and lax.ppermute only.
A program may use at most 64 MiB of HBM per device.

v0:
```python
import jax
import jax.numpy as jnp
from jax import lax
from jax.sharding import PartitionSpec as P

QB = 4
RANK = 32


def spread(block, axis, holder):
    block = jnp.where(lax.axis_index(axis) == holder, block, jnp.zeros_like(block))
    return lax.psum(block, axis)


def shards(hidden_acts, out_grads, left_factors, right_factors, doc_tokens, owners):
    tok_rows = hidden_acts.shape[0]
    proj_hs = []
    proj_gs = []
    for batch in range(2):
        left_now, right_now = (
            spread(left_factors[0], "dp", owners[batch]),
            spread(right_factors[0], "dp", owners[batch]),
        )
        proj_hs.append(jnp.dot(hidden_acts, left_now, preferred_element_type=jnp.float32))
        proj_gs.append(jnp.dot(out_grads, right_now, preferred_element_type=jnp.float32))
    proj_h = jnp.concatenate(proj_hs, axis=1)
    proj_g = jnp.concatenate(proj_gs, axis=1)
    full_h, full_g = lax.psum((proj_h, proj_g), "tensor")
    token_score = (full_h * full_g).reshape(tok_rows, 2 * QB, RANK).sum(axis=2)
    counts = doc_tokens[0]
    ends = jnp.cumsum(counts)
    starts = ends - counts
    places = jnp.arange(tok_rows, dtype=jnp.int32)
    inside = ((places[None, :] >= starts[:, None]) & (places[None, :] < ends[:, None])).astype(
        jnp.float32
    )
    summed = jnp.dot(
        inside, token_score, precision=lax.Precision.HIGHEST, preferred_element_type=jnp.float32
    )
    return summed / jnp.sqrt(jnp.float32(RANK * (tok_rows // 4)))


def solution(mesh):
    return jax.shard_map(
        shards,
        mesh=mesh,
        in_specs=(
            P("dp", "tensor"),
            P("dp", "tensor"),
            P("dp", "tensor", None),
            P("dp", "tensor", None),
            P("dp", None),
            P(),
        ),
        out_specs=P("dp", None),
        check_vma=False,
    )
```

profile of v0, /device:TPU:56, one launch (start us, length us, event | category | flops | bytes accessed | tf_op | source)
XLA Modules:
  0.0 693.6 jit_solution(15171026261886644606)
XLA Ops:
  6.5 0.0 copy-start
  6.5 0.0 all-reduce.7.cloned.1.call-start
  6.5 1.4 fusion.4
  9.2 2.5 select_bitcast_fusion.1
  11.7 1.8 select_bitcast_fusion.3
  13.5 0.0 all-reduce.7.cloned.1.call-update
  13.5 0.0 all-reduce.5.cloned.1.call-start
  13.6 536.1 %all-reduce.7.cloned.1.call-done = (bf16[3584,128]{1,0:T(8,128)(2,1)}, bf16[3584,128]{1,0:T(8,128)(2,1)}, bf16[1024,128]{1,0:T(8,128)(2,1)}, bf16[1024,128]{1,0:T(8,128)(2,1)}) async-done(((bf16[3584,128]{1,0:T(8,128)(2,1)}, bf16[3584,128]{1,0:T(8,128)(2,1)}, bf16[1024,128]{1,0:T(8,128)(2,1)}, bf16[1024,128]{1,0:T(8,128)(2,1)}), (bf16[3584,128]{1,0:T(8,128)(2,1)}, bf16[3584,128]{1,0:T(8,128)(2,1)}, ...) | async-done | bytes 2359312 | tf_op jit(solution)/shard_map/psum | solution.py:12
  549.6 1.6 convolution_bitcast_fusion
  551.2 0.0 copy-start.1
  551.3 1.7 convolution_bitcast_fusion.1
  552.9 0.0 copy-done
  552.9 2.1 convolution_bitcast_fusion.2
  555.1 0.0 copy-done.1
  555.1 0.0 copy-start.2
  555.1 0.9 convolution_bitcast_fusion.3
  556.0 1.0 pad_maximum_fusion
  557.0 0.0 all-reduce.5.cloned.1.call-update
  557.0 0.2 reduce-window.7
  557.2 125.5 %all-reduce.5.cloned.1.call-done = (f32[416,256]{1,0:T(8,128)}, f32[416,256]{1,0:T(8,128)}) async-done(((f32[416,256]{1,0:T(8,128)}, f32[416,256]{1,0:T(8,128)}), (f32[416,256]{1,0:T(8,128)}, f32[416,256]{1,0:T(8,128)})) %all-reduce.5.cloned.1.call-update) | async-done | bytes 851984 | tf_op jit(solution)/shard_map/psum | solution.py:28
  682.7 2.0 mul.3
  684.7 1.2 copy.8
  685.9 0.1 bitcast_reduce_fusion
  686.0 0.8 convolution_multiply_fusion
  (2 shorter events, 0.0 us)
Async XLA Ops:
  6.5 546.4 %copy-start = (bf16[416,3584]{1,0:T(8,128)(2,1)S(1)}, bf16[416,3584]{1,0:T(8,128)(2,1)}, u32[]{:S(2)}) copy-start(bf16[416,3584]{1,0:T(8,128)(2,1)} %param.6) | copy-start | bytes 8945668
  6.5 543.1 %all-reduce.7.cloned.1.call-start = ((), (), s32[]{:S(2)}) async-start(), calls=%async_computation.1 | async-start | bytes 4718592 | tf_op jit(solution)/shard_map/psum | solution.py:12
  13.5 669.2 %all-reduce.5.cloned.1.call-start = ((), (), s32[]{:S(2)}) async-start(), calls=%async_computation | async-start | bytes 1703936 | tf_op jit(solution)/shard_map/psum | solution.py:28
  551.2 3.8 copy-start.1
  555.1 2.0 copy-start.2
Sparse Core Ops, SparseCore 0:
  13.6 535.9 all-reduce.6
  557.2 125.5 all-reduce.4
where the time goes:
time: 696 us; the launch traced here: 694 us
  waiting for transfers between devices  662 us (95%)
  between operations  14.7 us (2%)
  other arithmetic  7.54 us (1%)
  matrix products  7.09 us (1%)
    psum x1, waiting for transfers between devices, spread(): return lax.psum(block, axis)  536 us
    psum x1, waiting for transfers between devices, shards(): full_h, full_g = lax.psum((proj_h, proj_g), 'tensor')  125 us
  transfers between devices with their start and end apart: 2, of which 2 were waited for; matrix products, arithmetic and copies ran while one was open for 0% of the time, Pallas kernels for 0%

commit v1 on v0

v1 whole, which is shorter than its diff:
```python
import jax
import jax.numpy as jnp
from jax import lax
from jax.sharding import Mesh
from jax.sharding import PartitionSpec as P

QB = 4
RANK = 32
COLS = QB * RANK
Z, Y, C, H, X = 8, 4, 2, 2, 4


def swap(block, axis):
    return lax.ppermute(block, axis, [(0, 1), (1, 0)])


def halves(left, right):
    rows_l, rows_r = left.shape[0] // 2, right.shape[0] // 2
    return jnp.concatenate([left[:rows_l], right[:rows_r], left[rows_l:], right[rows_r:]], axis=0)


def shards(hidden_acts, out_grads, left_factors, right_factors, doc_tokens, owners):
    tok_rows = hidden_acts.shape[0]
    core, hi, at_x = lax.axis_index("c"), lax.axis_index("h"), lax.axis_index("x")
    rows_l, rows_r = left_factors.shape[1] // 2, right_factors.shape[1] // 2

    own = halves(left_factors[0], right_factors[0])
    piece = own.shape[0] // (Z * Y * C)
    got = lax.all_to_all(own, ("c", "z", "y"), 0, 0, tiled=True)
    got = got.reshape(Z * Y * C, piece, COLS)
    picked = []
    for batch in range(2):
        owner = owners[batch]
        source = (owner % C) * (Z * Y) + owner // C
        picked.append(lax.dynamic_index_in_dim(got, source, 0, keepdims=False))
    picked = jnp.concatenate(picked, axis=1)

    copies = jnp.broadcast_to(picked[None], (Z * Y, piece, 2 * COLS)).reshape(Z * Y * piece, 2 * COLS)
    mine = lax.all_to_all(copies, ("z", "y"), 0, 0, tiled=True)
    other = swap(mine, "c")

    def project(part, side):
        acts = lax.dynamic_slice_in_dim(hidden_acts, side * rows_l, rows_l, 1)
        grads = lax.dynamic_slice_in_dim(out_grads, side * rows_r, rows_r, 1)
        return (
            jnp.dot(acts, part[:rows_l], preferred_element_type=jnp.float32),
            jnp.dot(grads, part[rows_l:], preferred_element_type=jnp.float32),
        )

    h_mine, g_mine = project(mine, core)
    h_other, g_other = project(other, 1 - core)
    proj = jnp.concatenate([h_mine + h_other, g_mine + g_other], axis=1)

    share = tok_rows // X
    parts = lax.all_to_all(proj, "x", 0, 0, tiled=True).reshape(X, share, 4 * COLS)
    part = parts.sum(axis=0)
    h0, h1, g0, g1 = (part[:, i * COLS:(i + 1) * COLS] for i in range(4))
    first = hi == 0
    keep = jnp.concatenate([jnp.where(first, h0, h1), jnp.where(first, g0, g1)], axis=1)
    send = jnp.concatenate([jnp.where(first, h1, h0), jnp.where(first, g1, g0)], axis=1)
    full = keep + swap(send, "h")
    token_score = (full[:, :COLS] * full[:, COLS:]).reshape(share, QB, RANK).sum(axis=2)

    counts = doc_tokens[0]
    ends = jnp.cumsum(counts)
    starts = ends - counts
    places = jnp.arange(share, dtype=jnp.int32) + at_x * share
    inside = ((places[None, :] >= starts[:, None]) & (places[None, :] < ends[:, None])).astype(
        jnp.float32
    )
    partial = jnp.dot(
        inside, token_score, precision=lax.Precision.HIGHEST, preferred_element_type=jnp.float32
    )
    docs = partial.shape[0]
    flat = jnp.broadcast_to(partial.reshape(1, docs * QB), (H * X, docs * QB))
    every = lax.all_to_all(flat, ("h", "x"), 0, 0, tiled=True)
    summed = every.reshape(H, X, docs, QB).sum(axis=1)
    summed = jnp.concatenate([summed[0], summed[1]], axis=1)
    return summed / jnp.sqrt(jnp.float32(RANK * (tok_rows // 4)))


def solution(mesh):
    fine = Mesh(mesh.devices.reshape(Z, Y, C, H, X), ("z", "y", "c", "h", "x"))
    dp, tensor = ("z", "y", "c"), ("h", "x")
    return jax.shard_map(
        shards,
        mesh=fine,
        in_specs=(
            P(dp, tensor),
            P(dp, tensor),
            P(dp, tensor, None),
            P(dp, tensor, None),
            P(dp, None),
            P(),
        ),
        out_specs=P(dp, None),
        check_vma=False,
    )
```

time: 696 us -> 146 us (0.21)
  the two profiles are of different devices: /device:TPU:56 before, /device:TPU:8 now
where the time goes in v1:
time: 146 us; the launch traced here: 145 us
  blocking collectives  53.9 us (37%)
  waiting for transfers between devices  45.2 us (31%)
  starting transfers between devices  26 us (18%)
  matrix products  6.31 us (4%)
  between operations  5.09 us (3%)
  local copies, waits for them, and re-layouts  4.41 us (3%)
  other arithmetic  4.39 us (3%)
    all_to_all x1, blocking collectives, shards(): mine = lax.all_to_all(copies, ('z', 'y'), 0, 0, tiled=True)  38 us
    all_to_all x1, waiting for transfers between devices, shards(): got = lax.all_to_all(own, ('c', 'z', 'y'), 0, 0, tiled=True)  25 us
    all_to_all x1, blocking collectives, shards(): every = lax.all_to_all(flat, ('h', 'x'), 0, 0, tiled=True)  15.8 us
    all_to_all x1, starting transfers between devices, shards(): got = lax.all_to_all(own, ('c', 'z', 'y'), 0, 0, tiled=True)  14.7 us
    all_to_all x1, waiting for transfers between devices, shards(): lax.all_to_all(proj, 'x', 0, 0, tiled=True).reshape(X, share, 4 * COLS)  13.7 us
    ppermute x2, starting transfers between devices, swap(): return lax.ppermute(block, axis, [(0, 1), (1, 0)])  6.95 us
    ppermute x2, waiting for transfers between devices, swap(): return lax.ppermute(block, axis, [(0, 1), (1, 0)])  6.52 us
    all_to_all x1, starting transfers between devices, shards(): lax.all_to_all(proj, 'x', 0, 0, tiled=True).reshape(X, share, 4 * COLS)  4.42 us
  transfers between devices with their start and end apart: 4, of which 3 were waited for; matrix products, arithmetic and copies ran while one was open for 3% of the time, Pallas kernels for 0%

profile of v1, /device:TPU:8, one launch (start us, length us, event | category | flops | bytes accessed | tf_op | source)
XLA Modules:
  0.0 145.3 jit_solution(3656391174244378330)
XLA Ops:
  0.0 1.4 slice_bitcast_fusion.1
  1.4 1.1 pad_maximum_fusion
  2.6 14.7 %all-to-all-start = ((bf16[64,72,128]{2,1,0:T(8,128)(2,1)}), bf16[64,72,128]{2,1,0:T(8,128)(2,1)}, u32[]{:S(2)}, u32[]{:S(2)}) async-start(bf16[64,72,128]{2,1,0:T(8,128)(2,1)} %bitcast.27), calls=%async_computation | async-start | bytes 2359296 | tf_op jit(solution)/shard_map/all_to_all | solution.py:29
  17.2 0.6 fusion.26
  22.7 25.0 %all-to-all-done = bf16[64,72,128]{2,1,0:T(8,128)(2,1)} async-done(((bf16[64,72,128]{2,1,0:T(8,128)(2,1)}), bf16[64,72,128]{2,1,0:T(8,128)(2,1)}, u32[]{:S(2)}, u32[]{:S(2)}) %all-to-all-start) | async-done | bytes 1179680 | tf_op jit(solution)/shard_map/all_to_all | solution.py:29
  47.7 0.7 dynamic-slice_bitcast_fusion.1
  48.5 38.0 %all_to_all.33 = bf16[32,72,256]{2,1,0:T(8,128)(2,1)} all-to-all(bf16[32,72,256]{2,1,0:T(8,128)(2,1)S(1)} %broadcast_in_dim.6), channel_id=1, replica_groups=mesh['z'=8,'y'=4,'c'=2,'h'=2,'x'=4] {'z','y'}, dimensions={0} | all-to-all | bytes 2359296 | tf_op jit(solution)/shard_map/all_to_all | solution.py:39
  86.6 1.9 %collective-permute-start = (bf16[2304,256]{1,0:T(8,128)(2,1)}, bf16[2304,256]{1,0:T(8,128)(2,1)}, u32[]{:S(2)}, u32[]{:S(2)}) collective-permute-start(bf16[2304,256]{1,0:T(8,128)(2,1)} %bitcast.12), channel_id=1, source_target_pairs={{0,8},{8,0},{1,9},{9,1},{2,10},{10,2},{3,11},{11,3},{4,12},{12,4},... | collective-permute-start | bytes 3538952 | tf_op jit(solution)/shard_map/ppermute | solution.py:14
  88.5 1.4 fusion.10
  89.9 1.7 %fusion.2 = f32[416,256]{1,0:T(8,128)S(1)} fusion(bf16[416,3584]{1,0:T(8,128)(2,1)S(1)} %copy-done, s32[]{:T(128)S(6)} %select_n.58, bf16[2304,256]{1,0:T(8,128)(2,1)} %bitcast.12), kind=kOutput, calls=%fused_computation.2 | convolution fusion | flops 381681664 | bytes 2834436 | tf_op jit(solution)/shard_map/dot_general | solution.py:46
  91.7 1.8 %fusion.4 = f32[416,256]{1,0:T(8,128)S(1)} fusion(f32[416,256]{1,0:T(8,128)S(1)} %fusion.2, bf16[416,3584]{1,0:T(8,128)(2,1)S(1)} %copy-done, s32[]{:T(128)S(6)} %select_n.65, bf16[2304,256]{1,0:T(8,128)(2,1)} %collective-permute-done), kind=kOutput, calls=%fused_computation.5 | convolution fusion | flops 381788160 | bytes 3260420 | tf_op jit(solution)/shard_map/dot_general | solution.py:46
  93.5 1.2 convolution_add_fusion
  94.7 1.1 pad_maximum_fusion.1
  95.8 4.4 %all-to-all-start.2 = ((f32[4,104,512]{2,1,0:T(8,128)}), f32[4,104,512]{2,1,0:T(8,128)}, u32[]{:S(2)}, u32[]{:S(2)}) async-start(f32[4,104,512]{2,1,0:T(8,128)} %bitcast.28), calls=%async_computation.2 | async-start | bytes 1703936 | tf_op jit(solution)/shard_map/all_to_all | solution.py:55
  100.2 0.2 reduce-window.7
  100.4 13.7 %all-to-all-done.2 = f32[4,104,512]{2,1,0:T(8,128)} async-done(((f32[4,104,512]{2,1,0:T(8,128)}), f32[4,104,512]{2,1,0:T(8,128)}, u32[]{:S(2)}, u32[]{:S(2)}) %all-to-all-start.2) | async-done | bytes 852000 | tf_op jit(solution)/shard_map/all_to_all | solution.py:55
  114.1 1.2 reduce_sum.27
  115.4 5.0 %collective-permute-start.1 = (f32[104,256]{1,0:T(8,128)S(1)}, f32[104,256]{1,0:T(8,128)S(1)}, u32[]{:S(2)}, u32[]{:S(2)}) collective-permute-start(f32[104,256]{1,0:T(8,128)S(1)} %pad_maximum_fusion.2), channel_id=1, source_target_pairs={{0,4},{4,0},{1,5},{5,1},{2,6},{6,2},{3,7},{7,3},{8,12},{12,8},{9,1... | collective-permute-start | bytes 319496 | tf_op jit(solution)/shard_map/ppermute | solution.py:14
  120.4 6.5 %collective-permute-done.1 = f32[104,256]{1,0:T(8,128)S(1)} collective-permute-done((f32[104,256]{1,0:T(8,128)S(1)}, f32[104,256]{1,0:T(8,128)S(1)}, u32[]{:S(2)}, u32[]{:S(2)}) %collective-permute-start.1) | collective-permute-done | bytes 106528 | tf_op jit(solution)/shard_map/ppermute | solution.py:14
  127.1 0.2 fusion.14
  127.4 15.8 %all_to_all.34 = f32[8,1,32]{2,1,0:T(1,128)S(1)} all-to-all(f32[8,1,32]{2,1,0:T(1,128)S(1)} %broadcast_in_dim.8), channel_id=1, replica_groups=mesh['z'=8,'y'=4,'c'=2,'h'=2,'x'=4] {'h','x'}, dimensions={0} | all-to-all | bytes 2048 | tf_op jit(solution)/shard_map/all_to_all | solution.py:76
  143.2 0.5 broadcast.16
  143.7 0.7 reduce.4
  144.7 0.7 copy.15
  (30 shorter events, 0.7 us)
Async XLA Ops:
  0.0 89.9 %copy-start = (bf16[416,3584]{1,0:T(8,128)(2,1)S(1)}, bf16[416,3584]{1,0:T(8,128)(2,1)}, u32[]{:S(2)}) copy-start(bf16[416,3584]{1,0:T(8,128)(2,1)} %param.6) | copy-start | bytes 8945668
  0.0 1.4 copy-start.2
  2.6 14.7 %copy-start.3 = (s32[2]{0:T(128)S(1)}, s32[2]{0:T(128)}, u32[]{:S(2)}) copy-start(s32[2]{0:T(128)} %param.11) | copy-start | bytes 28
  2.6 45.1 %all-to-all-start = ((bf16[64,72,128]{2,1,0:T(8,128)(2,1)}), bf16[64,72,128]{2,1,0:T(8,128)(2,1)}, u32[]{:S(2)}, u32[]{:S(2)}) async-start(bf16[64,72,128]{2,1,0:T(8,128)(2,1)} %bitcast.27), calls=%async_computation | async-start | bytes 2359296 | tf_op jit(solution)/shard_map/all_to_all | solution.py:29
  86.6 5.1 %collective-permute-start = (bf16[2304,256]{1,0:T(8,128)(2,1)}, bf16[2304,256]{1,0:T(8,128)(2,1)}, u32[]{:S(2)}, u32[]{:S(2)}) collective-permute-start(bf16[2304,256]{1,0:T(8,128)(2,1)} %bitcast.12), channel_id=1, source_target_pairs={{0,8},{8,0},{1,9},{9,1},{2,10},{10,2},{3,11},{11,3},{4,12},{12,4},... | collective-permute-start | bytes 3538952 | tf_op jit(solution)/shard_map/ppermute | solution.py:14
  91.6 1.8 %copy-start.1 = (bf16[416,1024]{1,0:T(8,128)(2,1)S(1)}, bf16[416,1024]{1,0:T(8,128)(2,1)}, u32[]{:S(2)}) copy-start(bf16[416,1024]{1,0:T(8,128)(2,1)} %param.7) | copy-start | bytes 2555908
  95.8 4.4 %copy-start.4 = (s32[1,8]{1,0:T(1,128)S(1)}, s32[1,8]{1,0:T(1,128)}, u32[]{:S(2)}) copy-start(s32[1,8]{1,0:T(1,128)} %param.10) | copy-start | bytes 100
  95.8 18.3 %all-to-all-start.2 = ((f32[4,104,512]{2,1,0:T(8,128)}), f32[4,104,512]{2,1,0:T(8,128)}, u32[]{:S(2)}, u32[]{:S(2)}) async-start(f32[4,104,512]{2,1,0:T(8,128)} %bitcast.28), calls=%async_computation.2 | async-start | bytes 1703936 | tf_op jit(solution)/shard_map/all_to_all | solution.py:55
  115.4 11.6 %collective-permute-start.1 = (f32[104,256]{1,0:T(8,128)S(1)}, f32[104,256]{1,0:T(8,128)S(1)}, u32[]{:S(2)}, u32[]{:S(2)}) collective-permute-start(f32[104,256]{1,0:T(8,128)S(1)} %pad_maximum_fusion.2), channel_id=1, source_target_pairs={{0,4},{4,0},{1,5},{5,1},{2,6},{6,2},{3,7},{7,3},{8,12},{12,8},{9,1... | collective-permute-start | bytes 319496 | tf_op jit(solution)/shard_map/ppermute | solution.py:14

commit v2 on v1

v2 whole, which is shorter than its diff:
```python
import jax
import jax.numpy as jnp
from jax import lax
from jax.sharding import Mesh
from jax.sharding import PartitionSpec as P

QB = 4
RANK = 32
COLS = QB * RANK
Z, Y, C, H, X = 8, 4, 2, 2, 4


def swap(block, axis):
    return lax.ppermute(block, axis, [(0, 1), (1, 0)])


def scatter(own):
    return lax.all_to_all(own, ("c", "z", "y"), 0, 0, tiled=True)


def pick(got, owners):
    picked = []
    for batch in range(2):
        owner = owners[batch]
        source = (owner % C) * (Z * Y) + owner // C
        picked.append(lax.dynamic_index_in_dim(got, source, 0, keepdims=False))
    return jnp.concatenate(picked, axis=1)


def gather(picked):
    piece, cols = picked.shape
    copies = jnp.broadcast_to(picked[None], (Z * Y, piece, cols)).reshape(Z * Y * piece, cols)
    return lax.all_to_all(copies, ("z", "y"), 0, 0, tiled=True)


def project(acts, mine, other, core):
    rows = mine.shape[0]
    near = lax.dynamic_slice_in_dim(acts, core * rows, rows, 1)
    far = lax.dynamic_slice_in_dim(acts, (1 - core) * rows, rows, 1)
    first = jnp.dot(near, mine, preferred_element_type=jnp.float32)
    first, other = lax.optimization_barrier((first, other))
    return first + jnp.dot(far, other, preferred_element_type=jnp.float32)


def reduce_tensor(proj):
    share = proj.shape[0] // X
    parts = lax.all_to_all(proj, "x", 0, 0, tiled=True).reshape(X, share, proj.shape[1])
    part = parts.sum(axis=0)
    return part + swap(part, "h")


def reduce_tensor_beside(proj, at_x):
    share = proj.shape[0] // X
    part = lax.dynamic_slice_in_dim(proj, at_x * share, share, 0)
    for step in range(1, X):
        rows = lax.dynamic_slice_in_dim(proj, lax.rem(at_x + step, X) * share, share, 0)
        part = part + lax.ppermute(rows, "x", [(i, (i + step) % X) for i in range(X)])
    return part + swap(part, "h")


def shards(hidden_acts, out_grads, left_factors, right_factors, doc_tokens, owners):
    tok_rows = hidden_acts.shape[0]
    core, at_x = lax.axis_index("c"), lax.axis_index("x")
    share = tok_rows // X

    members = Z * Y * C
    own_l = left_factors.reshape(members, -1, COLS)
    own_r = right_factors.reshape(members, -1, COLS)
    rows_r = own_r.shape[1]
    picked = pick(scatter(jnp.concatenate([own_r, own_l], axis=1)), owners)
    mine_r = gather(picked[:rows_r])
    picked_l, mine_r = lax.optimization_barrier((picked[rows_r:], mine_r))
    other_r = swap(mine_r, "c")
    full_g = reduce_tensor_beside(project(out_grads, mine_r, other_r, core), at_x)
    mine_l, full_g = lax.optimization_barrier((gather(picked_l), full_g))
    other_l = swap(mine_l, "c")

    full_h = reduce_tensor(project(hidden_acts, mine_l, other_l, core))
    token_score = (full_h * full_g).reshape(share, 2 * QB, RANK).sum(axis=2)

    counts = doc_tokens[0]
    ends = jnp.cumsum(counts)
    starts = ends - counts
    places = jnp.arange(share, dtype=jnp.int32) + at_x * share
    inside = ((places[None, :] >= starts[:, None]) & (places[None, :] < ends[:, None])).astype(
        jnp.float32
    )
    partial = jnp.dot(
        inside, token_score, precision=lax.Precision.HIGHEST, preferred_element_type=jnp.float32
    )
    docs, queries = partial.shape
    copies = jnp.broadcast_to(partial[None], (X, docs, queries)).reshape(X * docs, queries)
    summed = lax.all_to_all(copies, "x", 0, 0, tiled=True).reshape(X, docs, queries).sum(axis=0)
    return summed / jnp.sqrt(jnp.float32(RANK * (tok_rows // 4)))


def solution(mesh):
    fine = Mesh(mesh.devices.reshape(Z, Y, C, H, X), ("z", "y", "c", "h", "x"))
    dp, tensor = ("z", "y", "c"), ("h", "x")
    return jax.shard_map(
        shards,
        mesh=fine,
        in_specs=(
            P(dp, tensor),
            P(dp, tensor),
            P(dp, tensor, None),
            P(dp, tensor, None),
            P(dp, None),
            P(),
        ),
        out_specs=P(dp, None),
        check_vma=False,
    )
```

time: 146 us -> 150 us (1.027)
  the two profiles are of different devices: /device:TPU:8 before, /device:TPU:56 now
where the time goes in v2:
time: 150 us; the launch traced here: 149 us
  waiting for transfers between devices  64.2 us (43%)
  starting transfers between devices  54.6 us (36%)
  blocking collectives  7.71 us (5%)
  other arithmetic  6.78 us (5%)
  matrix products  6.21 us (4%)
  between operations  5.43 us (4%)
  local copies, waits for them, and re-layouts  3.94 us (3%)
    all_to_all x1, waiting for transfers between devices, scatter(): return lax.all_to_all(own, ('c', 'z', 'y'), 0, 0, tiled=True)  25.1 us
    ppermute x4, waiting for transfers between devices, swap(): return lax.ppermute(block, axis, [(0, 1), (1, 0)])  15.5 us
    all_to_all x1, starting transfers between devices, scatter(): return lax.all_to_all(own, ('c', 'z', 'y'), 0, 0, tiled=True)  14.4 us
    ppermute x4, starting transfers between devices, swap(): return lax.ppermute(block, axis, [(0, 1), (1, 0)])  13.3 us
    all_to_all x2, starting transfers between devices, gather(): return lax.all_to_all(copies, ('z', 'y'), 0, 0, tiled=True)  12.1 us
    ppermute x3, starting transfers between devices, reduce_tensor_beside(): lax.ppermute(rows, 'x', [(i, (i + step) % X) for i in range(X)])  11.4 us
    all_to_all x2, waiting for transfers between devices, gather(): return lax.all_to_all(copies, ('z', 'y'), 0, 0, tiled=True)  11.3 us
    all_to_all x1, waiting for transfers between devices, reduce_tensor(): lax.all_to_all(proj, 'x', 0, 0, tiled=True).reshape(X, share, proj.shape[1])  8.77 us
  transfers between devices with their start and end apart: 11, of which 9 were waited for; matrix products, arithmetic and copies ran while one was open for 5% of the time, Pallas kernels for 0%

profile of v2, /device:TPU:56, one launch (start us, length us, event | category | flops | bytes accessed | tf_op | source)
XLA Modules:
  0.0 148.9 jit_solution(7127276838555283292)
XLA Ops:
  0.0 2.5 %pad_maximum_fusion = bf16[64,72,128]{2,1,0:T(8,128)(2,1)} fusion(bf16[64,56,128]{2,1,0:T(8,128)(2,1)} %bitcast.25, bf16[64,16,128]{2,1,0:T(8,128)(2,1)} %bitcast.26), kind=kLoop, calls=%fused_computation.4 | loop fusion | flops 2359296 | bytes 2359296 | tf_op jit(solution)/shard_map/concatenate | solution.py:70
  2.5 14.4 %all-to-all-start = ((bf16[64,72,128]{2,1,0:T(8,128)(2,1)}), bf16[64,72,128]{2,1,0:T(8,128)(2,1)}, u32[]{:S(2)}, u32[]{:S(2)}) async-start(bf16[64,72,128]{2,1,0:T(8,128)(2,1)} %pad_maximum_fusion), calls=%async_computation | async-start | bytes 2359296 | tf_op jit(solution)/shard_map/all_to_all | solution.py:18
  22.7 25.1 %all-to-all-done = bf16[64,72,128]{2,1,0:T(8,128)(2,1)} async-done(((bf16[64,72,128]{2,1,0:T(8,128)(2,1)}), bf16[64,72,128]{2,1,0:T(8,128)(2,1)}, u32[]{:S(2)}, u32[]{:S(2)}) %all-to-all-start) | async-done | bytes 1179680 | tf_op jit(solution)/shard_map/all_to_all | solution.py:18
  49.3 6.1 %all-to-all-start.1 = ((bf16[32,16,256]{2,1,0:T(8,128)(2,1)}), bf16[32,16,256]{2,1,0:T(8,128)(2,1)S(1)}, u32[]{:S(2)}, u32[]{:S(2)}) async-start(bf16[32,16,256]{2,1,0:T(8,128)(2,1)} %broadcast_in_dim.6), calls=%async_computation.1 | async-start | bytes 524288 | tf_op jit(solution)/shard_map/all_to_all | solution.py:33
  55.3 11.3 %all-to-all-done.1 = bf16[32,16,256]{2,1,0:T(8,128)(2,1)S(1)} async-done(((bf16[32,16,256]{2,1,0:T(8,128)(2,1)}), bf16[32,16,256]{2,1,0:T(8,128)(2,1)S(1)}, u32[]{:S(2)}, u32[]{:S(2)}) %all-to-all-start.1) | async-done | bytes 262176 | tf_op jit(solution)/shard_map/all_to_all | solution.py:33
  66.6 1.0 broadcast_in_dim.7
  67.7 6.0 %all-to-all-start.2 = ((bf16[32,56,256]{2,1,0:T(8,128)(2,1)}), bf16[32,56,256]{2,1,0:T(8,128)(2,1)}, u32[]{:S(2)}, u32[]{:S(2)}) async-start(bf16[32,56,256]{2,1,0:T(8,128)(2,1)} %broadcast_in_dim.7), calls=%async_computation.2 | async-start | bytes 1835008 | tf_op jit(solution)/shard_map/all_to_all | solution.py:33
  73.7 1.9 %collective-permute-start = (bf16[512,256]{1,0:T(8,128)(2,1)S(1)}, bf16[512,256]{1,0:T(8,128)(2,1)S(1)}, u32[]{:S(2)}, u32[]{:S(2)}) collective-permute-start(bf16[512,256]{1,0:T(8,128)(2,1)S(1)} %bitcast.23), channel_id=1, source_target_pairs={{0,8},{8,0},{1,9},{9,1},{2,10},{10,2},{3,11},{11,3},{4,12},{12,4},... | collective-permute-start | bytes 786440 | tf_op jit(solution)/shard_map/ppermute | solution.py:14
  75.6 1.3 fusion.6
  77.1 1.3 fusion.4
  79.2 3.4 %collective-permute-start.1 = (f32[104,256]{1,0:T(8,128)}, f32[104,256]{1,0:T(8,128)S(1)}, u32[]{:S(2)}, u32[]{:S(2)}) collective-permute-start(f32[104,256]{1,0:T(8,128)} %get-tuple-element.23), channel_id=1, source_target_pairs={{0,1},{1,2},{2,3},{3,0},{4,5},{5,6},{6,7},{7,4},{8,9},{9,10},{10,1... | collective-permute-start | bytes 319496 | tf_op jit(solution)/shard_map/ppermute | solution.py:57
  82.6 4.6 %collective-permute-start.2 = (f32[104,256]{1,0:T(8,128)}, f32[104,256]{1,0:T(8,128)}, u32[]{:S(2)}, u32[]{:S(2)}) collective-permute-start(f32[104,256]{1,0:T(8,128)} %get-tuple-element.25), channel_id=1, source_target_pairs={{0,2},{1,3},{2,0},{3,1},{4,6},{5,7},{6,4},{7,5},{8,10},{9,11},{10,... | collective-permute-start | bytes 319496 | tf_op jit(solution)/shard_map/ppermute | solution.py:57
  87.2 3.3 %collective-permute-start.3 = (f32[104,256]{1,0:T(8,128)}, f32[104,256]{1,0:T(8,128)}, u32[]{:S(2)}, u32[]{:S(2)}) collective-permute-start(f32[104,256]{1,0:T(8,128)} %get-tuple-element.24), channel_id=1, source_target_pairs={{0,3},{1,0},{2,1},{3,2},{4,7},{5,4},{6,5},{7,6},{8,11},{9,8},{10,9... | collective-permute-start | bytes 319496 | tf_op jit(solution)/shard_map/ppermute | solution.py:57
  91.2 2.9 %collective-permute-done.3 = f32[104,256]{1,0:T(8,128)} collective-permute-done((f32[104,256]{1,0:T(8,128)}, f32[104,256]{1,0:T(8,128)}, u32[]{:S(2)}, u32[]{:S(2)}) %collective-permute-start.3) | collective-permute-done | bytes 106528 | tf_op jit(solution)/shard_map/ppermute | solution.py:57
  95.1 4.7 %collective-permute-start.4 = (f32[104,256]{1,0:T(8,128)S(1)}, f32[104,256]{1,0:T(8,128)S(1)}, u32[]{:S(2)}, u32[]{:S(2)}) collective-permute-start(f32[104,256]{1,0:T(8,128)S(1)} %add_add_fusion), channel_id=1, source_target_pairs={{0,4},{4,0},{1,5},{5,1},{2,6},{6,2},{3,7},{7,3},{8,12},{12,8},{9,1... | collective-permute-start | bytes 319496 | tf_op jit(solution)/shard_map/ppermute | solution.py:14
  99.9 7.2 %collective-permute-done.4 = f32[104,256]{1,0:T(8,128)S(1)} collective-permute-done((f32[104,256]{1,0:T(8,128)S(1)}, f32[104,256]{1,0:T(8,128)S(1)}, u32[]{:S(2)}, u32[]{:S(2)}) %collective-permute-start.4) | collective-permute-done | bytes 106528 | tf_op jit(solution)/shard_map/ppermute | solution.py:14
  107.7 1.9 %collective-permute-start.5 = (bf16[1792,256]{1,0:T(8,128)(2,1)}, bf16[1792,256]{1,0:T(8,128)(2,1)}, u32[]{:S(2)}, u32[]{:S(2)}) collective-permute-start(bf16[1792,256]{1,0:T(8,128)(2,1)} %bitcast.10), channel_id=1, source_target_pairs={{0,8},{8,0},{1,9},{9,1},{2,10},{10,2},{3,11},{11,3},{4,12},{12,4},... | collective-permute-start | bytes 2752520 | tf_op jit(solution)/shard_map/ppermute | solution.py:14
  109.6 1.7 %fusion.2 = f32[416,256]{1,0:T(8,128)S(1)} fusion(bf16[1792,256]{1,0:T(8,128)(2,1)} %bitcast.10, bf16[416,3584]{1,0:T(8,128)(2,1)S(1)} %copy-done, s32[]{:T(128)S(6)} %select_n.49), kind=kOutput, calls=%fused_computation.2 | convolution fusion | flops 381681664 | bytes 2834436 | tf_op jit(solution)/shard_map/dot_general | solution.py:40
  112.4 1.7 %fusion = f32[416,256]{1,0:T(8,128)S(1)} fusion(bf16[1792,256]{1,0:T(8,128)(2,1)} %collective-permute-done.5, bf16[416,3584]{1,0:T(8,128)(2,1)S(1)} %copy-done, s32[]{:T(128)S(6)} %select_n.62), kind=kOutput, calls=%fused_computation | convolution fusion | flops 381681664 | bytes 2834436 | tf_op jit(solution)/shard_map/dot_general | solution.py:42
  114.9 3.5 %all-to-all-start.3 = ((f32[4,104,256]{2,1,0:T(8,128)}), f32[4,104,256]{2,1,0:T(8,128)S(1)}, u32[]{:S(2)}, u32[]{:S(2)}) async-start(f32[4,104,256]{2,1,0:T(8,128)} %bitcast.11), calls=%async_computation.3 | async-start | bytes 851968 | tf_op jit(solution)/shard_map/all_to_all | solution.py:47
  118.6 8.8 %all-to-all-done.3 = f32[4,104,256]{2,1,0:T(8,128)S(1)} async-done(((f32[4,104,256]{2,1,0:T(8,128)}), f32[4,104,256]{2,1,0:T(8,128)S(1)}, u32[]{:S(2)}, u32[]{:S(2)}) %all-to-all-start.3) | async-done | bytes 426016 | tf_op jit(solution)/shard_map/all_to_all | solution.py:47
  127.4 4.7 %collective-permute-start.6 = (f32[104,256]{1,0:T(8,128)S(1)}, f32[104,256]{1,0:T(8,128)S(1)}, u32[]{:S(2)}, u32[]{:S(2)}) collective-permute-start(f32[104,256]{1,0:T(8,128)S(1)} %reduce_sum.27), channel_id=1, source_target_pairs={{0,4},{4,0},{1,5},{5,1},{2,6},{6,2},{3,7},{7,3},{8,12},{12,8},{9,1... | collective-permute-start | bytes 319496 | tf_op jit(solution)/shard_map/ppermute | solution.py:14
  132.1 7.2 %collective-permute-done.6 = f32[104,256]{1,0:T(8,128)S(1)} collective-permute-done((f32[104,256]{1,0:T(8,128)S(1)}, f32[104,256]{1,0:T(8,128)S(1)}, u32[]{:S(2)}, u32[]{:S(2)}) %collective-permute-start.6) | collective-permute-done | bytes 106528 | tf_op jit(solution)/shard_map/ppermute | solution.py:14
  140.6 7.7 %all_to_all.38 = f32[4,8,8]{2,1,0:T(8,128)S(1)} all-to-all(f32[4,8,8]{2,1,0:T(8,128)S(1)} %broadcast_in_dim.8), channel_id=1, replica_groups=mesh['z'=8,'y'=4,'c'=2,'h'=2,'x'=4] {'x'}, dimensions={0} | all-to-all | bytes 2048 | tf_op jit(solution)/shard_map/all_to_all | solution.py:93
  (32 shorter events, 9.2 us)
Async XLA Ops:
  0.0 109.6 %copy-start = (bf16[416,3584]{1,0:T(8,128)(2,1)S(1)}, bf16[416,3584]{1,0:T(8,128)(2,1)}, u32[]{:S(2)}) copy-start(bf16[416,3584]{1,0:T(8,128)(2,1)} %param.6) | copy-start | bytes 8945668
  2.5 14.4 %copy-start.1 = (s32[2]{0:T(128)S(1)}, s32[2]{0:T(128)}, u32[]{:S(2)}) copy-start(s32[2]{0:T(128)} %param.11) | copy-start | bytes 28
  2.5 45.3 %all-to-all-start = ((bf16[64,72,128]{2,1,0:T(8,128)(2,1)}), bf16[64,72,128]{2,1,0:T(8,128)(2,1)}, u32[]{:S(2)}, u32[]{:S(2)}) async-start(bf16[64,72,128]{2,1,0:T(8,128)(2,1)} %pad_maximum_fusion), calls=%async_computation | async-start | bytes 2359296 | tf_op jit(solution)/shard_map/all_to_all | solution.py:18
  49.3 17.4 %all-to-all-start.1 = ((bf16[32,16,256]{2,1,0:T(8,128)(2,1)}), bf16[32,16,256]{2,1,0:T(8,128)(2,1)S(1)}, u32[]{:S(2)}, u32[]{:S(2)}) async-start(bf16[32,16,256]{2,1,0:T(8,128)(2,1)} %broadcast_in_dim.6), calls=%async_computation.1 | async-start | bytes 524288 | tf_op jit(solution)/shard_map/all_to_all | solution.py:33
  67.7 40.0 %all-to-all-start.2 = ((bf16[32,56,256]{2,1,0:T(8,128)(2,1)}), bf16[32,56,256]{2,1,0:T(8,128)(2,1)}, u32[]{:S(2)}, u32[]{:S(2)}) async-start(bf16[32,56,256]{2,1,0:T(8,128)(2,1)} %broadcast_in_dim.7), calls=%async_computation.2 | async-start | bytes 1835008 | tf_op jit(solution)/shard_map/all_to_all | solution.py:33
  73.7 3.4 %collective-permute-start = (bf16[512,256]{1,0:T(8,128)(2,1)S(1)}, bf16[512,256]{1,0:T(8,128)(2,1)S(1)}, u32[]{:S(2)}, u32[]{:S(2)}) collective-permute-start(bf16[512,256]{1,0:T(8,128)(2,1)S(1)} %bitcast.23), channel_id=1, source_target_pairs={{0,8},{8,0},{1,9},{9,1},{2,10},{10,2},{3,11},{11,3},{4,12},{12,4},... | collective-permute-start | bytes 786440 | tf_op jit(solution)/shard_map/ppermute | solution.py:14
  79.2 11.4 %collective-permute-start.1 = (f32[104,256]{1,0:T(8,128)}, f32[104,256]{1,0:T(8,128)S(1)}, u32[]{:S(2)}, u32[]{:S(2)}) collective-permute-start(f32[104,256]{1,0:T(8,128)} %get-tuple-element.23), channel_id=1, source_target_pairs={{0,1},{1,2},{2,3},{3,0},{4,5},{5,6},{6,7},{7,4},{8,9},{9,10},{10,1... | collective-permute-start | bytes 319496 | tf_op jit(solution)/shard_map/ppermute | solution.py:57
  82.6 8.6 %collective-permute-start.2 = (f32[104,256]{1,0:T(8,128)}, f32[104,256]{1,0:T(8,128)}, u32[]{:S(2)}, u32[]{:S(2)}) collective-permute-start(f32[104,256]{1,0:T(8,128)} %get-tuple-element.25), channel_id=1, source_target_pairs={{0,2},{1,3},{2,0},{3,1},{4,6},{5,7},{6,4},{7,5},{8,10},{9,11},{10,... | collective-permute-start | bytes 319496 | tf_op jit(solution)/shard_map/ppermute | solution.py:57
  87.2 6.9 %collective-permute-start.3 = (f32[104,256]{1,0:T(8,128)}, f32[104,256]{1,0:T(8,128)}, u32[]{:S(2)}, u32[]{:S(2)}) collective-permute-start(f32[104,256]{1,0:T(8,128)} %get-tuple-element.24), channel_id=1, source_target_pairs={{0,3},{1,0},{2,1},{3,2},{4,7},{5,4},{6,5},{7,6},{8,11},{9,8},{10,9... | collective-permute-start | bytes 319496 | tf_op jit(solution)/shard_map/ppermute | solution.py:57
  95.1 11.9 %collective-permute-start.4 = (f32[104,256]{1,0:T(8,128)S(1)}, f32[104,256]{1,0:T(8,128)S(1)}, u32[]{:S(2)}, u32[]{:S(2)}) collective-permute-start(f32[104,256]{1,0:T(8,128)S(1)} %add_add_fusion), channel_id=1, source_target_pairs={{0,4},{4,0},{1,5},{5,1},{2,6},{6,2},{3,7},{7,3},{8,12},{12,8},{9,1... | collective-permute-start | bytes 319496 | tf_op jit(solution)/shard_map/ppermute | solution.py:14
  107.7 4.7 %collective-permute-start.5 = (bf16[1792,256]{1,0:T(8,128)(2,1)}, bf16[1792,256]{1,0:T(8,128)(2,1)}, u32[]{:S(2)}, u32[]{:S(2)}) collective-permute-start(bf16[1792,256]{1,0:T(8,128)(2,1)} %bitcast.10), channel_id=1, source_target_pairs={{0,8},{8,0},{1,9},{9,1},{2,10},{10,2},{3,11},{11,3},{4,12},{12,4},... | collective-permute-start | bytes 2752520 | tf_op jit(solution)/shard_map/ppermute | solution.py:14
  114.1 4.3 %copy-start.2 = (s32[1,8]{1,0:T(1,128)S(1)}, s32[1,8]{1,0:T(1,128)}, u32[]{:S(2)}) copy-start(s32[1,8]{1,0:T(1,128)} %param.10) | copy-start | bytes 100
  114.9 12.4 %all-to-all-start.3 = ((f32[4,104,256]{2,1,0:T(8,128)}), f32[4,104,256]{2,1,0:T(8,128)S(1)}, u32[]{:S(2)}, u32[]{:S(2)}) async-start(f32[4,104,256]{2,1,0:T(8,128)} %bitcast.11), calls=%async_computation.3 | async-start | bytes 851968 | tf_op jit(solution)/shard_map/all_to_all | solution.py:47
  127.4 11.9 %collective-permute-start.6 = (f32[104,256]{1,0:T(8,128)S(1)}, f32[104,256]{1,0:T(8,128)S(1)}, u32[]{:S(2)}, u32[]{:S(2)}) collective-permute-start(f32[104,256]{1,0:T(8,128)S(1)} %reduce_sum.27), channel_id=1, source_target_pairs={{0,4},{4,0},{1,5},{5,1},{2,6},{6,2},{3,7},{7,3},{8,12},{12,8},{9,1... | collective-permute-start | bytes 319496 | tf_op jit(solution)/shard_map/ppermute | solution.py:14

commit v3 on v2

v3 whole, which is shorter than its diff:
```python
import jax
import jax.numpy as jnp
from jax import lax
from jax.sharding import Mesh
from jax.sharding import PartitionSpec as P

QB = 4
RANK = 32
COLS = QB * RANK
Z, Y, C, H, X = 8, 4, 2, 2, 4


def swap(block, axis):
    return lax.ppermute(block, axis, [(0, 1), (1, 0)])


def turn(block, axis, size, step):
    return lax.ppermute(block, axis, [(i, (i + step) % size) for i in range(size)])


def scatter(own):
    members = Z * Y * C
    return lax.all_to_all(own.reshape(members, -1, COLS), ("c", "z", "y"), 0, 0, tiled=True)


def pick(got, owners):
    picked = []
    for batch in range(2):
        owner = owners[batch]
        source = (owner % C) * (Z * Y) + owner // C
        picked.append(lax.dynamic_index_in_dim(got, source, 0, keepdims=False))
    return jnp.concatenate(picked, axis=1)


def gather(picked):
    piece, cols = picked.shape
    copies = jnp.broadcast_to(picked[None], (Z * Y, piece, cols)).reshape(Z * Y * piece, cols)
    return lax.all_to_all(copies, ("z", "y"), 0, 0, tiled=True)


def project(acts, mine, other, core):
    rows = mine.shape[0]
    near = lax.dynamic_slice_in_dim(acts, core * rows, rows, 1)
    far = lax.dynamic_slice_in_dim(acts, (1 - core) * rows, rows, 1)
    first = jnp.dot(near, mine, preferred_element_type=jnp.float32)
    first, other = lax.optimization_barrier((first, other))
    return first + jnp.dot(far, other, preferred_element_type=jnp.float32)


def sum_x(proj, at_x):
    share = proj.shape[0] // X
    part = lax.dynamic_slice_in_dim(proj, at_x * share, share, 0)
    for step in range(1, X):
        rows = lax.dynamic_slice_in_dim(proj, lax.rem(at_x + step, X) * share, share, 0)
        part = part + turn(rows, "x", X, step)
    return part


def gather_x(part, at_x):
    share = part.shape[0]
    full = jnp.zeros((X * share, part.shape[1]), part.dtype)
    full = lax.dynamic_update_slice_in_dim(full, part, at_x * share, 0)
    for step in range(1, X):
        rows = turn(part, "x", X, step)
        full = lax.dynamic_update_slice_in_dim(full, rows, lax.rem(at_x - step + X, X) * share, 0)
    return full


def shards(hidden_acts, out_grads, left_factors, right_factors, doc_tokens, owners):
    tok_rows = hidden_acts.shape[0]
    core, at_x = lax.axis_index("c"), lax.axis_index("x")

    mine_r = gather(pick(scatter(right_factors), owners))
    left_factors, mine_r = lax.optimization_barrier((left_factors, mine_r))
    part_g = sum_x(project(out_grads, mine_r, swap(mine_r, "c"), core), at_x)
    got_l, part_g = lax.optimization_barrier((scatter(left_factors), part_g))
    full_g = gather_x(part_g + swap(part_g, "h"), at_x)
    mine_l, full_g = lax.optimization_barrier((gather(pick(got_l, owners)), full_g))

    part_h = project(hidden_acts, mine_l, swap(mine_l, "c"), core)
    token_score = (part_h * full_g).reshape(tok_rows, 2 * QB, RANK).sum(axis=2)

    counts = doc_tokens[0]
    ends = jnp.cumsum(counts)
    starts = ends - counts
    places = jnp.arange(tok_rows, dtype=jnp.int32)
    inside = ((places[None, :] >= starts[:, None]) & (places[None, :] < ends[:, None])).astype(
        jnp.float32
    )
    partial = jnp.dot(
        inside, token_score, precision=lax.Precision.HIGHEST, preferred_element_type=jnp.float32
    )
    docs, queries = partial.shape
    copies = jnp.broadcast_to(partial[None], (H * X, docs, queries))
    summed = lax.all_to_all(copies, ("h", "x"), 0, 0, tiled=True).sum(axis=0)
    return summed / jnp.sqrt(jnp.float32(RANK * (tok_rows // 4)))


def solution(mesh):
    fine = Mesh(mesh.devices.reshape(Z, Y, C, H, X), ("z", "y", "c", "h", "x"))
    dp, tensor = ("z", "y", "c"), ("h", "x")
    return jax.shard_map(
        shards,
        mesh=fine,
        in_specs=(
            P(dp, tensor),
            P(dp, tensor),
            P(dp, tensor, None),
            P(dp, tensor, None),
            P(dp, None),
            P(),
        ),
        out_specs=P(dp, None),
        check_vma=False,
    )
```

time: 150 us -> 147 us (0.980)
  the two profiles are of different devices: /device:TPU:56 before, /device:TPU:24 now
where the time goes in v3:
time: 147 us; the launch traced here: 146 us
  starting transfers between devices  59.5 us (40%)
  waiting for transfers between devices  33.6 us (23%)
  blocking collectives  32.8 us (22%)
  matrix products  6.21 us (4%)
  between operations  5.45 us (4%)
  local copies, waits for them, and re-layouts  5.35 us (4%)
  other arithmetic  2.83 us (2%)
    ppermute x6, starting transfers between devices, turn(): lax.ppermute(block, axis, [(i, (i + step) % size) for i in range(size)])  22.8 us
    all_to_all x2, starting transfers between devices, scatter(): lax.all_to_all(own.reshape(members, -1, COLS), ('c', 'z', 'y'), 0, 0, til...  21 us
    ppermute x3, waiting for transfers between devices, swap(): return lax.ppermute(block, axis, [(0, 1), (1, 0)])  18.1 us
    all_to_all x1, blocking collectives, gather(): return lax.all_to_all(copies, ('z', 'y'), 0, 0, tiled=True)  16.6 us
    all_to_all x1, blocking collectives, shards(): summed = lax.all_to_all(copies, ('h', 'x'), 0, 0, tiled=True).sum(axis=0)  16.2 us
    ppermute x3, starting transfers between devices, swap(): return lax.ppermute(block, axis, [(0, 1), (1, 0)])  9.2 us
    all_to_all x2, waiting for transfers between devices, scatter(): lax.all_to_all(own.reshape(members, -1, COLS), ('c', 'z', 'y'), 0, 0, til...  8.93 us
    ppermute x6, waiting for transfers between devices, turn(): lax.ppermute(block, axis, [(i, (i + step) % size) for i in range(size)])  6.54 us
  transfers between devices with their start and end apart: 12, of which 8 were waited for; matrix products, arithmetic and copies ran while one was open for 5% of the time, Pallas kernels for 0%

profile of v3, /device:TPU:24, one launch (start us, length us, event | category | flops | bytes accessed | tf_op | source)
XLA Modules:
  0.0 145.7 jit_solution(1929746200066885640)
XLA Ops:
  0.0 14.4 %all-to-all-start = ((bf16[64,16,128]{2,1,0:T(8,128)(2,1)}), bf16[64,16,128]{2,1,0:T(8,128)(2,1)S(1)}, u32[]{:S(2)}, u32[]{:S(2)}) async-start(bf16[64,16,128]{2,1,0:T(8,128)(2,1)} %bitcast.29), calls=%async_computation | async-start | bytes 524288 | tf_op jit(solution)/shard_map/all_to_all | solution.py:23
  14.4 1.3 fusion.17
  20.9 5.2 %all-to-all-done = bf16[64,16,128]{2,1,0:T(8,128)(2,1)S(1)} async-done(((bf16[64,16,128]{2,1,0:T(8,128)(2,1)}), bf16[64,16,128]{2,1,0:T(8,128)(2,1)S(1)}, u32[]{:S(2)}, u32[]{:S(2)}) %all-to-all-start) | async-done | bytes 262176 | tf_op jit(solution)/shard_map/all_to_all | solution.py:23
  26.2 16.6 %all_to_all.33 = bf16[32,16,256]{2,1,0:T(8,128)(2,1)S(1)} all-to-all(bf16[32,16,256]{2,1,0:T(8,128)(2,1)S(1)} %broadcast_in_dim.8), channel_id=1, replica_groups=mesh['z'=8,'y'=4,'c'=2,'h'=2,'x'=4] {'z','y'}, dimensions={0} | all-to-all | bytes 524288 | tf_op jit(solution)/shard_map/all_to_all | solution.py:38
  42.8 6.6 %all-to-all-start.2 = ((bf16[64,56,128]{2,1,0:T(8,128)(2,1)}), bf16[64,56,128]{2,1,0:T(8,128)(2,1)}, u32[]{:S(2)}, u32[]{:S(2)}) async-start(bf16[64,56,128]{2,1,0:T(8,128)(2,1)} %bitcast.28), calls=%async_computation.2 | async-start | bytes 1835008 | tf_op jit(solution)/shard_map/all_to_all | solution.py:23
  49.4 2.2 %collective-permute-start = (bf16[512,256]{1,0:T(8,128)(2,1)S(1)}, bf16[512,256]{1,0:T(8,128)(2,1)S(1)}, u32[]{:S(2)}, u32[]{:S(2)}) collective-permute-start(bf16[512,256]{1,0:T(8,128)(2,1)S(1)} %bitcast.26), channel_id=1, source_target_pairs={{0,8},{8,0},{1,9},{9,1},{2,10},{10,2},{3,11},{11,3},{4,12},{12,4},... | collective-permute-start | bytes 786440 | tf_op jit(solution)/shard_map/ppermute | solution.py:14
  51.7 1.3 fusion.6
  53.0 1.3 fusion.4
  55.1 3.4 %collective-permute-start.1 = (f32[104,256]{1,0:T(8,128)}, f32[104,256]{1,0:T(8,128)S(1)}, u32[]{:S(2)}, u32[]{:S(2)}) collective-permute-start(f32[104,256]{1,0:T(8,128)} %get-tuple-element.29), channel_id=1, source_target_pairs={{0,1},{1,2},{2,3},{3,0},{4,5},{5,6},{6,7},{7,4},{8,9},{9,10},{10,1... | collective-permute-start | bytes 319496 | tf_op jit(solution)/shard_map/ppermute | solution.py:18
  58.5 4.6 %collective-permute-start.2 = (f32[104,256]{1,0:T(8,128)}, f32[104,256]{1,0:T(8,128)}, u32[]{:S(2)}, u32[]{:S(2)}) collective-permute-start(f32[104,256]{1,0:T(8,128)} %get-tuple-element.31), channel_id=1, source_target_pairs={{0,2},{1,3},{2,0},{3,1},{4,6},{5,7},{6,4},{7,5},{8,10},{9,11},{10,... | collective-permute-start | bytes 319496 | tf_op jit(solution)/shard_map/ppermute | solution.py:18
  63.1 3.3 %collective-permute-start.3 = (f32[104,256]{1,0:T(8,128)}, f32[104,256]{1,0:T(8,128)}, u32[]{:S(2)}, u32[]{:S(2)}) collective-permute-start(f32[104,256]{1,0:T(8,128)} %get-tuple-element.30), channel_id=1, source_target_pairs={{0,3},{1,0},{2,1},{3,2},{4,7},{5,4},{6,5},{7,6},{8,11},{9,8},{10,9... | collective-permute-start | bytes 319496 | tf_op jit(solution)/shard_map/ppermute | solution.py:18
  67.1 2.9 %collective-permute-done.3 = f32[104,256]{1,0:T(8,128)} collective-permute-done((f32[104,256]{1,0:T(8,128)}, f32[104,256]{1,0:T(8,128)}, u32[]{:S(2)}, u32[]{:S(2)}) %collective-permute-start.3) | collective-permute-done | bytes 106528 | tf_op jit(solution)/shard_map/ppermute | solution.py:18
  71.1 3.7 %all-to-all-done.2 = bf16[64,56,128]{2,1,0:T(8,128)(2,1)} async-done(((bf16[64,56,128]{2,1,0:T(8,128)(2,1)}), bf16[64,56,128]{2,1,0:T(8,128)(2,1)}, u32[]{:S(2)}, u32[]{:S(2)}) %all-to-all-start.2) | async-done | bytes 917536 | tf_op jit(solution)/shard_map/all_to_all | solution.py:23
  76.6 6.5 %all-to-all-start.3 = ((bf16[32,56,256]{2,1,0:T(8,128)(2,1)}), bf16[32,56,256]{2,1,0:T(8,128)(2,1)}, u32[]{:S(2)}, u32[]{:S(2)}) async-start(bf16[32,56,256]{2,1,0:T(8,128)(2,1)} %broadcast_in_dim.9), calls=%async_computation.3 | async-start | bytes 1835008 | tf_op jit(solution)/shard_map/all_to_all | solution.py:38
  83.1 5.0 %collective-permute-start.4 = (f32[104,256]{1,0:T(8,128)S(1)}, f32[104,256]{1,0:T(8,128)S(1)}, u32[]{:S(2)}, u32[]{:S(2)}) collective-permute-start(f32[104,256]{1,0:T(8,128)S(1)} %add_add_fusion), channel_id=1, source_target_pairs={{0,4},{4,0},{1,5},{5,1},{2,6},{6,2},{3,7},{7,3},{8,12},{12,8},{9,1... | collective-permute-start | bytes 319496 | tf_op jit(solution)/shard_map/ppermute | solution.py:14
  88.2 17.3 %collective-permute-done.4 = f32[104,256]{1,0:T(8,128)S(1)} collective-permute-done((f32[104,256]{1,0:T(8,128)S(1)}, f32[104,256]{1,0:T(8,128)S(1)}, u32[]{:S(2)}, u32[]{:S(2)}) %collective-permute-start.4) | collective-permute-done | bytes 106528 | tf_op jit(solution)/shard_map/ppermute | solution.py:14
  105.5 3.4 %collective-permute-start.5 = (f32[104,256]{1,0:T(8,128)S(1)}, f32[104,256]{1,0:T(8,128)S(1)}, u32[]{:S(2)}, u32[]{:S(2)}) collective-permute-start(f32[104,256]{1,0:T(8,128)S(1)} %get-tuple-element.26), channel_id=1, source_target_pairs={{0,1},{1,2},{2,3},{3,0},{4,5},{5,6},{6,7},{7,4},{8,9},{9,10},{10,1... | collective-permute-start | bytes 319496 | tf_op jit(solution)/shard_map/ppermute | solution.py:18
  109.0 4.6 %collective-permute-start.6 = (f32[104,256]{1,0:T(8,128)S(1)}, f32[104,256]{1,0:T(8,128)S(1)}, u32[]{:S(2)}, u32[]{:S(2)}) collective-permute-start(f32[104,256]{1,0:T(8,128)S(1)} %get-tuple-element.26), channel_id=1, source_target_pairs={{0,2},{1,3},{2,0},{3,1},{4,6},{5,7},{6,4},{7,5},{8,10},{9,11},{10,... | collective-permute-start | bytes 319496 | tf_op jit(solution)/shard_map/ppermute | solution.py:18
  113.6 3.4 %collective-permute-start.7 = (f32[104,256]{1,0:T(8,128)S(1)}, f32[104,256]{1,0:T(8,128)S(1)}, u32[]{:S(2)}, u32[]{:S(2)}) collective-permute-start(f32[104,256]{1,0:T(8,128)S(1)} %get-tuple-element.26), channel_id=1, source_target_pairs={{0,3},{1,0},{2,1},{3,2},{4,7},{5,4},{6,5},{7,6},{8,11},{9,8},{10,9... | collective-permute-start | bytes 319496 | tf_op jit(solution)/shard_map/ppermute | solution.py:18
  117.1 3.1 %collective-permute-done.7 = f32[104,256]{1,0:T(8,128)S(1)} collective-permute-done((f32[104,256]{1,0:T(8,128)S(1)}, f32[104,256]{1,0:T(8,128)S(1)}, u32[]{:S(2)}, u32[]{:S(2)}) %collective-permute-start.7) | collective-permute-done | bytes 106528 | tf_op jit(solution)/shard_map/ppermute | solution.py:18
  120.2 1.9 %collective-permute-start.8 = (bf16[1792,256]{1,0:T(8,128)(2,1)}, bf16[1792,256]{1,0:T(8,128)(2,1)}, u32[]{:S(2)}, u32[]{:S(2)}) collective-permute-start(bf16[1792,256]{1,0:T(8,128)(2,1)} %bitcast.12), channel_id=1, source_target_pairs={{0,8},{8,0},{1,9},{9,1},{2,10},{10,2},{3,11},{11,3},{4,12},{12,4},... | collective-permute-start | bytes 2752520 | tf_op jit(solution)/shard_map/ppermute | solution.py:14
  122.3 1.7 %fusion.2 = f32[416,256]{1,0:T(8,128)S(1)} fusion(bf16[1792,256]{1,0:T(8,128)(2,1)} %bitcast.12, bf16[416,3584]{1,0:T(8,128)(2,1)S(1)} %copy-done, s32[]{:T(128)S(6)} %select_n.62), kind=kOutput, calls=%fused_computation.2 | convolution fusion | flops 381681664 | bytes 2834436 | tf_op jit(solution)/shard_map/dot_general | solution.py:45
  124.9 1.7 %fusion = f32[416,256]{1,0:T(8,128)S(1)} fusion(bf16[1792,256]{1,0:T(8,128)(2,1)} %collective-permute-done.8, bf16[416,3584]{1,0:T(8,128)(2,1)S(1)} %copy-done, s32[]{:T(128)S(6)} %select_n.75), kind=kOutput, calls=%fused_computation | convolution fusion | flops 381681664 | bytes 2834436 | tf_op jit(solution)/shard_map/dot_general | solution.py:47
  129.0 16.2 %all_to_all.34 = f32[8,8,8]{2,1,0:T(8,128)S(1)} all-to-all(f32[8,8,8]{2,1,0:T(8,128)S(1)} %broadcast_in_dim.11), channel_id=1, replica_groups=mesh['z'=8,'y'=4,'c'=2,'h'=2,'x'=4] {'h','x'}, dimensions={0} | all-to-all | bytes 4096 | tf_op jit(solution)/shard_map/all_to_all | solution.py:95
  (36 shorter events, 8.4 us)
Async XLA Ops:
  0.0 122.3 %copy-start = (bf16[416,3584]{1,0:T(8,128)(2,1)S(1)}, bf16[416,3584]{1,0:T(8,128)(2,1)}, u32[]{:S(2)}) copy-start(bf16[416,3584]{1,0:T(8,128)(2,1)} %param.6) | copy-start | bytes 8945668
  0.0 26.1 %all-to-all-start = ((bf16[64,16,128]{2,1,0:T(8,128)(2,1)}), bf16[64,16,128]{2,1,0:T(8,128)(2,1)S(1)}, u32[]{:S(2)}, u32[]{:S(2)}) async-start(bf16[64,16,128]{2,1,0:T(8,128)(2,1)} %bitcast.29), calls=%async_computation | async-start | bytes 524288 | tf_op jit(solution)/shard_map/all_to_all | solution.py:23
  42.8 32.0 %all-to-all-start.2 = ((bf16[64,56,128]{2,1,0:T(8,128)(2,1)}), bf16[64,56,128]{2,1,0:T(8,128)(2,1)}, u32[]{:S(2)}, u32[]{:S(2)}) async-start(bf16[64,56,128]{2,1,0:T(8,128)(2,1)} %bitcast.28), calls=%async_computation.2 | async-start | bytes 1835008 | tf_op jit(solution)/shard_map/all_to_all | solution.py:23
  49.4 3.6 %collective-permute-start = (bf16[512,256]{1,0:T(8,128)(2,1)S(1)}, bf16[512,256]{1,0:T(8,128)(2,1)S(1)}, u32[]{:S(2)}, u32[]{:S(2)}) collective-permute-start(bf16[512,256]{1,0:T(8,128)(2,1)S(1)} %bitcast.26), channel_id=1, source_target_pairs={{0,8},{8,0},{1,9},{9,1},{2,10},{10,2},{3,11},{11,3},{4,12},{12,4},... | collective-permute-start | bytes 786440 | tf_op jit(solution)/shard_map/ppermute | solution.py:14
  54.3 67.8 %copy-start.2 = (s32[1,8]{1,0:T(1,128)S(1)}, s32[1,8]{1,0:T(1,128)}, u32[]{:S(2)}) copy-start(s32[1,8]{1,0:T(1,128)} %param.10) | copy-start | bytes 100
  55.1 11.4 %collective-permute-start.1 = (f32[104,256]{1,0:T(8,128)}, f32[104,256]{1,0:T(8,128)S(1)}, u32[]{:S(2)}, u32[]{:S(2)}) collective-permute-start(f32[104,256]{1,0:T(8,128)} %get-tuple-element.29), channel_id=1, source_target_pairs={{0,1},{1,2},{2,3},{3,0},{4,5},{5,6},{6,7},{7,4},{8,9},{9,10},{10,1... | collective-permute-start | bytes 319496 | tf_op jit(solution)/shard_map/ppermute | solution.py:18
  58.5 8.5 %collective-permute-start.2 = (f32[104,256]{1,0:T(8,128)}, f32[104,256]{1,0:T(8,128)}, u32[]{:S(2)}, u32[]{:S(2)}) collective-permute-start(f32[104,256]{1,0:T(8,128)} %get-tuple-element.31), channel_id=1, source_target_pairs={{0,2},{1,3},{2,0},{3,1},{4,6},{5,7},{6,4},{7,5},{8,10},{9,11},{10,... | collective-permute-start | bytes 319496 | tf_op jit(solution)/shard_map/ppermute | solution.py:18
  63.1 6.9 %collective-permute-start.3 = (f32[104,256]{1,0:T(8,128)}, f32[104,256]{1,0:T(8,128)}, u32[]{:S(2)}, u32[]{:S(2)}) collective-permute-start(f32[104,256]{1,0:T(8,128)} %get-tuple-element.30), channel_id=1, source_target_pairs={{0,3},{1,0},{2,1},{3,2},{4,7},{5,4},{6,5},{7,6},{8,11},{9,8},{10,9... | collective-permute-start | bytes 319496 | tf_op jit(solution)/shard_map/ppermute | solution.py:18
  66.5 0.6 copy-start.1
  76.6 43.6 %all-to-all-start.3 = ((bf16[32,56,256]{2,1,0:T(8,128)(2,1)}), bf16[32,56,256]{2,1,0:T(8,128)(2,1)}, u32[]{:S(2)}, u32[]{:S(2)}) async-start(bf16[32,56,256]{2,1,0:T(8,128)(2,1)} %broadcast_in_dim.9), calls=%async_computation.3 | async-start | bytes 1835008 | tf_op jit(solution)/shard_map/all_to_all | solution.py:38
  83.1 22.3 %collective-permute-start.4 = (f32[104,256]{1,0:T(8,128)S(1)}, f32[104,256]{1,0:T(8,128)S(1)}, u32[]{:S(2)}, u32[]{:S(2)}) collective-permute-start(f32[104,256]{1,0:T(8,128)S(1)} %add_add_fusion), channel_id=1, source_target_pairs={{0,4},{4,0},{1,5},{5,1},{2,6},{6,2},{3,7},{7,3},{8,12},{12,8},{9,1... | collective-permute-start | bytes 319496 | tf_op jit(solution)/shard_map/ppermute | solution.py:14
  105.5 11.4 %collective-permute-start.5 = (f32[104,256]{1,0:T(8,128)S(1)}, f32[104,256]{1,0:T(8,128)S(1)}, u32[]{:S(2)}, u32[]{:S(2)}) collective-permute-start(f32[104,256]{1,0:T(8,128)S(1)} %get-tuple-element.26), channel_id=1, source_target_pairs={{0,1},{1,2},{2,3},{3,0},{4,5},{5,6},{6,7},{7,4},{8,9},{9,10},{10,1... | collective-permute-start | bytes 319496 | tf_op jit(solution)/shard_map/ppermute | solution.py:18
  109.0 8.1 %collective-permute-start.6 = (f32[104,256]{1,0:T(8,128)S(1)}, f32[104,256]{1,0:T(8,128)S(1)}, u32[]{:S(2)}, u32[]{:S(2)}) collective-permute-start(f32[104,256]{1,0:T(8,128)S(1)} %get-tuple-element.26), channel_id=1, source_target_pairs={{0,2},{1,3},{2,0},{3,1},{4,6},{5,7},{6,4},{7,5},{8,10},{9,11},{10,... | collective-permute-start | bytes 319496 | tf_op jit(solution)/shard_map/ppermute | solution.py:18
  113.6 6.6 %collective-permute-start.7 = (f32[104,256]{1,0:T(8,128)S(1)}, f32[104,256]{1,0:T(8,128)S(1)}, u32[]{:S(2)}, u32[]{:S(2)}) collective-permute-start(f32[104,256]{1,0:T(8,128)S(1)} %get-tuple-element.26), channel_id=1, source_target_pairs={{0,3},{1,0},{2,1},{3,2},{4,7},{5,4},{6,5},{7,6},{8,11},{9,8},{10,9... | collective-permute-start | bytes 319496 | tf_op jit(solution)/shard_map/ppermute | solution.py:18
  120.2 4.7 %collective-permute-start.8 = (bf16[1792,256]{1,0:T(8,128)(2,1)}, bf16[1792,256]{1,0:T(8,128)(2,1)}, u32[]{:S(2)}, u32[]{:S(2)}) collective-permute-start(bf16[1792,256]{1,0:T(8,128)(2,1)} %bitcast.12), channel_id=1, source_target_pairs={{0,8},{8,0},{1,9},{9,1},{2,10},{10,2},{3,11},{11,3},{4,12},{12,4},... | collective-permute-start | bytes 2752520 | tf_op jit(solution)/shard_map/ppermute | solution.py:14

commit v4 on v3

--- a/solution.py
+++ b/solution.py
@@ -56,16 +56,6 @@
     return part
 
 
-def gather_x(part, at_x):
-    share = part.shape[0]
-    full = jnp.zeros((X * share, part.shape[1]), part.dtype)
-    full = lax.dynamic_update_slice_in_dim(full, part, at_x * share, 0)
-    for step in range(1, X):
-        rows = turn(part, "x", X, step)
-        full = lax.dynamic_update_slice_in_dim(full, rows, lax.rem(at_x - step + X, X) * share, 0)
-    return full
-
-
 def shards(hidden_acts, out_grads, left_factors, right_factors, doc_tokens, owners):
     tok_rows = hidden_acts.shape[0]
     core, at_x = lax.axis_index("c"), lax.axis_index("x")
@@ -73,8 +63,9 @@
     mine_r = gather(pick(scatter(right_factors), owners))
     left_factors, mine_r = lax.optimization_barrier((left_factors, mine_r))
     part_g = sum_x(project(out_grads, mine_r, swap(mine_r, "c"), core), at_x)
+    other_g = swap(part_g, "h")
     got_l, part_g = lax.optimization_barrier((scatter(left_factors), part_g))
-    full_g = gather_x(part_g + swap(part_g, "h"), at_x)
+    full_g = lax.all_gather(part_g + other_g, "x", axis=0, tiled=True)
     mine_l, full_g = lax.optimization_barrier((gather(pick(got_l, owners)), full_g))
 
     part_h = project(hidden_acts, mine_l, swap(mine_l, "c"), core)

time: 147 us -> 145 us (0.986)
  blocking collectives: 32.8 us -> 45.7 us
  starting transfers between devices: 59.5 us -> 48.1 us
  waiting for transfers between devices: 33.6 us -> 30.4 us
    all_gather x0 -> x1, blocking collectives: none -> 13.4 us  [shards(): full_g = lax.all_gather(part_g + other_g, 'x', axis=0, tiled=True)]
    ppermute x6 -> x3, starting transfers between devices: 22.8 us -> 11.4 us  [turn(): lax.ppermute(block, axis, [(i, (i + step) % size) for i in range(size)])]
    ppermute x6 -> x3, waiting for transfers between devices: 6.54 us -> 3.38 us  [turn(): lax.ppermute(block, axis, [(i, (i + step) % size) for i in range(size)])]
  transfers between devices with their start and end apart: 12 -> 9, of which waited for: 8 -> 6; matrix products, arithmetic and copies ran while one was open for 5% -> 5% of each run, Pallas kernels for 0% -> 0%
where the time goes in v4:
time: 145 us; the launch traced here: 144 us
  starting transfers between devices  48.1 us (33%)
  blocking collectives  45.7 us (32%)
  waiting for transfers between devices  30.4 us (21%)
  matrix products  6.2 us (4%)
  between operations  5.4 us (4%)
  local copies, waits for them, and re-layouts  5.26 us (4%)
  other arithmetic  2.81 us (2%)
    all_to_all x2, starting transfers between devices, scatter(): lax.all_to_all(own.reshape(members, -1, COLS), ('c', 'z', 'y'), 0, 0, til...  21 us
    ppermute x3, waiting for transfers between devices, swap(): return lax.ppermute(block, axis, [(0, 1), (1, 0)])  18.1 us
    all_to_all x1, blocking collectives, gather(): return lax.all_to_all(copies, ('z', 'y'), 0, 0, tiled=True)  16.6 us
    all_to_all x1, blocking collectives, shards(): summed = lax.all_to_all(copies, ('h', 'x'), 0, 0, tiled=True).sum(axis=0)  15.6 us
    all_gather x1, blocking collectives, shards(): full_g = lax.all_gather(part_g + other_g, 'x', axis=0, tiled=True)  13.4 us
    ppermute x3, starting transfers between devices, turn(): lax.ppermute(block, axis, [(i, (i + step) % size) for i in range(size)])  11.4 us
    ppermute x3, starting transfers between devices, swap(): return lax.ppermute(block, axis, [(0, 1), (1, 0)])  9.2 us
    all_to_all x2, waiting for transfers between devices, scatter(): lax.all_to_all(own.reshape(members, -1, COLS), ('c', 'z', 'y'), 0, 0, til...  8.92 us
  transfers between devices with their start and end apart: 9, of which 6 were waited for; matrix products, arithmetic and copies ran while one was open for 5% of the time, Pallas kernels for 0%

profile of v4, /device:TPU:24, one launch (start us, length us, event | category | flops | bytes accessed | tf_op | source)
XLA Modules:
  0.0 143.9 jit_solution(12660149710055420067)
XLA Ops:
  0.0 14.4 %all-to-all-start = ((bf16[64,16,128]{2,1,0:T(8,128)(2,1)}), bf16[64,16,128]{2,1,0:T(8,128)(2,1)S(1)}, u32[]{:S(2)}, u32[]{:S(2)}) async-start(bf16[64,16,128]{2,1,0:T(8,128)(2,1)} %bitcast.29), calls=%async_computation | async-start | bytes 524288 | tf_op jit(solution)/shard_map/all_to_all | solution.py:23
  14.4 1.3 fusion.17
  20.9 5.2 %all-to-all-done = bf16[64,16,128]{2,1,0:T(8,128)(2,1)S(1)} async-done(((bf16[64,16,128]{2,1,0:T(8,128)(2,1)}), bf16[64,16,128]{2,1,0:T(8,128)(2,1)S(1)}, u32[]{:S(2)}, u32[]{:S(2)}) %all-to-all-start) | async-done | bytes 262176 | tf_op jit(solution)/shard_map/all_to_all | solution.py:23
  26.2 16.6 %all_to_all.33 = bf16[32,16,256]{2,1,0:T(8,128)(2,1)S(1)} all-to-all(bf16[32,16,256]{2,1,0:T(8,128)(2,1)S(1)} %broadcast_in_dim.6), channel_id=1, replica_groups=mesh['z'=8,'y'=4,'c'=2,'h'=2,'x'=4] {'z','y'}, dimensions={0} | all-to-all | bytes 524288 | tf_op jit(solution)/shard_map/all_to_all | solution.py:38
  42.8 6.6 %all-to-all-start.2 = ((bf16[64,56,128]{2,1,0:T(8,128)(2,1)}), bf16[64,56,128]{2,1,0:T(8,128)(2,1)}, u32[]{:S(2)}, u32[]{:S(2)}) async-start(bf16[64,56,128]{2,1,0:T(8,128)(2,1)} %bitcast.28), calls=%async_computation.2 | async-start | bytes 1835008 | tf_op jit(solution)/shard_map/all_to_all | solution.py:23
  49.4 2.2 %collective-permute-start = (bf16[512,256]{1,0:T(8,128)(2,1)S(1)}, bf16[512,256]{1,0:T(8,128)(2,1)S(1)}, u32[]{:S(2)}, u32[]{:S(2)}) collective-permute-start(bf16[512,256]{1,0:T(8,128)(2,1)S(1)} %bitcast.26), channel_id=1, source_target_pairs={{0,8},{8,0},{1,9},{9,1},{2,10},{10,2},{3,11},{11,3},{4,12},{12,4},... | collective-permute-start | bytes 786440 | tf_op jit(solution)/shard_map/ppermute | solution.py:14
  51.7 1.3 fusion.6
  53.0 1.3 fusion.4
  55.1 3.4 %collective-permute-start.1 = (f32[104,256]{1,0:T(8,128)}, f32[104,256]{1,0:T(8,128)S(1)}, u32[]{:S(2)}, u32[]{:S(2)}) collective-permute-start(f32[104,256]{1,0:T(8,128)} %get-tuple-element.27), channel_id=1, source_target_pairs={{0,1},{1,2},{2,3},{3,0},{4,5},{5,6},{6,7},{7,4},{8,9},{9,10},{10,1... | collective-permute-start | bytes 319496 | tf_op jit(solution)/shard_map/ppermute | solution.py:18
  58.5 4.6 %collective-permute-start.2 = (f32[104,256]{1,0:T(8,128)}, f32[104,256]{1,0:T(8,128)}, u32[]{:S(2)}, u32[]{:S(2)}) collective-permute-start(f32[104,256]{1,0:T(8,128)} %get-tuple-element.29), channel_id=1, source_target_pairs={{0,2},{1,3},{2,0},{3,1},{4,6},{5,7},{6,4},{7,5},{8,10},{9,11},{10,... | collective-permute-start | bytes 319496 | tf_op jit(solution)/shard_map/ppermute | solution.py:18
  63.2 3.3 %collective-permute-start.3 = (f32[104,256]{1,0:T(8,128)}, f32[104,256]{1,0:T(8,128)}, u32[]{:S(2)}, u32[]{:S(2)}) collective-permute-start(f32[104,256]{1,0:T(8,128)} %get-tuple-element.28), channel_id=1, source_target_pairs={{0,3},{1,0},{2,1},{3,2},{4,7},{5,4},{6,5},{7,6},{8,11},{9,8},{10,9... | collective-permute-start | bytes 319496 | tf_op jit(solution)/shard_map/ppermute | solution.py:18
  67.1 2.9 %collective-permute-done.3 = f32[104,256]{1,0:T(8,128)} collective-permute-done((f32[104,256]{1,0:T(8,128)}, f32[104,256]{1,0:T(8,128)}, u32[]{:S(2)}, u32[]{:S(2)}) %collective-permute-start.3) | collective-permute-done | bytes 106528 | tf_op jit(solution)/shard_map/ppermute | solution.py:18
  70.1 1.0 add_add_fusion
  71.1 3.7 %all-to-all-done.2 = bf16[64,56,128]{2,1,0:T(8,128)(2,1)} async-done(((bf16[64,56,128]{2,1,0:T(8,128)(2,1)}), bf16[64,56,128]{2,1,0:T(8,128)(2,1)}, u32[]{:S(2)}, u32[]{:S(2)}) %all-to-all-start.2) | async-done | bytes 917536 | tf_op jit(solution)/shard_map/all_to_all | solution.py:23
  75.6 1.0 broadcast_in_dim.7
  76.6 6.5 %all-to-all-start.3 = ((bf16[32,56,256]{2,1,0:T(8,128)(2,1)}), bf16[32,56,256]{2,1,0:T(8,128)(2,1)}, u32[]{:S(2)}, u32[]{:S(2)}) async-start(bf16[32,56,256]{2,1,0:T(8,128)(2,1)} %broadcast_in_dim.7), calls=%async_computation.3 | async-start | bytes 1835008 | tf_op jit(solution)/shard_map/all_to_all | solution.py:38
  83.1 5.0 %collective-permute-start.4 = (f32[104,256]{1,0:T(8,128)S(1)}, f32[104,256]{1,0:T(8,128)S(1)}, u32[]{:S(2)}, u32[]{:S(2)}) collective-permute-start(f32[104,256]{1,0:T(8,128)S(1)} %add_add_fusion), channel_id=1, source_target_pairs={{0,4},{4,0},{1,5},{5,1},{2,6},{6,2},{3,7},{7,3},{8,12},{12,8},{9,1... | collective-permute-start | bytes 319496 | tf_op jit(solution)/shard_map/ppermute | solution.py:14
  88.2 17.3 %collective-permute-done.4 = f32[104,256]{1,0:T(8,128)S(1)} collective-permute-done((f32[104,256]{1,0:T(8,128)S(1)}, f32[104,256]{1,0:T(8,128)S(1)}, u32[]{:S(2)}, u32[]{:S(2)}) %collective-permute-start.4) | collective-permute-done | bytes 106528 | tf_op jit(solution)/shard_map/ppermute | solution.py:14
  105.5 13.4 %all_gather.3 = f32[416,256]{1,0:T(8,128)S(1)} all-gather(f32[104,256]{1,0:T(8,128)S(1)} %add.100), channel_id=1, replica_groups=mesh['z'=8,'y'=4,'c'=2,'h'=2,'x'=4] {'x'}, dimensions={0}, use_global_device_ids=true | all-gather | bytes 532480 | tf_op jit(solution)/shard_map/all_gather | solution.py:68
  118.9 1.9 %collective-permute-start.5 = (bf16[1792,256]{1,0:T(8,128)(2,1)}, bf16[1792,256]{1,0:T(8,128)(2,1)}, u32[]{:S(2)}, u32[]{:S(2)}) collective-permute-start(bf16[1792,256]{1,0:T(8,128)(2,1)} %bitcast.12), channel_id=1, source_target_pairs={{0,8},{8,0},{1,9},{9,1},{2,10},{10,2},{3,11},{11,3},{4,12},{12,4},... | collective-permute-start | bytes 2752520 | tf_op jit(solution)/shard_map/ppermute | solution.py:14
  121.0 1.7 %fusion.2 = f32[416,256]{1,0:T(8,128)S(1)} fusion(bf16[1792,256]{1,0:T(8,128)(2,1)} %bitcast.12, bf16[416,3584]{1,0:T(8,128)(2,1)S(1)} %copy-done, s32[]{:T(128)S(6)} %select_n.58), kind=kOutput, calls=%fused_computation.2 | convolution fusion | flops 381681664 | bytes 2834436 | tf_op jit(solution)/shard_map/dot_general | solution.py:45
  123.6 1.7 %fusion = f32[416,256]{1,0:T(8,128)S(1)} fusion(bf16[1792,256]{1,0:T(8,128)(2,1)} %collective-permute-done.5, bf16[416,3584]{1,0:T(8,128)(2,1)S(1)} %copy-done, s32[]{:T(128)S(6)} %select_n.71), kind=kOutput, calls=%fused_computation | convolution fusion | flops 381681664 | bytes 2834436 | tf_op jit(solution)/shard_map/dot_general | solution.py:47
  126.2 1.2 copy.9
  127.6 15.6 %all_to_all.34 = f32[8,8,8]{2,1,0:T(8,128)S(1)} all-to-all(f32[8,8,8]{2,1,0:T(8,128)S(1)} %broadcast_in_dim.8), channel_id=1, replica_groups=mesh['z'=8,'y'=4,'c'=2,'h'=2,'x'=4] {'h','x'}, dimensions={0} | all-to-all | bytes 4096 | tf_op jit(solution)/shard_map/all_to_all | solution.py:86
  (27 shorter events, 5.0 us)
Async XLA Ops:
  0.0 121.0 %copy-start = (bf16[416,3584]{1,0:T(8,128)(2,1)S(1)}, bf16[416,3584]{1,0:T(8,128)(2,1)}, u32[]{:S(2)}) copy-start(bf16[416,3584]{1,0:T(8,128)(2,1)} %param.6) | copy-start | bytes 8945668
  0.0 26.1 %all-to-all-start = ((bf16[64,16,128]{2,1,0:T(8,128)(2,1)}), bf16[64,16,128]{2,1,0:T(8,128)(2,1)S(1)}, u32[]{:S(2)}, u32[]{:S(2)}) async-start(bf16[64,16,128]{2,1,0:T(8,128)(2,1)} %bitcast.29), calls=%async_computation | async-start | bytes 524288 | tf_op jit(solution)/shard_map/all_to_all | solution.py:23
  42.8 32.0 %all-to-all-start.2 = ((bf16[64,56,128]{2,1,0:T(8,128)(2,1)}), bf16[64,56,128]{2,1,0:T(8,128)(2,1)}, u32[]{:S(2)}, u32[]{:S(2)}) async-start(bf16[64,56,128]{2,1,0:T(8,128)(2,1)} %bitcast.28), calls=%async_computation.2 | async-start | bytes 1835008 | tf_op jit(solution)/shard_map/all_to_all | solution.py:23
  49.4 3.6 %collective-permute-start = (bf16[512,256]{1,0:T(8,128)(2,1)S(1)}, bf16[512,256]{1,0:T(8,128)(2,1)S(1)}, u32[]{:S(2)}, u32[]{:S(2)}) collective-permute-start(bf16[512,256]{1,0:T(8,128)(2,1)S(1)} %bitcast.26), channel_id=1, source_target_pairs={{0,8},{8,0},{1,9},{9,1},{2,10},{10,2},{3,11},{11,3},{4,12},{12,4},... | collective-permute-start | bytes 786440 | tf_op jit(solution)/shard_map/ppermute | solution.py:14
  54.3 66.5 %copy-start.2 = (s32[1,8]{1,0:T(1,128)S(1)}, s32[1,8]{1,0:T(1,128)}, u32[]{:S(2)}) copy-start(s32[1,8]{1,0:T(1,128)} %param.10) | copy-start | bytes 100
  55.1 11.4 %collective-permute-start.1 = (f32[104,256]{1,0:T(8,128)}, f32[104,256]{1,0:T(8,128)S(1)}, u32[]{:S(2)}, u32[]{:S(2)}) collective-permute-start(f32[104,256]{1,0:T(8,128)} %get-tuple-element.27), channel_id=1, source_target_pairs={{0,1},{1,2},{2,3},{3,0},{4,5},{5,6},{6,7},{7,4},{8,9},{9,10},{10,1... | collective-permute-start | bytes 319496 | tf_op jit(solution)/shard_map/ppermute | solution.py:18
  58.5 8.5 %collective-permute-start.2 = (f32[104,256]{1,0:T(8,128)}, f32[104,256]{1,0:T(8,128)}, u32[]{:S(2)}, u32[]{:S(2)}) collective-permute-start(f32[104,256]{1,0:T(8,128)} %get-tuple-element.29), channel_id=1, source_target_pairs={{0,2},{1,3},{2,0},{3,1},{4,6},{5,7},{6,4},{7,5},{8,10},{9,11},{10,... | collective-permute-start | bytes 319496 | tf_op jit(solution)/shard_map/ppermute | solution.py:18
  63.2 6.9 %collective-permute-start.3 = (f32[104,256]{1,0:T(8,128)}, f32[104,256]{1,0:T(8,128)}, u32[]{:S(2)}, u32[]{:S(2)}) collective-permute-start(f32[104,256]{1,0:T(8,128)} %get-tuple-element.28), channel_id=1, source_target_pairs={{0,3},{1,0},{2,1},{3,2},{4,7},{5,4},{6,5},{7,6},{8,11},{9,8},{10,9... | collective-permute-start | bytes 319496 | tf_op jit(solution)/shard_map/ppermute | solution.py:18
  66.5 0.6 copy-start.1
  76.6 42.3 %all-to-all-start.3 = ((bf16[32,56,256]{2,1,0:T(8,128)(2,1)}), bf16[32,56,256]{2,1,0:T(8,128)(2,1)}, u32[]{:S(2)}, u32[]{:S(2)}) async-start(bf16[32,56,256]{2,1,0:T(8,128)(2,1)} %broadcast_in_dim.7), calls=%async_computation.3 | async-start | bytes 1835008 | tf_op jit(solution)/shard_map/all_to_all | solution.py:38
  83.1 22.3 %collective-permute-start.4 = (f32[104,256]{1,0:T(8,128)S(1)}, f32[104,256]{1,0:T(8,128)S(1)}, u32[]{:S(2)}, u32[]{:S(2)}) collective-permute-start(f32[104,256]{1,0:T(8,128)S(1)} %add_add_fusion), channel_id=1, source_target_pairs={{0,4},{4,0},{1,5},{5,1},{2,6},{6,2},{3,7},{7,3},{8,12},{12,8},{9,1... | collective-permute-start | bytes 319496 | tf_op jit(solution)/shard_map/ppermute | solution.py:14
  118.9 4.7 %collective-permute-start.5 = (bf16[1792,256]{1,0:T(8,128)(2,1)}, bf16[1792,256]{1,0:T(8,128)(2,1)}, u32[]{:S(2)}, u32[]{:S(2)}) collective-permute-start(bf16[1792,256]{1,0:T(8,128)(2,1)} %bitcast.12), channel_id=1, source_target_pairs={{0,8},{8,0},{1,9},{9,1},{2,10},{10,2},{3,11},{11,3},{4,12},{12,4},... | collective-permute-start | bytes 2752520 | tf_op jit(solution)/shard_map/ppermute | solution.py:14

commit v5 on v4

--- a/solution.py
+++ b/solution.py
@@ -63,10 +63,10 @@
     mine_r = gather(pick(scatter(right_factors), owners))
     left_factors, mine_r = lax.optimization_barrier((left_factors, mine_r))
     part_g = sum_x(project(out_grads, mine_r, swap(mine_r, "c"), core), at_x)
-    other_g = swap(part_g, "h")
-    got_l, part_g = lax.optimization_barrier((scatter(left_factors), part_g))
-    full_g = lax.all_gather(part_g + other_g, "x", axis=0, tiled=True)
-    mine_l, full_g = lax.optimization_barrier((gather(pick(got_l, owners)), full_g))
+    picked_l = pick(scatter(left_factors), owners)
+    picked_l, part_g = lax.optimization_barrier((picked_l, part_g + swap(part_g, "h")))
+    full_g = lax.all_gather(part_g, "x", axis=0, tiled=True)
+    mine_l, full_g = lax.optimization_barrier((gather(picked_l), full_g))
 
     part_h = project(hidden_acts, mine_l, swap(mine_l, "c"), core)
     token_score = (part_h * full_g).reshape(tok_rows, 2 * QB, RANK).sum(axis=2)

time: 145 us -> 147 us (1.014)
  the two profiles are of different devices: /device:TPU:24 before, /device:TPU:1 now
where the time goes in v5:
time: 147 us; the launch traced here: 146 us
  starting transfers between devices  56.8 us (39%)
  blocking collectives  40.9 us (28%)
  waiting for transfers between devices  28.5 us (19%)
  matrix products  6.21 us (4%)
  between operations  5.37 us (4%)
  local copies, waits for them, and re-layouts  5.13 us (3%)
  other arithmetic  2.76 us (2%)
    all_to_all x2, starting transfers between devices, scatter(): lax.all_to_all(own.reshape(members, -1, COLS), ('c', 'z', 'y'), 0, 0, til...  23.2 us
    all_to_all x1, blocking collectives, gather(): return lax.all_to_all(copies, ('z', 'y'), 0, 0, tiled=True)  15.6 us
    all_to_all x1, blocking collectives, shards(): summed = lax.all_to_all(copies, ('h', 'x'), 0, 0, tiled=True).sum(axis=0)  15 us
    all_to_all x1, waiting for transfers between devices, gather(): return lax.all_to_all(copies, ('z', 'y'), 0, 0, tiled=True)  14.8 us
    ppermute x3, starting transfers between devices, swap(): return lax.ppermute(block, axis, [(0, 1), (1, 0)])  12.2 us
    all_to_all x1, starting transfers between devices, gather(): return lax.all_to_all(copies, ('z', 'y'), 0, 0, tiled=True)  11 us
    ppermute x3, starting transfers between devices, turn(): lax.ppermute(block, axis, [(i, (i + step) % size) for i in range(size)])  10.5 us
    all_gather x1, blocking collectives, shards(): full_g = lax.all_gather(part_g, 'x', axis=0, tiled=True)  10.3 us
  transfers between devices with their start and end apart: 9, of which 6 were waited for; matrix products, arithmetic and copies ran while one was open for 5% of the time, Pallas kernels for 0%

profile of v5, /device:TPU:1, one launch (start us, length us, event | category | flops | bytes accessed | tf_op | source)
XLA Modules:
  0.0 145.8 jit_solution(12316709015833174409)
XLA Ops:
  0.0 15.8 %all-to-all-start = ((bf16[64,16,128]{2,1,0:T(8,128)(2,1)}), bf16[64,16,128]{2,1,0:T(8,128)(2,1)S(1)}, u32[]{:S(2)}, u32[]{:S(2)}) async-start(bf16[64,16,128]{2,1,0:T(8,128)(2,1)} %bitcast.29), calls=%async_computation | async-start | bytes 524288 | tf_op jit(solution)/shard_map/all_to_all | solution.py:23
  15.8 1.4 fusion.17
  22.3 5.5 %all-to-all-done = bf16[64,16,128]{2,1,0:T(8,128)(2,1)S(1)} async-done(((bf16[64,16,128]{2,1,0:T(8,128)(2,1)}), bf16[64,16,128]{2,1,0:T(8,128)(2,1)S(1)}, u32[]{:S(2)}, u32[]{:S(2)}) %all-to-all-start) | async-done | bytes 262176 | tf_op jit(solution)/shard_map/all_to_all | solution.py:23
  27.9 15.6 %all_to_all.33 = bf16[32,16,256]{2,1,0:T(8,128)(2,1)S(1)} all-to-all(bf16[32,16,256]{2,1,0:T(8,128)(2,1)S(1)} %broadcast_in_dim.6), channel_id=1, replica_groups=mesh['z'=8,'y'=4,'c'=2,'h'=2,'x'=4] {'z','y'}, dimensions={0} | all-to-all | bytes 524288 | tf_op jit(solution)/shard_map/all_to_all | solution.py:38
  43.5 7.4 %all-to-all-start.2 = ((bf16[64,56,128]{2,1,0:T(8,128)(2,1)}), bf16[64,56,128]{2,1,0:T(8,128)(2,1)}, u32[]{:S(2)}, u32[]{:S(2)}) async-start(bf16[64,56,128]{2,1,0:T(8,128)(2,1)} %bitcast.28), calls=%async_computation.2 | async-start | bytes 1835008 | tf_op jit(solution)/shard_map/all_to_all | solution.py:23
  50.9 2.3 %collective-permute-start = (bf16[512,256]{1,0:T(8,128)(2,1)S(1)}, bf16[512,256]{1,0:T(8,128)(2,1)S(1)}, u32[]{:S(2)}, u32[]{:S(2)}) collective-permute-start(bf16[512,256]{1,0:T(8,128)(2,1)S(1)} %bitcast.26), channel_id=1, source_target_pairs={{0,8},{8,0},{1,9},{9,1},{2,10},{10,2},{3,11},{11,3},{4,12},{12,4},... | collective-permute-start | bytes 786440 | tf_op jit(solution)/shard_map/ppermute | solution.py:14
  53.3 1.3 fusion.6
  54.6 1.3 fusion.4
  56.7 3.1 %collective-permute-start.1 = (f32[104,256]{1,0:T(8,128)}, f32[104,256]{1,0:T(8,128)S(1)}, u32[]{:S(2)}, u32[]{:S(2)}) collective-permute-start(f32[104,256]{1,0:T(8,128)} %get-tuple-element.27), channel_id=1, source_target_pairs={{0,1},{1,2},{2,3},{3,0},{4,5},{5,6},{6,7},{7,4},{8,9},{9,10},{10,1... | collective-permute-start | bytes 319496 | tf_op jit(solution)/shard_map/ppermute | solution.py:18
  59.8 4.4 %collective-permute-start.2 = (f32[104,256]{1,0:T(8,128)}, f32[104,256]{1,0:T(8,128)}, u32[]{:S(2)}, u32[]{:S(2)}) collective-permute-start(f32[104,256]{1,0:T(8,128)} %get-tuple-element.29), channel_id=1, source_target_pairs={{0,2},{1,3},{2,0},{3,1},{4,6},{5,7},{6,4},{7,5},{8,10},{9,11},{10,... | collective-permute-start | bytes 319496 | tf_op jit(solution)/shard_map/ppermute | solution.py:18
  64.2 3.1 %collective-permute-start.3 = (f32[104,256]{1,0:T(8,128)}, f32[104,256]{1,0:T(8,128)}, u32[]{:S(2)}, u32[]{:S(2)}) collective-permute-start(f32[104,256]{1,0:T(8,128)} %get-tuple-element.28), channel_id=1, source_target_pairs={{0,3},{1,0},{2,1},{3,2},{4,7},{5,4},{6,5},{7,6},{8,11},{9,8},{10,9... | collective-permute-start | bytes 319496 | tf_op jit(solution)/shard_map/ppermute | solution.py:18
  67.6 2.6 %collective-permute-done.3 = f32[104,256]{1,0:T(8,128)} collective-permute-done((f32[104,256]{1,0:T(8,128)}, f32[104,256]{1,0:T(8,128)}, u32[]{:S(2)}, u32[]{:S(2)}) %collective-permute-start.3) | collective-permute-done | bytes 106528 | tf_op jit(solution)/shard_map/ppermute | solution.py:18
  70.2 1.0 add_add_fusion
  71.2 4.8 %collective-permute-start.4 = (f32[104,256]{1,0:T(8,128)S(1)}, f32[104,256]{1,0:T(8,128)S(1)}, u32[]{:S(2)}, u32[]{:S(2)}) collective-permute-start(f32[104,256]{1,0:T(8,128)S(1)} %add_add_fusion), channel_id=1, source_target_pairs={{0,4},{4,0},{1,5},{5,1},{2,6},{6,2},{3,7},{7,3},{8,12},{12,8},{9,1... | collective-permute-start | bytes 319496 | tf_op jit(solution)/shard_map/ppermute | solution.py:14
  76.0 4.7 %collective-permute-done.4 = f32[104,256]{1,0:T(8,128)S(1)} collective-permute-done((f32[104,256]{1,0:T(8,128)S(1)}, f32[104,256]{1,0:T(8,128)S(1)}, u32[]{:S(2)}, u32[]{:S(2)}) %collective-permute-start.4) | collective-permute-done | bytes 106528 | tf_op jit(solution)/shard_map/ppermute | solution.py:14
  81.4 1.0 broadcast_in_dim.7
  82.5 11.0 %all-to-all-start.3 = ((bf16[32,56,256]{2,1,0:T(8,128)(2,1)}), bf16[32,56,256]{2,1,0:T(8,128)(2,1)}, u32[]{:S(2)}, u32[]{:S(2)}) async-start(bf16[32,56,256]{2,1,0:T(8,128)(2,1)} %broadcast_in_dim.7), calls=%async_computation.3 | async-start | bytes 1835008 | tf_op jit(solution)/shard_map/all_to_all | solution.py:38
  93.4 10.3 %all_gather.3 = f32[416,256]{1,0:T(8,128)S(1)} all-gather(f32[104,256]{1,0:T(8,128)S(1)} %add.100), channel_id=1, replica_groups=mesh['z'=8,'y'=4,'c'=2,'h'=2,'x'=4] {'x'}, dimensions={0}, use_global_device_ids=true | all-gather | bytes 532480 | tf_op jit(solution)/shard_map/all_gather | solution.py:68
  103.7 14.8 %all-to-all-done.3 = bf16[32,56,256]{2,1,0:T(8,128)(2,1)} async-done(((bf16[32,56,256]{2,1,0:T(8,128)(2,1)}), bf16[32,56,256]{2,1,0:T(8,128)(2,1)}, u32[]{:S(2)}, u32[]{:S(2)}) %all-to-all-start.3) | async-done | bytes 917536 | tf_op jit(solution)/shard_map/all_to_all | solution.py:38
  118.5 5.1 %collective-permute-start.5 = (bf16[1792,256]{1,0:T(8,128)(2,1)}, bf16[1792,256]{1,0:T(8,128)(2,1)}, u32[]{:S(2)}, u32[]{:S(2)}) collective-permute-start(bf16[1792,256]{1,0:T(8,128)(2,1)} %bitcast.12), channel_id=1, source_target_pairs={{0,8},{8,0},{1,9},{9,1},{2,10},{10,2},{3,11},{11,3},{4,12},{12,4},... | collective-permute-start | bytes 2752520 | tf_op jit(solution)/shard_map/ppermute | solution.py:14
  123.8 1.7 %fusion.2 = f32[416,256]{1,0:T(8,128)S(1)} fusion(bf16[1792,256]{1,0:T(8,128)(2,1)} %bitcast.12, bf16[416,3584]{1,0:T(8,128)(2,1)S(1)} %copy-done, s32[]{:T(128)S(6)} %select_n.58), kind=kOutput, calls=%fused_computation.2 | convolution fusion | flops 381681664 | bytes 2834436 | tf_op jit(solution)/shard_map/dot_general | solution.py:45
  126.1 1.7 %fusion = f32[416,256]{1,0:T(8,128)S(1)} fusion(bf16[1792,256]{1,0:T(8,128)(2,1)} %collective-permute-done.5, bf16[416,3584]{1,0:T(8,128)(2,1)S(1)} %copy-done, s32[]{:T(128)S(6)} %select_n.71), kind=kOutput, calls=%fused_computation | convolution fusion | flops 381681664 | bytes 2834436 | tf_op jit(solution)/shard_map/dot_general | solution.py:47
  128.6 1.2 copy.9
  130.1 15.0 %all_to_all.34 = f32[8,8,8]{2,1,0:T(8,128)S(1)} all-to-all(f32[8,8,8]{2,1,0:T(8,128)S(1)} %broadcast_in_dim.8), channel_id=1, replica_groups=mesh['z'=8,'y'=4,'c'=2,'h'=2,'x'=4] {'h','x'}, dimensions={0} | all-to-all | bytes 4096 | tf_op jit(solution)/shard_map/all_to_all | solution.py:86
  (25 shorter events, 4.3 us)
Async XLA Ops:
  0.0 123.8 %copy-start = (bf16[416,3584]{1,0:T(8,128)(2,1)S(1)}, bf16[416,3584]{1,0:T(8,128)(2,1)}, u32[]{:S(2)}) copy-start(bf16[416,3584]{1,0:T(8,128)(2,1)} %param.6) | copy-start | bytes 8945668
  0.0 27.8 %all-to-all-start = ((bf16[64,16,128]{2,1,0:T(8,128)(2,1)}), bf16[64,16,128]{2,1,0:T(8,128)(2,1)S(1)}, u32[]{:S(2)}, u32[]{:S(2)}) async-start(bf16[64,16,128]{2,1,0:T(8,128)(2,1)} %bitcast.29), calls=%async_computation | async-start | bytes 524288 | tf_op jit(solution)/shard_map/all_to_all | solution.py:23
  43.5 37.2 %all-to-all-start.2 = ((bf16[64,56,128]{2,1,0:T(8,128)(2,1)}), bf16[64,56,128]{2,1,0:T(8,128)(2,1)}, u32[]{:S(2)}, u32[]{:S(2)}) async-start(bf16[64,56,128]{2,1,0:T(8,128)(2,1)} %bitcast.28), calls=%async_computation.2 | async-start | bytes 1835008 | tf_op jit(solution)/shard_map/all_to_all | solution.py:23
  50.9 3.7 %collective-permute-start = (bf16[512,256]{1,0:T(8,128)(2,1)S(1)}, bf16[512,256]{1,0:T(8,128)(2,1)S(1)}, u32[]{:S(2)}, u32[]{:S(2)}) collective-permute-start(bf16[512,256]{1,0:T(8,128)(2,1)S(1)} %bitcast.26), channel_id=1, source_target_pairs={{0,8},{8,0},{1,9},{9,1},{2,10},{10,2},{3,11},{11,3},{4,12},{12,4},... | collective-permute-start | bytes 786440 | tf_op jit(solution)/shard_map/ppermute | solution.py:14
  55.8 67.8 %copy-start.1 = (s32[1,8]{1,0:T(1,128)S(1)}, s32[1,8]{1,0:T(1,128)}, u32[]{:S(2)}) copy-start(s32[1,8]{1,0:T(1,128)} %param.10) | copy-start | bytes 100
  56.7 10.5 %collective-permute-start.1 = (f32[104,256]{1,0:T(8,128)}, f32[104,256]{1,0:T(8,128)S(1)}, u32[]{:S(2)}, u32[]{:S(2)}) collective-permute-start(f32[104,256]{1,0:T(8,128)} %get-tuple-element.27), channel_id=1, source_target_pairs={{0,1},{1,2},{2,3},{3,0},{4,5},{5,6},{6,7},{7,4},{8,9},{9,10},{10,1... | collective-permute-start | bytes 319496 | tf_op jit(solution)/shard_map/ppermute | solution.py:18
  59.8 7.8 %collective-permute-start.2 = (f32[104,256]{1,0:T(8,128)}, f32[104,256]{1,0:T(8,128)}, u32[]{:S(2)}, u32[]{:S(2)}) collective-permute-start(f32[104,256]{1,0:T(8,128)} %get-tuple-element.29), channel_id=1, source_target_pairs={{0,2},{1,3},{2,0},{3,1},{4,6},{5,7},{6,4},{7,5},{8,10},{9,11},{10,... | collective-permute-start | bytes 319496 | tf_op jit(solution)/shard_map/ppermute | solution.py:18
  64.2 6.1 %collective-permute-start.3 = (f32[104,256]{1,0:T(8,128)}, f32[104,256]{1,0:T(8,128)}, u32[]{:S(2)}, u32[]{:S(2)}) collective-permute-start(f32[104,256]{1,0:T(8,128)} %get-tuple-element.28), channel_id=1, source_target_pairs={{0,3},{1,0},{2,1},{3,2},{4,7},{5,4},{6,5},{7,6},{8,11},{9,8},{10,9... | collective-permute-start | bytes 319496 | tf_op jit(solution)/shard_map/ppermute | solution.py:18
  71.2 9.5 %collective-permute-start.4 = (f32[104,256]{1,0:T(8,128)S(1)}, f32[104,256]{1,0:T(8,128)S(1)}, u32[]{:S(2)}, u32[]{:S(2)}) collective-permute-start(f32[104,256]{1,0:T(8,128)S(1)} %add_add_fusion), channel_id=1, source_target_pairs={{0,4},{4,0},{1,5},{5,1},{2,6},{6,2},{3,7},{7,3},{8,12},{12,8},{9,1... | collective-permute-start | bytes 319496 | tf_op jit(solution)/shard_map/ppermute | solution.py:14
  82.5 36.1 %all-to-all-start.3 = ((bf16[32,56,256]{2,1,0:T(8,128)(2,1)}), bf16[32,56,256]{2,1,0:T(8,128)(2,1)}, u32[]{:S(2)}, u32[]{:S(2)}) async-start(bf16[32,56,256]{2,1,0:T(8,128)(2,1)} %broadcast_in_dim.7), calls=%async_computation.3 | async-start | bytes 1835008 | tf_op jit(solution)/shard_map/all_to_all | solution.py:38
  118.5 7.5 %collective-permute-start.5 = (bf16[1792,256]{1,0:T(8,128)(2,1)}, bf16[1792,256]{1,0:T(8,128)(2,1)}, u32[]{:S(2)}, u32[]{:S(2)}) collective-permute-start(bf16[1792,256]{1,0:T(8,128)(2,1)} %bitcast.12), channel_id=1, source_target_pairs={{0,8},{8,0},{1,9},{9,1},{2,10},{10,2},{3,11},{11,3},{4,12},{12,4},... | collective-permute-start | bytes 2752520 | tf_op jit(solution)/shard_map/ppermute | solution.py:14

commit v6 on v5

v6 whole, which is shorter than its diff:
```python
import jax
import jax.numpy as jnp
from jax import lax
from jax.sharding import Mesh
from jax.sharding import PartitionSpec as P

QB = 4
RANK = 32
COLS = QB * RANK
Z, Y, C, H, X = 8, 4, 2, 2, 4


def swap(block, axis):
    return lax.ppermute(block, axis, [(0, 1), (1, 0)])


def pick(got, owners):
    picked = []
    for batch in range(2):
        owner = owners[batch]
        source = (owner % C) * (Z * Y) + owner // C
        picked.append(lax.dynamic_index_in_dim(got, source, 0, keepdims=False))
    return jnp.concatenate(picked, axis=1)


def dot(acts, part, side):
    rows = part.shape[0]
    acts = lax.dynamic_slice_in_dim(acts, side * rows, rows, 1)
    return jnp.dot(acts, part, preferred_element_type=jnp.float32)


def sum_x(proj):
    parts = lax.all_to_all(proj, "x", 0, 0, tiled=True)
    return parts.reshape(X, -1, proj.shape[1]).sum(axis=0)


def shards(hidden_acts, out_grads, left_factors, right_factors, doc_tokens, owners):
    tok_rows = hidden_acts.shape[0]
    core, at_x = lax.axis_index("c"), lax.axis_index("x")
    share = tok_rows // X

    right, left = right_factors[0], left_factors[0]
    rows_r, rows_l = right.shape[0] // C, left.shape[0] // C
    own = jnp.concatenate([right[:rows_r], left[:rows_l], right[rows_r:], left[rows_l:]], axis=0)
    own = own.reshape(Z * Y * C, -1, COLS)
    picked = pick(lax.all_to_all(own, ("c", "z", "y"), 0, 0, tiled=True), owners)

    copies = jnp.broadcast_to(picked[None], (Z * Y, *picked.shape))
    mine = lax.all_to_all(copies, ("z", "y"), 0, 0, tiled=True).reshape(-1, 2 * COLS)
    other = swap(mine, "c")

    near_g = dot(out_grads, mine[:rows_r], core)
    near_h = dot(hidden_acts, mine[rows_r:], core)
    near_g, near_h, other = lax.optimization_barrier((near_g, near_h, other))
    proj_g = near_g + dot(out_grads, other[:rows_r], 1 - core)
    proj_h = near_h + dot(hidden_acts, other[rows_r:], 1 - core)

    part_g = sum_x(proj_g)
    part_h = sum_x(proj_h)
    full_g = part_g + swap(part_g, "h")
    full_h = part_h + swap(part_h, "h")
    token_score = (full_h * full_g).reshape(share, 2 * QB, RANK).sum(axis=2)

    counts = doc_tokens[0]
    ends = jnp.cumsum(counts)
    starts = ends - counts
    places = jnp.arange(share, dtype=jnp.int32) + at_x * share
    inside = ((places[None, :] >= starts[:, None]) & (places[None, :] < ends[:, None])).astype(
        jnp.float32
    )
    partial = jnp.dot(
        inside, token_score, precision=lax.Precision.HIGHEST, preferred_element_type=jnp.float32
    )
    copies = jnp.broadcast_to(partial[None], (X, *partial.shape))
    summed = lax.all_to_all(copies, "x", 0, 0, tiled=True).sum(axis=0)
    return summed / jnp.sqrt(jnp.float32(RANK * (tok_rows // 4)))


def solution(mesh):
    fine = Mesh(mesh.devices.reshape(Z, Y, C, H, X), ("z", "y", "c", "h", "x"))
    dp, tensor = ("z", "y", "c"), ("h", "x")
    return jax.shard_map(
        shards,
        mesh=fine,
        in_specs=(
            P(dp, tensor),
            P(dp, tensor),
            P(dp, tensor, None),
            P(dp, tensor, None),
            P(dp, None),
            P(),
        ),
        out_specs=P(dp, None),
        check_vma=False,
    )
```

time: 147 us -> 142 us (0.966)
  the two profiles are of different devices: /device:TPU:1 before, /device:TPU:56 now
where the time goes in v6:
time: 142 us; the launch traced here: 140 us
  blocking collectives  45 us (32%)
  waiting for transfers between devices  40.9 us (29%)
  starting transfers between devices  33.5 us (24%)
  matrix products  6.35 us (4%)
  other arithmetic  6.29 us (4%)
  between operations  5.07 us (4%)
  local copies, waits for them, and re-layouts  2.9 us (2%)
    all_to_all x1, blocking collectives, shards(): lax.all_to_all(copies, ('z', 'y'), 0, 0, tiled=True).reshape(-1, 2 * COLS)  36.9 us
    all_to_all x1, waiting for transfers between devices, shards(): lax.all_to_all(own, ('c', 'z', 'y'), 0, 0, tiled=True)  25.4 us
    all_to_all x1, starting transfers between devices, shards(): lax.all_to_all(own, ('c', 'z', 'y'), 0, 0, tiled=True)  14.4 us
    ppermute x3, starting transfers between devices, swap(): return lax.ppermute(block, axis, [(0, 1), (1, 0)])  11.3 us
    all_to_all x2, waiting for transfers between devices, sum_x(): parts = lax.all_to_all(proj, 'x', 0, 0, tiled=True)  9.43 us
    all_to_all x1, blocking collectives, shards(): summed = lax.all_to_all(copies, 'x', 0, 0, tiled=True).sum(axis=0)  8.09 us
    all_to_all x2, starting transfers between devices, sum_x(): parts = lax.all_to_all(proj, 'x', 0, 0, tiled=True)  7.75 us
    dot_general x4, matrix products, dot(): return jnp.dot(acts, part, preferred_element_type=jnp.float32)  6.17 us
  transfers between devices with their start and end apart: 6, of which 4 were waited for; matrix products, arithmetic and copies ran while one was open for 6% of the time, Pallas kernels for 0%

profile of v6, /device:TPU:56, one launch (start us, length us, event | category | flops | bytes accessed | tf_op | source)
XLA Modules:
  0.0 140.0 jit_solution(13107808562943920968)
XLA Ops:
  0.0 1.4 slice_bitcast_fusion.1
  1.4 1.1 pad_maximum_fusion
  2.6 14.4 %all-to-all-start = ((bf16[64,72,128]{2,1,0:T(8,128)(2,1)}), bf16[64,72,128]{2,1,0:T(8,128)(2,1)}, u32[]{:S(2)}, u32[]{:S(2)}) async-start(bf16[64,72,128]{2,1,0:T(8,128)(2,1)} %bitcast.26), calls=%async_computation | async-start | bytes 2359296 | tf_op jit(solution)/shard_map/all_to_all | solution.py:46
  22.5 25.4 %all-to-all-done = bf16[64,72,128]{2,1,0:T(8,128)(2,1)} async-done(((bf16[64,72,128]{2,1,0:T(8,128)(2,1)}), bf16[64,72,128]{2,1,0:T(8,128)(2,1)}, u32[]{:S(2)}, u32[]{:S(2)}) %all-to-all-start) | async-done | bytes 1179680 | tf_op jit(solution)/shard_map/all_to_all | solution.py:46
  47.8 0.7 dynamic-slice_bitcast_fusion.1
  48.7 36.9 %all_to_all.33 = bf16[32,72,256]{2,1,0:T(8,128)(2,1)} all-to-all(bf16[32,72,256]{2,1,0:T(8,128)(2,1)S(1)} %broadcast_in_dim.4), channel_id=1, replica_groups=mesh['z'=8,'y'=4,'c'=2,'h'=2,'x'=4] {'z','y'}, dimensions={0} | all-to-all | bytes 2359296 | tf_op jit(solution)/shard_map/all_to_all | solution.py:49
  85.6 1.9 %collective-permute-start = (bf16[2304,256]{1,0:T(8,128)(2,1)}, bf16[2304,256]{1,0:T(8,128)(2,1)}, u32[]{:S(2)}, u32[]{:S(2)}) collective-permute-start(bf16[2304,256]{1,0:T(8,128)(2,1)} %bitcast.12), channel_id=1, source_target_pairs={{0,8},{8,0},{1,9},{9,1},{2,10},{10,2},{3,11},{11,3},{4,12},{12,4},... | collective-permute-start | bytes 3538952 | tf_op jit(solution)/shard_map/ppermute | solution.py:14
  87.5 1.4 fusion.8
  88.9 1.7 %fusion.2 = f32[416,256]{1,0:T(8,128)S(1)} fusion(bf16[416,3584]{1,0:T(8,128)(2,1)S(1)} %copy-done, s32[]{:T(128)S(6)} %select_n.44, bf16[2304,256]{1,0:T(8,128)(2,1)} %bitcast.12), kind=kOutput, calls=%fused_computation.2 | convolution fusion | flops 381681664 | bytes 2834436 | tf_op jit(solution)/shard_map/dot_general | solution.py:29
  90.7 1.7 %fusion = f32[416,256]{1,0:T(8,128)S(1)} fusion(bf16[416,3584]{1,0:T(8,128)(2,1)S(1)} %copy-done, s32[]{:T(128)S(6)} %select_n.45, bf16[2304,256]{1,0:T(8,128)(2,1)} %collective-permute-done), kind=kOutput, calls=%fused_computation | convolution fusion | flops 381681664 | bytes 2834436 | tf_op jit(solution)/shard_map/dot_general | solution.py:29
  92.4 0.8 add.67
  93.2 4.3 %all-to-all-start.2 = ((f32[4,104,256]{2,1,0:T(8,128)}), f32[4,104,256]{2,1,0:T(8,128)}, u32[]{:S(2)}, u32[]{:S(2)}) async-start(f32[4,104,256]{2,1,0:T(8,128)} %bitcast.28), calls=%async_computation.2 | async-start | bytes 851968 | tf_op jit(solution)/shard_map/all_to_all | solution.py:33
  97.5 1.3 fusion.6
  98.9 0.8 add.70
  99.7 7.1 %all-to-all-done.2 = f32[4,104,256]{2,1,0:T(8,128)} async-done(((f32[4,104,256]{2,1,0:T(8,128)}), f32[4,104,256]{2,1,0:T(8,128)}, u32[]{:S(2)}, u32[]{:S(2)}) %all-to-all-start.2) | async-done | bytes 426016 | tf_op jit(solution)/shard_map/all_to_all | solution.py:33
  106.8 3.5 %all-to-all-start.3 = ((f32[4,104,256]{2,1,0:T(8,128)}), f32[4,104,256]{2,1,0:T(8,128)S(1)}, u32[]{:S(2)}, u32[]{:S(2)}) async-start(f32[4,104,256]{2,1,0:T(8,128)} %bitcast.27), calls=%async_computation.3 | async-start | bytes 851968 | tf_op jit(solution)/shard_map/all_to_all | solution.py:33
  110.5 1.0 reduce_sum.36
  111.5 4.7 %collective-permute-start.1 = (f32[104,256]{1,0:T(8,128)S(1)}, f32[104,256]{1,0:T(8,128)}, u32[]{:S(2)}, u32[]{:S(2)}) collective-permute-start(f32[104,256]{1,0:T(8,128)S(1)} %reduce_sum.36), channel_id=1, source_target_pairs={{0,4},{4,0},{1,5},{5,1},{2,6},{6,2},{3,7},{7,3},{8,12},{12,8},{9,1... | collective-permute-start | bytes 319496 | tf_op jit(solution)/shard_map/ppermute | solution.py:14
  116.2 2.3 %all-to-all-done.3 = f32[4,104,256]{2,1,0:T(8,128)S(1)} async-done(((f32[4,104,256]{2,1,0:T(8,128)}), f32[4,104,256]{2,1,0:T(8,128)S(1)}, u32[]{:S(2)}, u32[]{:S(2)}) %all-to-all-start.3) | async-done | bytes 426016 | tf_op jit(solution)/shard_map/all_to_all | solution.py:33
  118.6 0.7 reduce_sum.37
  119.2 4.7 %collective-permute-start.2 = (f32[104,256]{1,0:T(8,128)}, f32[104,256]{1,0:T(8,128)S(1)}, u32[]{:S(2)}, u32[]{:S(2)}) collective-permute-start(f32[104,256]{1,0:T(8,128)} %reduce_sum.37), channel_id=1, source_target_pairs={{0,4},{4,0},{1,5},{5,1},{2,6},{6,2},{3,7},{7,3},{8,12},{12,8},{9,1... | collective-permute-start | bytes 319496 | tf_op jit(solution)/shard_map/ppermute | solution.py:14
  124.0 6.1 %collective-permute-done.2 = f32[104,256]{1,0:T(8,128)S(1)} collective-permute-done((f32[104,256]{1,0:T(8,128)}, f32[104,256]{1,0:T(8,128)S(1)}, u32[]{:S(2)}, u32[]{:S(2)}) %collective-permute-start.2) | collective-permute-done | bytes 106528 | tf_op jit(solution)/shard_map/ppermute | solution.py:14
  130.0 1.0 add_multiply_fusion
  131.3 8.1 %all_to_all.34 = f32[4,8,8]{2,1,0:T(8,128)S(1)} all-to-all(f32[4,8,8]{2,1,0:T(8,128)S(1)} %broadcast_in_dim.5), channel_id=1, replica_groups=mesh['z'=8,'y'=4,'c'=2,'h'=2,'x'=4] {'x'}, dimensions={0} | all-to-all | bytes 2048 | tf_op jit(solution)/shard_map/all_to_all | solution.py:75
  (23 shorter events, 1.8 us)
Async XLA Ops:
  0.0 88.9 %copy-start = (bf16[416,3584]{1,0:T(8,128)(2,1)S(1)}, bf16[416,3584]{1,0:T(8,128)(2,1)}, u32[]{:S(2)}) copy-start(bf16[416,3584]{1,0:T(8,128)(2,1)} %param.6) | copy-start | bytes 8945668
  0.0 1.4 copy-start.1
  2.6 14.4 %copy-start.2 = (s32[2]{0:T(128)S(1)}, s32[2]{0:T(128)}, u32[]{:S(2)}) copy-start(s32[2]{0:T(128)} %param.11) | copy-start | bytes 28
  2.6 45.3 %all-to-all-start = ((bf16[64,72,128]{2,1,0:T(8,128)(2,1)}), bf16[64,72,128]{2,1,0:T(8,128)(2,1)}, u32[]{:S(2)}, u32[]{:S(2)}) async-start(bf16[64,72,128]{2,1,0:T(8,128)(2,1)} %bitcast.26), calls=%async_computation | async-start | bytes 2359296 | tf_op jit(solution)/shard_map/all_to_all | solution.py:46
  85.6 5.1 %collective-permute-start = (bf16[2304,256]{1,0:T(8,128)(2,1)}, bf16[2304,256]{1,0:T(8,128)(2,1)}, u32[]{:S(2)}, u32[]{:S(2)}) collective-permute-start(bf16[2304,256]{1,0:T(8,128)(2,1)} %bitcast.12), channel_id=1, source_target_pairs={{0,8},{8,0},{1,9},{9,1},{2,10},{10,2},{3,11},{11,3},{4,12},{12,4},... | collective-permute-start | bytes 3538952 | tf_op jit(solution)/shard_map/ppermute | solution.py:14
  93.2 13.6 %all-to-all-start.2 = ((f32[4,104,256]{2,1,0:T(8,128)}), f32[4,104,256]{2,1,0:T(8,128)}, u32[]{:S(2)}, u32[]{:S(2)}) async-start(f32[4,104,256]{2,1,0:T(8,128)} %bitcast.28), calls=%async_computation.2 | async-start | bytes 851968 | tf_op jit(solution)/shard_map/all_to_all | solution.py:33
  98.9 11.4 %copy-start.3 = (s32[1,8]{1,0:T(1,128)S(1)}, s32[1,8]{1,0:T(1,128)}, u32[]{:S(2)}) copy-start(s32[1,8]{1,0:T(1,128)} %param.10) | copy-start | bytes 100
  106.8 11.8 %all-to-all-start.3 = ((f32[4,104,256]{2,1,0:T(8,128)}), f32[4,104,256]{2,1,0:T(8,128)S(1)}, u32[]{:S(2)}, u32[]{:S(2)}) async-start(f32[4,104,256]{2,1,0:T(8,128)} %bitcast.27), calls=%async_computation.3 | async-start | bytes 851968 | tf_op jit(solution)/shard_map/all_to_all | solution.py:33
  111.5 12.4 %collective-permute-start.1 = (f32[104,256]{1,0:T(8,128)S(1)}, f32[104,256]{1,0:T(8,128)}, u32[]{:S(2)}, u32[]{:S(2)}) collective-permute-start(f32[104,256]{1,0:T(8,128)S(1)} %reduce_sum.36), channel_id=1, source_target_pairs={{0,4},{4,0},{1,5},{5,1},{2,6},{6,2},{3,7},{7,3},{8,12},{12,8},{9,1... | collective-permute-start | bytes 319496 | tf_op jit(solution)/shard_map/ppermute | solution.py:14
  119.2 10.8 %collective-permute-start.2 = (f32[104,256]{1,0:T(8,128)}, f32[104,256]{1,0:T(8,128)S(1)}, u32[]{:S(2)}, u32[]{:S(2)}) collective-permute-start(f32[104,256]{1,0:T(8,128)} %reduce_sum.37), channel_id=1, source_target_pairs={{0,4},{4,0},{1,5},{5,1},{2,6},{6,2},{3,7},{7,3},{8,12},{12,8},{9,1... | collective-permute-start | bytes 319496 | tf_op jit(solution)/shard_map/ppermute | solution.py:14

commit v7 on v6

--- a/solution.py
+++ b/solution.py
@@ -14,13 +14,34 @@
     return lax.ppermute(block, axis, [(0, 1), (1, 0)])
 
 
-def pick(got, owners):
-    picked = []
-    for batch in range(2):
-        owner = owners[batch]
-        source = (owner % C) * (Z * Y) + owner // C
-        picked.append(lax.dynamic_index_in_dim(got, source, 0, keepdims=False))
+def pick(got, sources):
+    picked = [lax.dynamic_index_in_dim(got, source, 0, keepdims=False) for source in sources]
     return jnp.concatenate(picked, axis=1)
+
+
+def scatter_cores(right, left, owners):
+    rows_r, rows_l = right.shape[0] // C, left.shape[0] // C
+    own = jnp.concatenate([right[:rows_r], left[:rows_l], right[rows_r:], left[rows_l:]], axis=0)
+    own = own.reshape(Z * Y * C, -1, COLS)
+    got = lax.all_to_all(own, ("c", "z", "y"), 0, 0, tiled=True)
+    return pick(got, [(owner % C) * (Z * Y) + owner // C for owner in owners])
+
+
+def scatter_chips(right, left, owners):
+    core, chip = lax.axis_index("c"), lax.axis_index(("z", "y"))
+    rows_r, rows_l = right.shape[0] // C, left.shape[0] // C
+
+    def half(side):
+        return (
+            lax.dynamic_slice_in_dim(right, side * rows_r, rows_r, 0),
+            lax.dynamic_slice_in_dim(left, side * rows_l, rows_l, 0),
+        )
+
+    far = swap(jnp.concatenate(half(1 - core), axis=0), "c")
+    wanted = jnp.where(chip == owners[0] // C, owners[0] % C, owners[1] % C)
+    mine = jnp.where(wanted == core, jnp.concatenate(half(core), axis=0), far)
+    got = lax.all_to_all(mine.reshape(Z * Y, -1, COLS), ("z", "y"), 0, 0, tiled=True)
+    return pick(got, [owner // C for owner in owners])
 
 
 def dot(acts, part, side):
@@ -40,10 +61,10 @@
     share = tok_rows // X
 
     right, left = right_factors[0], left_factors[0]
-    rows_r, rows_l = right.shape[0] // C, left.shape[0] // C
-    own = jnp.concatenate([right[:rows_r], left[:rows_l], right[rows_r:], left[rows_l:]], axis=0)
-    own = own.reshape(Z * Y * C, -1, COLS)
-    picked = pick(lax.all_to_all(own, ("c", "z", "y"), 0, 0, tiled=True), owners)
+    rows_r = right.shape[0] // C
+    owner = owners[0], owners[1]
+    two_cores = (owner[0] // C == owner[1] // C) & (owner[0] != owner[1])
+    picked = lax.cond(two_cores, scatter_cores, scatter_chips, right, left, owner)
 
     copies = jnp.broadcast_to(picked[None], (Z * Y, *picked.shape))
     mine = lax.all_to_all(copies, ("z", "y"), 0, 0, tiled=True).reshape(-1, 2 * COLS)
@@ -55,10 +76,9 @@
     proj_g = near_g + dot(out_grads, other[:rows_r], 1 - core)
     proj_h = near_h + dot(hidden_acts, other[rows_r:], 1 - core)
 
-    part_g = sum_x(proj_g)
-    part_h = sum_x(proj_h)
-    full_g = part_g + swap(part_g, "h")
-    full_h = part_h + swap(part_h, "h")
+    part = sum_x(jnp.concatenate([proj_g, proj_h], axis=1))
+    full = part + swap(part, "h")
+    full_g, full_h = full[:, : 2 * COLS], full[:, 2 * COLS :]
     token_score = (full_h * full_g).reshape(share, 2 * QB, RANK).sum(axis=2)
 
     counts = doc_tokens[0]

time: 142 us -> 145 us (1.021)
  starting transfers between devices: 33.5 us -> 26.8 us
  loops' own time: 0 us -> 5.23 us
  waiting for transfers between devices: 40.9 us -> 43.4 us
  between operations: 5.07 us -> 6.55 us
    all_to_all x1, waiting for transfers between devices: 25.4 us -> 18.2 us  [scatter_chips(): lax.all_to_all(mine.reshape(Z * Y, -1, COLS), ('z', 'y'), 0, 0, tiled=True)]
    ppermute x3, waiting for transfers between devices: 6.11 us -> 11.5 us  [swap(): return lax.ppermute(block, axis, [(0, 1), (1, 0)])]
    another operation x0 -> x1, loops' own time: none -> 5.23 us  [shards(): lax.cond(two_cores, scatter_cores, scatter_chips, right, left, owner)]
    all_to_all x2 -> x1, waiting for transfers between devices: 9.43 us -> 13.7 us  [sum_x(): parts = lax.all_to_all(proj, 'x', 0, 0, tiled=True)]
    all_to_all x2 -> x1, starting transfers between devices: 7.75 us -> 4.43 us  [sum_x(): parts = lax.all_to_all(proj, 'x', 0, 0, tiled=True)]
    ppermute x3, starting transfers between devices: 11.3 us -> 8.54 us  [swap(): return lax.ppermute(block, axis, [(0, 1), (1, 0)])]
    dynamic_slice x0 -> x2, local copies, waits for them, and re-layouts: none -> 1.95 us  [the longest x1 1.26 us: half(): lax.dynamic_slice_in_dim(left, side * rows_l, rows_l, 0)]
    select_n x0 -> x1, other arithmetic: none -> 1.88 us  [scatter_chips(): mine = jnp.where(wanted == core, jnp.concatenate(half(core), axis=0), far)]
  transfers between devices with their start and end apart: 6 -> 5, of which waited for: 4 -> 3; matrix products, arithmetic and copies ran while one was open for 6% -> 2% of each run, Pallas kernels for 0% -> 0%
where the time goes in v7:
time: 145 us; the launch traced here: 142 us
  blocking collectives  43.6 us (30%)
  waiting for transfers between devices  43.4 us (30%)
  starting transfers between devices  26.8 us (18%)
  between operations  6.55 us (5%)
  matrix products  6.32 us (4%)
  other arithmetic  6.02 us (4%)
  loops' own time  5.23 us (4%)
  local copies, waits for them, and re-layouts  4.28 us (3%)
    all_to_all x1, blocking collectives, shards(): lax.all_to_all(copies, ('z', 'y'), 0, 0, tiled=True).reshape(-1, 2 * COLS)  35.8 us
    all_to_all x1, waiting for transfers between devices, scatter_chips(): lax.all_to_all(mine.reshape(Z * Y, -1, COLS), ('z', 'y'), 0, 0, tiled=True)  18.2 us
    all_to_all x1, starting transfers between devices, scatter_chips(): lax.all_to_all(mine.reshape(Z * Y, -1, COLS), ('z', 'y'), 0, 0, tiled=True)  13.8 us
    all_to_all x1, waiting for transfers between devices, sum_x(): parts = lax.all_to_all(proj, 'x', 0, 0, tiled=True)  13.7 us
    ppermute x3, waiting for transfers between devices, swap(): return lax.ppermute(block, axis, [(0, 1), (1, 0)])  11.5 us
    ppermute x3, starting transfers between devices, swap(): return lax.ppermute(block, axis, [(0, 1), (1, 0)])  8.54 us
    all_to_all x1, blocking collectives, shards(): summed = lax.all_to_all(copies, 'x', 0, 0, tiled=True).sum(axis=0)  7.71 us
    dot_general x4, matrix products, dot(): return jnp.dot(acts, part, preferred_element_type=jnp.float32)  6.13 us
  transfers between devices with their start and end apart: 5, of which 3 were waited for; matrix products, arithmetic and copies ran while one was open for 2% of the time, Pallas kernels for 0%

profile of v7, /device:TPU:56, one launch (start us, length us, event | category | flops | bytes accessed | tf_op | source)
XLA Modules:
  0.0 142.2 jit_solution(1994386770285211958)
XLA Ops:
  0.0 1.4 fusion.25
  7.8 44.6 %conditional.1 = (bf16[72,256]{1,0:T(8,128)(2,1)S(1)}) conditional(s32[]{:T(128)} %convert_element_type.4, (s32[]{:T(128)}, s32[]{:T(128)}, bf16[1024,128]{1,0:T(8,128)(2,1)}, bf16[3584,128]{1,0:T(8,128)(2,1)}) %tuple.26, (bf16[1024,128]{1,0:T(8,128)(2,1)}, bf16[3584,128]{1,0:T(8,128)(2,1)}, s32[]{:T(128)}, s32[]{:T(128)}) %tuple.27), branch_computations={%region_1.2_spmd, %region_2.3_spmd} | conditional | flops 4792368 | bytes 10634138 | solution.py:67
  7.8 1.3 constant_dynamic-slice_fusion.2
  9.1 0.7 constant_dynamic-slice_fusion.3
  9.8 0.9 pad_maximum_fusion
  10.6 1.9 %collective-permute-start = (bf16[2304,128]{1,0:T(8,128)(2,1)}, bf16[2304,128]{1,0:T(8,128)(2,1)}, u32[]{:S(2)}, u32[]{:S(2)}) collective-permute-start(bf16[2304,128]{1,0:T(8,128)(2,1)} %pad_maximum_fusion), channel_id=1, source_target_pairs={{0,8},{8,0},{1,9},{9,1},{2,10},{10,2},{3,11},{11,3},{4,12},{12,4},... | collective-permute-start | bytes 1769480 | tf_op jit(solution)/shard_map/cond/branch_0_fun/ppermute | solution.py:14
  17.0 1.9 %maximum_select_fusion = bf16[2304,128]{1,0:T(8,128)(2,1)} fusion(bf16[2304,128]{1,0:T(8,128)(2,1)} %collective-permute-done, bf16[1792,128]{1,0:T(8,128)(2,1)S(1)} %get-tuple-element.38, bf16[512,128]{1,0:T(8,128)(2,1)} %get-tuple-element.42, pred[]{:T(512)S(6)} %eq.12), kind=kLoop, calls=%fused_computation | loop fusion | flops 1474560 | bytes 1769473 | tf_op jit(solution)/shard_map/cond/branch_0_fun/jit(_where)/select_n | solution.py:42
  18.9 13.8 %all-to-all-start = ((bf16[32,72,128]{2,1,0:T(8,128)(2,1)}), bf16[32,72,128]{2,1,0:T(8,128)(2,1)}, u32[]{:S(2)}, u32[]{:S(2)}) async-start(bf16[32,72,128]{2,1,0:T(8,128)(2,1)} %bitcast.28), calls=%async_computation | async-start | bytes 1179648 | tf_op jit(solution)/shard_map/cond/branch_0_fun/all_to_all | solution.py:43
  33.4 18.2 %all-to-all-done = bf16[32,72,128]{2,1,0:T(8,128)(2,1)} async-done(((bf16[32,72,128]{2,1,0:T(8,128)(2,1)}), bf16[32,72,128]{2,1,0:T(8,128)(2,1)}, u32[]{:S(2)}, u32[]{:S(2)}) %all-to-all-start) | async-done | bytes 589856 | tf_op jit(solution)/shard_map/cond/branch_0_fun/all_to_all | solution.py:43
  51.7 0.7 dynamic-slice_bitcast_fusion.1
  52.5 35.8 %all_to_all.27 = bf16[32,72,256]{2,1,0:T(8,128)(2,1)} all-to-all(bf16[32,72,256]{2,1,0:T(8,128)(2,1)S(1)} %broadcast_in_dim.4), channel_id=1, replica_groups=mesh['z'=8,'y'=4,'c'=2,'h'=2,'x'=4] {'z','y'}, dimensions={0} | all-to-all | bytes 2359296 | tf_op jit(solution)/shard_map/all_to_all | solution.py:70
  88.4 1.9 %collective-permute-start.1 = (bf16[2304,256]{1,0:T(8,128)(2,1)}, bf16[2304,256]{1,0:T(8,128)(2,1)}, u32[]{:S(2)}, u32[]{:S(2)}) collective-permute-start(bf16[2304,256]{1,0:T(8,128)(2,1)} %bitcast.13), channel_id=1, source_target_pairs={{0,8},{8,0},{1,9},{9,1},{2,10},{10,2},{3,11},{11,3},{4,12},{12,4},... | collective-permute-start | bytes 3538952 | tf_op jit(solution)/shard_map/ppermute | solution.py:14
  90.3 1.4 fusion.8
  91.7 1.8 %fusion.2 = f32[416,256]{1,0:T(8,128)S(1)} fusion(bf16[416,3584]{1,0:T(8,128)(2,1)S(1)} %copy-done, s32[]{:T(128)S(6)} %select_n.91, bf16[2304,256]{1,0:T(8,128)(2,1)} %bitcast.13), kind=kOutput, calls=%fused_computation.15 | convolution fusion | flops 381681664 | bytes 2834436 | tf_op jit(solution)/shard_map/dot_general | solution.py:50
  93.5 1.2 fusion.6
  94.7 1.7 %fusion = f32[416,256]{1,0:T(8,128)S(1)} fusion(bf16[416,3584]{1,0:T(8,128)(2,1)S(1)} %copy-done, s32[]{:T(128)S(6)} %select_n.93, bf16[2304,256]{1,0:T(8,128)(2,1)} %collective-permute-done.1), kind=kOutput, calls=%fused_computation.13 | convolution fusion | flops 381681664 | bytes 2834436 | tf_op jit(solution)/shard_map/dot_general | solution.py:50
  96.6 1.1 pad_maximum_fusion.4
  97.7 4.4 %all-to-all-start.3 = ((f32[4,104,512]{2,1,0:T(8,128)}), f32[4,104,512]{2,1,0:T(8,128)}, u32[]{:S(2)}, u32[]{:S(2)}) async-start(f32[4,104,512]{2,1,0:T(8,128)} %bitcast.27), calls=%async_computation.3 | async-start | bytes 1703936 | tf_op jit(solution)/shard_map/all_to_all | solution.py:54
  102.3 13.7 %all-to-all-done.3 = f32[4,104,512]{2,1,0:T(8,128)} async-done(((f32[4,104,512]{2,1,0:T(8,128)}), f32[4,104,512]{2,1,0:T(8,128)}, u32[]{:S(2)}, u32[]{:S(2)}) %all-to-all-start.3) | async-done | bytes 852000 | tf_op jit(solution)/shard_map/all_to_all | solution.py:54
  116.0 1.2 reduce_sum.27
  117.3 4.7 %collective-permute-start.2 = (f32[104,512]{1,0:T(8,128)S(1)}, f32[104,512]{1,0:T(8,128)S(1)}, u32[]{:S(2)}, u32[]{:S(2)}) collective-permute-start(f32[104,512]{1,0:T(8,128)S(1)} %reduce_sum.27), channel_id=1, source_target_pairs={{0,4},{4,0},{1,5},{5,1},{2,6},{6,2},{3,7},{7,3},{8,12},{12,8},{9,1... | collective-permute-start | bytes 638984 | tf_op jit(solution)/shard_map/ppermute | solution.py:14
  122.0 11.5 %collective-permute-done.2 = f32[104,512]{1,0:T(8,128)S(1)} collective-permute-done((f32[104,512]{1,0:T(8,128)S(1)}, f32[104,512]{1,0:T(8,128)S(1)}, u32[]{:S(2)}, u32[]{:S(2)}) %collective-permute-start.2) | collective-permute-done | bytes 213024 | tf_op jit(solution)/shard_map/ppermute | solution.py:14
  133.9 7.7 %all_to_all.28 = f32[4,8,8]{2,1,0:T(8,128)S(1)} all-to-all(f32[4,8,8]{2,1,0:T(8,128)S(1)} %broadcast_in_dim.5), channel_id=1, replica_groups=mesh['z'=8,'y'=4,'c'=2,'h'=2,'x'=4] {'x'}, dimensions={0} | all-to-all | bytes 2048 | tf_op jit(solution)/shard_map/all_to_all | solution.py:95
  141.6 0.6 broadcast_multiply_fusion
  (24 shorter events, 0.8 us)
Async XLA Ops:
  0.0 91.6 %copy-start = (bf16[416,3584]{1,0:T(8,128)(2,1)S(1)}, bf16[416,3584]{1,0:T(8,128)(2,1)}, u32[]{:S(2)}) copy-start(bf16[416,3584]{1,0:T(8,128)(2,1)} %param.8) | copy-start | bytes 8945668
  7.8 1.3 copy-start.1
  10.6 6.4 %collective-permute-start = (bf16[2304,128]{1,0:T(8,128)(2,1)}, bf16[2304,128]{1,0:T(8,128)(2,1)}, u32[]{:S(2)}, u32[]{:S(2)}) collective-permute-start(bf16[2304,128]{1,0:T(8,128)(2,1)} %pad_maximum_fusion), channel_id=1, source_target_pairs={{0,8},{8,0},{1,9},{9,1},{2,10},{10,2},{3,11},{11,3},{4,12},{12,4},... | collective-permute-start | bytes 1769480 | tf_op jit(solution)/shard_map/cond/branch_0_fun/ppermute | solution.py:14
  18.9 32.7 %all-to-all-start = ((bf16[32,72,128]{2,1,0:T(8,128)(2,1)}), bf16[32,72,128]{2,1,0:T(8,128)(2,1)}, u32[]{:S(2)}, u32[]{:S(2)}) async-start(bf16[32,72,128]{2,1,0:T(8,128)(2,1)} %bitcast.28), calls=%async_computation | async-start | bytes 1179648 | tf_op jit(solution)/shard_map/cond/branch_0_fun/all_to_all | solution.py:43
  88.4 5.1 %collective-permute-start.1 = (bf16[2304,256]{1,0:T(8,128)(2,1)}, bf16[2304,256]{1,0:T(8,128)(2,1)}, u32[]{:S(2)}, u32[]{:S(2)}) collective-permute-start(bf16[2304,256]{1,0:T(8,128)(2,1)} %bitcast.13), channel_id=1, source_target_pairs={{0,8},{8,0},{1,9},{9,1},{2,10},{10,2},{3,11},{11,3},{4,12},{12,4},... | collective-permute-start | bytes 3538952 | tf_op jit(solution)/shard_map/ppermute | solution.py:14
  91.6 1.8 %copy-start.3 = (bf16[416,1024]{1,0:T(8,128)(2,1)S(1)}, bf16[416,1024]{1,0:T(8,128)(2,1)}, u32[]{:S(2)}) copy-start(bf16[416,1024]{1,0:T(8,128)(2,1)} %param.9) | copy-start | bytes 2555908
  97.7 4.4 %copy-start.4 = (s32[1,8]{1,0:T(1,128)S(1)}, s32[1,8]{1,0:T(1,128)}, u32[]{:S(2)}) copy-start(s32[1,8]{1,0:T(1,128)} %param.12) | copy-start | bytes 100
  97.7 18.3 %all-to-all-start.3 = ((f32[4,104,512]{2,1,0:T(8,128)}), f32[4,104,512]{2,1,0:T(8,128)}, u32[]{:S(2)}, u32[]{:S(2)}) async-start(f32[4,104,512]{2,1,0:T(8,128)} %bitcast.27), calls=%async_computation.3 | async-start | bytes 1703936 | tf_op jit(solution)/shard_map/all_to_all | solution.py:54
  117.3 16.2 %collective-permute-start.2 = (f32[104,512]{1,0:T(8,128)S(1)}, f32[104,512]{1,0:T(8,128)S(1)}, u32[]{:S(2)}, u32[]{:S(2)}) collective-permute-start(f32[104,512]{1,0:T(8,128)S(1)} %reduce_sum.27), channel_id=1, source_target_pairs={{0,4},{4,0},{1,5},{5,1},{2,6},{6,2},{3,7},{7,3},{8,12},{12,8},{9,1... | collective-permute-start | bytes 638984 | tf_op jit(solution)/shard_map/ppermute | solution.py:14

commit v8 on v7

--- a/solution.py
+++ b/solution.py
@@ -14,9 +14,12 @@
     return lax.ppermute(block, axis, [(0, 1), (1, 0)])
 
 
+def cut(block, start, size, axis):
+    return lax.dynamic_slice_in_dim(block, start, size, axis, allow_negative_indices=False)
+
+
 def pick(got, sources):
-    picked = [lax.dynamic_index_in_dim(got, source, 0, keepdims=False) for source in sources]
-    return jnp.concatenate(picked, axis=1)
+    return jnp.concatenate([cut(got, source, 1, 0)[0] for source in sources], axis=1)
 
 
 def scatter_cores(right, left, owners):
@@ -24,7 +27,7 @@
     own = jnp.concatenate([right[:rows_r], left[:rows_l], right[rows_r:], left[rows_l:]], axis=0)
     own = own.reshape(Z * Y * C, -1, COLS)
     got = lax.all_to_all(own, ("c", "z", "y"), 0, 0, tiled=True)
-    return pick(got, [(owner % C) * (Z * Y) + owner // C for owner in owners])
+    return pick(got, [(owner & 1) * (Z * Y) + (owner >> 1) for owner in owners])
 
 
 def scatter_chips(right, left, owners):
@@ -33,20 +36,20 @@
 
     def half(side):
         return (
-            lax.dynamic_slice_in_dim(right, side * rows_r, rows_r, 0),
-            lax.dynamic_slice_in_dim(left, side * rows_l, rows_l, 0),
+            cut(right, side * rows_r, rows_r, 0),
+            cut(left, side * rows_l, rows_l, 0),
         )
 
     far = swap(jnp.concatenate(half(1 - core), axis=0), "c")
-    wanted = jnp.where(chip == owners[0] // C, owners[0] % C, owners[1] % C)
+    wanted = jnp.where(chip == owners[0] >> 1, owners[0], owners[1]) & 1
     mine = jnp.where(wanted == core, jnp.concatenate(half(core), axis=0), far)
     got = lax.all_to_all(mine.reshape(Z * Y, -1, COLS), ("z", "y"), 0, 0, tiled=True)
-    return pick(got, [owner // C for owner in owners])
+    return pick(got, [owner >> 1 for owner in owners])
 
 
 def dot(acts, part, side):
     rows = part.shape[0]
-    acts = lax.dynamic_slice_in_dim(acts, side * rows, rows, 1)
+    acts = cut(acts, side * rows, rows, 1)
     return jnp.dot(acts, part, preferred_element_type=jnp.float32)
 
 
@@ -63,8 +66,7 @@
     right, left = right_factors[0], left_factors[0]
     rows_r = right.shape[0] // C
     owner = owners[0], owners[1]
-    two_cores = (owner[0] // C == owner[1] // C) & (owner[0] != owner[1])
-    picked = lax.cond(two_cores, scatter_cores, scatter_chips, right, left, owner)
+    picked = lax.cond(owner[0] ^ owner[1] == 1, scatter_cores, scatter_chips, right, left, owner)
 
     copies = jnp.broadcast_to(picked[None], (Z * Y, *picked.shape))
     mine = lax.all_to_all(copies, ("z", "y"), 0, 0, tiled=True).reshape(-1, 2 * COLS)
@@ -76,9 +78,10 @@
     proj_g = near_g + dot(out_grads, other[:rows_r], 1 - core)
     proj_h = near_h + dot(hidden_acts, other[rows_r:], 1 - core)
 
-    part = sum_x(jnp.concatenate([proj_g, proj_h], axis=1))
-    full = part + swap(part, "h")
-    full_g, full_h = full[:, : 2 * COLS], full[:, 2 * COLS :]
+    part_g = sum_x(proj_g)
+    part_h = sum_x(proj_h)
+    full_g = part_g + swap(part_g, "h")
+    full_h = part_h + swap(part_h, "h")
     token_score = (full_h * full_g).reshape(share, 2 * QB, RANK).sum(axis=2)
 
     counts = doc_tokens[0]

time: 145 us -> 137 us (0.945)
  waiting for transfers between devices: 43.4 us -> 33.5 us
  starting transfers between devices: 26.8 us -> 34.8 us
  between operations: 6.55 us -> 1.43 us
  loops' own time: 5.23 us -> 2.59 us
  other arithmetic: 6.02 us -> 8.04 us
    ppermute x3 -> x4, waiting for transfers between devices: 11.5 us -> 6.55 us  [swap(): return lax.ppermute(block, axis, [(0, 1), (1, 0)])]
    ppermute x3 -> x4, starting transfers between devices: 8.54 us -> 13.2 us  [swap(): return lax.ppermute(block, axis, [(0, 1), (1, 0)])]
    all_to_all x1 -> x2, waiting for transfers between devices: 13.7 us -> 9.41 us  [sum_x(): parts = lax.all_to_all(proj, 'x', 0, 0, tiled=True)]
    all_to_all x1 -> x2, starting transfers between devices: 4.43 us -> 7.75 us  [sum_x(): parts = lax.all_to_all(proj, 'x', 0, 0, tiled=True)]
    another operation x1, loops' own time: 5.23 us -> 2.59 us  [shards(): lax.cond(owner[0] ^ owner[1] == 1, scatter_cores, scatter_chips, right, l...]
  transfers between devices with their start and end apart: 5 -> 7, of which waited for: 3 -> 5; matrix products, arithmetic and copies ran while one was open for 2% -> 5% of each run, Pallas kernels for 0% -> 0%
where the time goes in v8:
time: 137 us; the launch traced here: 135 us
  blocking collectives  43.9 us (32%)
  starting transfers between devices  34.8 us (25%)
  waiting for transfers between devices  33.5 us (24%)
  other arithmetic  8.04 us (6%)
  matrix products  6.35 us (5%)
  local copies, waits for them, and re-layouts  4.34 us (3%)
  loops' own time  2.59 us (2%)
  between operations  1.43 us (1%)
    all_to_all x1, blocking collectives, shards(): lax.all_to_all(copies, ('z', 'y'), 0, 0, tiled=True).reshape(-1, 2 * COLS)  35.8 us
    all_to_all x1, waiting for transfers between devices, scatter_chips(): lax.all_to_all(mine.reshape(Z * Y, -1, COLS), ('z', 'y'), 0, 0, tiled=True)  17.6 us
    all_to_all x1, starting transfers between devices, scatter_chips(): lax.all_to_all(mine.reshape(Z * Y, -1, COLS), ('z', 'y'), 0, 0, tiled=True)  13.8 us
    ppermute x4, starting transfers between devices, swap(): return lax.ppermute(block, axis, [(0, 1), (1, 0)])  13.2 us
    all_to_all x2, waiting for transfers between devices, sum_x(): parts = lax.all_to_all(proj, 'x', 0, 0, tiled=True)  9.41 us
    all_to_all x1, blocking collectives, shards(): summed = lax.all_to_all(copies, 'x', 0, 0, tiled=True).sum(axis=0)  8.09 us
    all_to_all x2, starting transfers between devices, sum_x(): parts = lax.all_to_all(proj, 'x', 0, 0, tiled=True)  7.75 us
    ppermute x4, waiting for transfers between devices, swap(): return lax.ppermute(block, axis, [(0, 1), (1, 0)])  6.55 us
  transfers between devices with their start and end apart: 7, of which 5 were waited for; matrix products, arithmetic and copies ran while one was open for 5% of the time, Pallas kernels for 0%

profile of v8, /device:TPU:56, one launch (start us, length us, event | category | flops | bytes accessed | tf_op | source)
XLA Modules:
  0.0 135.0 jit_solution(14861034134260365623)
XLA Ops:
  0.0 1.4 %fusion.25 = (s32[1]{0:T(128)}, s32[1]{0:T(128)}) fusion(s32[2]{0:T(128)} %param.13), kind=kLoop, calls=%fused_computation.43 | loop fusion | bytes 16 | tf_op jit(solution)/shard_map/slice | solution.py:68
  2.7 42.0 %conditional.1 = (bf16[72,256]{1,0:T(8,128)(2,1)S(1)}) conditional(s32[]{:T(128)} %convert_element_type.4, (s32[]{:T(128)}, s32[]{:T(128)}, bf16[1024,128]{1,0:T(8,128)(2,1)}, bf16[3584,128]{1,0:T(8,128)(2,1)}) %tuple.26, (bf16[1024,128]{1,0:T(8,128)(2,1)}, bf16[3584,128]{1,0:T(8,128)(2,1)}, s32[]{:T(128)}, s32[]{:T(128)}) %tuple.27), branch_computations={%region_1.2_spmd, %region_2.3_spmd} | conditional | flops 4792328 | bytes 10633596 | solution.py:69
  2.7 1.3 constant_dynamic-slice_fusion.2
  4.7 0.9 pad_maximum_fusion
  5.5 1.9 %collective-permute-start = (bf16[2304,128]{1,0:T(8,128)(2,1)}, bf16[2304,128]{1,0:T(8,128)(2,1)}, u32[]{:S(2)}, u32[]{:S(2)}) collective-permute-start(bf16[2304,128]{1,0:T(8,128)(2,1)} %pad_maximum_fusion), channel_id=1, source_target_pairs={{0,8},{8,0},{1,9},{9,1},{2,10},{10,2},{3,11},{11,3},{4,12},{12,4},... | collective-permute-start | bytes 1769480 | tf_op jit(solution)/shard_map/cond/branch_0_fun/ppermute | solution.py:14
  9.8 2.1 %maximum_select_fusion = bf16[2304,128]{1,0:T(8,128)(2,1)} fusion(bf16[2304,128]{1,0:T(8,128)(2,1)} %collective-permute-done, bf16[1792,128]{1,0:T(8,128)(2,1)S(1)} %get-tuple-element.38, bf16[512,128]{1,0:T(8,128)(2,1)} %get-tuple-element.42, pred[]{:T(512)S(6)} %eq.7), kind=kLoop, calls=%fused_computation | loop fusion | flops 1474560 | bytes 1769473 | tf_op jit(solution)/shard_map/cond/branch_0_fun/jit(_where)/select_n | solution.py:45
  11.8 13.8 %all-to-all-start = ((bf16[32,72,128]{2,1,0:T(8,128)(2,1)}), bf16[32,72,128]{2,1,0:T(8,128)(2,1)}, u32[]{:S(2)}, u32[]{:S(2)}) async-start(bf16[32,72,128]{2,1,0:T(8,128)(2,1)} %bitcast.28), calls=%async_computation | async-start | bytes 1179648 | tf_op jit(solution)/shard_map/cond/branch_0_fun/all_to_all | solution.py:46
  26.2 17.6 %all-to-all-done = bf16[32,72,128]{2,1,0:T(8,128)(2,1)} async-done(((bf16[32,72,128]{2,1,0:T(8,128)(2,1)}), bf16[32,72,128]{2,1,0:T(8,128)(2,1)}, u32[]{:S(2)}, u32[]{:S(2)}) %all-to-all-start) | async-done | bytes 589856 | tf_op jit(solution)/shard_map/cond/branch_0_fun/all_to_all | solution.py:46
  44.7 35.8 %all_to_all.36 = bf16[32,72,256]{2,1,0:T(8,128)(2,1)} all-to-all(bf16[32,72,256]{2,1,0:T(8,128)(2,1)S(1)} %broadcast_in_dim.4), channel_id=1, replica_groups=mesh['z'=8,'y'=4,'c'=2,'h'=2,'x'=4] {'z','y'}, dimensions={0} | all-to-all | bytes 2359296 | tf_op jit(solution)/shard_map/all_to_all | solution.py:72
  80.6 1.9 %collective-permute-start.1 = (bf16[2304,256]{1,0:T(8,128)(2,1)}, bf16[2304,256]{1,0:T(8,128)(2,1)}, u32[]{:S(2)}, u32[]{:S(2)}) collective-permute-start(bf16[2304,256]{1,0:T(8,128)(2,1)} %bitcast.13), channel_id=1, source_target_pairs={{0,8},{8,0},{1,9},{9,1},{2,10},{10,2},{3,11},{11,3},{4,12},{12,4},... | collective-permute-start | bytes 3538952 | tf_op jit(solution)/shard_map/ppermute | solution.py:14
  82.5 1.4 %fusion.8 = f32[416,256]{1,0:T(8,128)S(1)} fusion(bf16[416,1024]{1,0:T(8,128)(2,1)} %param.9, s32[]{:T(128)S(6)} %mul.40, bf16[2304,256]{1,0:T(8,128)(2,1)} %bitcast.13), kind=kOutput, calls=%fused_computation.21 | convolution fusion | flops 109051904 | bytes 1114116 | tf_op jit(solution)/shard_map/dot_general | solution.py:53
  83.9 1.7 %fusion.2 = f32[416,256]{1,0:T(8,128)S(1)} fusion(bf16[416,3584]{1,0:T(8,128)(2,1)S(1)} %copy-done, s32[]{:T(128)S(6)} %mul.41, bf16[2304,256]{1,0:T(8,128)(2,1)} %bitcast.13), kind=kOutput, calls=%fused_computation.15 | convolution fusion | flops 381681664 | bytes 2834436 | tf_op jit(solution)/shard_map/dot_general | solution.py:53
  85.6 1.7 %fusion = f32[416,256]{1,0:T(8,128)S(1)} fusion(bf16[416,3584]{1,0:T(8,128)(2,1)S(1)} %copy-done, s32[]{:T(128)S(6)} %mul.42, bf16[2304,256]{1,0:T(8,128)(2,1)} %collective-permute-done.1), kind=kOutput, calls=%fused_computation.13 | convolution fusion | flops 381681664 | bytes 2834436 | tf_op jit(solution)/shard_map/dot_general | solution.py:53
  88.2 4.3 %all-to-all-start.3 = ((f32[4,104,256]{2,1,0:T(8,128)}), f32[4,104,256]{2,1,0:T(8,128)}, u32[]{:S(2)}, u32[]{:S(2)}) async-start(f32[4,104,256]{2,1,0:T(8,128)} %bitcast.29), calls=%async_computation.3 | async-start | bytes 851968 | tf_op jit(solution)/shard_map/all_to_all | solution.py:57
  92.5 1.3 fusion.6
  94.6 7.1 %all-to-all-done.3 = f32[4,104,256]{2,1,0:T(8,128)} async-done(((f32[4,104,256]{2,1,0:T(8,128)}), f32[4,104,256]{2,1,0:T(8,128)}, u32[]{:S(2)}, u32[]{:S(2)}) %all-to-all-start.3) | async-done | bytes 426016 | tf_op jit(solution)/shard_map/all_to_all | solution.py:57
  101.7 3.5 %all-to-all-start.4 = ((f32[4,104,256]{2,1,0:T(8,128)}), f32[4,104,256]{2,1,0:T(8,128)S(1)}, u32[]{:S(2)}, u32[]{:S(2)}) async-start(f32[4,104,256]{2,1,0:T(8,128)} %bitcast.15), calls=%async_computation.4 | async-start | bytes 851968 | tf_op jit(solution)/shard_map/all_to_all | solution.py:57
  105.4 1.0 reduce_sum.36
  106.4 4.7 %collective-permute-start.2 = (f32[104,256]{1,0:T(8,128)S(1)}, f32[104,256]{1,0:T(8,128)}, u32[]{:S(2)}, u32[]{:S(2)}) collective-permute-start(f32[104,256]{1,0:T(8,128)S(1)} %reduce_sum.36), channel_id=1, source_target_pairs={{0,4},{4,0},{1,5},{5,1},{2,6},{6,2},{3,7},{7,3},{8,12},{12,8},{9,1... | collective-permute-start | bytes 319496 | tf_op jit(solution)/shard_map/ppermute | solution.py:14
  111.2 2.3 %all-to-all-done.4 = f32[4,104,256]{2,1,0:T(8,128)S(1)} async-done(((f32[4,104,256]{2,1,0:T(8,128)}), f32[4,104,256]{2,1,0:T(8,128)S(1)}, u32[]{:S(2)}, u32[]{:S(2)}) %all-to-all-start.4) | async-done | bytes 426016 | tf_op jit(solution)/shard_map/all_to_all | solution.py:57
  114.2 4.7 %collective-permute-start.3 = (f32[104,256]{1,0:T(8,128)}, f32[104,256]{1,0:T(8,128)S(1)}, u32[]{:S(2)}, u32[]{:S(2)}) collective-permute-start(f32[104,256]{1,0:T(8,128)} %reduce_sum.37), channel_id=1, source_target_pairs={{0,4},{4,0},{1,5},{5,1},{2,6},{6,2},{3,7},{7,3},{8,12},{12,8},{9,1... | collective-permute-start | bytes 319496 | tf_op jit(solution)/shard_map/ppermute | solution.py:14
  118.9 6.1 %collective-permute-done.3 = f32[104,256]{1,0:T(8,128)S(1)} collective-permute-done((f32[104,256]{1,0:T(8,128)}, f32[104,256]{1,0:T(8,128)S(1)}, u32[]{:S(2)}, u32[]{:S(2)}) %collective-permute-start.3) | collective-permute-done | bytes 106528 | tf_op jit(solution)/shard_map/ppermute | solution.py:14
  125.0 1.0 add_multiply_fusion
  126.3 8.1 %all_to_all.37 = f32[4,8,8]{2,1,0:T(8,128)S(1)} all-to-all(f32[4,8,8]{2,1,0:T(8,128)S(1)} %broadcast_in_dim.5), channel_id=1, replica_groups=mesh['z'=8,'y'=4,'c'=2,'h'=2,'x'=4] {'x'}, dimensions={0} | all-to-all | bytes 2048 | tf_op jit(solution)/shard_map/all_to_all | solution.py:98
  (25 shorter events, 5.4 us)
Async XLA Ops:
  0.0 83.8 %copy-start = (bf16[416,3584]{1,0:T(8,128)(2,1)S(1)}, bf16[416,3584]{1,0:T(8,128)(2,1)}, u32[]{:S(2)}) copy-start(bf16[416,3584]{1,0:T(8,128)(2,1)} %param.8) | copy-start | bytes 8945668
  2.7 1.3 copy-start.1
  5.5 4.2 %collective-permute-start = (bf16[2304,128]{1,0:T(8,128)(2,1)}, bf16[2304,128]{1,0:T(8,128)(2,1)}, u32[]{:S(2)}, u32[]{:S(2)}) collective-permute-start(bf16[2304,128]{1,0:T(8,128)(2,1)} %pad_maximum_fusion), channel_id=1, source_target_pairs={{0,8},{8,0},{1,9},{9,1},{2,10},{10,2},{3,11},{11,3},{4,12},{12,4},... | collective-permute-start | bytes 1769480 | tf_op jit(solution)/shard_map/cond/branch_0_fun/ppermute | solution.py:14
  11.8 32.0 %all-to-all-start = ((bf16[32,72,128]{2,1,0:T(8,128)(2,1)}), bf16[32,72,128]{2,1,0:T(8,128)(2,1)}, u32[]{:S(2)}, u32[]{:S(2)}) async-start(bf16[32,72,128]{2,1,0:T(8,128)(2,1)} %bitcast.28), calls=%async_computation | async-start | bytes 1179648 | tf_op jit(solution)/shard_map/cond/branch_0_fun/all_to_all | solution.py:46
  80.6 5.1 %collective-permute-start.1 = (bf16[2304,256]{1,0:T(8,128)(2,1)}, bf16[2304,256]{1,0:T(8,128)(2,1)}, u32[]{:S(2)}, u32[]{:S(2)}) collective-permute-start(bf16[2304,256]{1,0:T(8,128)(2,1)} %bitcast.13), channel_id=1, source_target_pairs={{0,8},{8,0},{1,9},{9,1},{2,10},{10,2},{3,11},{11,3},{4,12},{12,4},... | collective-permute-start | bytes 3538952 | tf_op jit(solution)/shard_map/ppermute | solution.py:14
  88.2 13.5 %all-to-all-start.3 = ((f32[4,104,256]{2,1,0:T(8,128)}), f32[4,104,256]{2,1,0:T(8,128)}, u32[]{:S(2)}, u32[]{:S(2)}) async-start(f32[4,104,256]{2,1,0:T(8,128)} %bitcast.29), calls=%async_computation.3 | async-start | bytes 851968 | tf_op jit(solution)/shard_map/all_to_all | solution.py:57
  93.8 11.4 %copy-start.3 = (s32[1,8]{1,0:T(1,128)S(1)}, s32[1,8]{1,0:T(1,128)}, u32[]{:S(2)}) copy-start(s32[1,8]{1,0:T(1,128)} %param.12) | copy-start | bytes 100
  101.7 11.8 %all-to-all-start.4 = ((f32[4,104,256]{2,1,0:T(8,128)}), f32[4,104,256]{2,1,0:T(8,128)S(1)}, u32[]{:S(2)}, u32[]{:S(2)}) async-start(f32[4,104,256]{2,1,0:T(8,128)} %bitcast.15), calls=%async_computation.4 | async-start | bytes 851968 | tf_op jit(solution)/shard_map/all_to_all | solution.py:57
  106.4 12.4 %collective-permute-start.2 = (f32[104,256]{1,0:T(8,128)S(1)}, f32[104,256]{1,0:T(8,128)}, u32[]{:S(2)}, u32[]{:S(2)}) collective-permute-start(f32[104,256]{1,0:T(8,128)S(1)} %reduce_sum.36), channel_id=1, source_target_pairs={{0,4},{4,0},{1,5},{5,1},{2,6},{6,2},{3,7},{7,3},{8,12},{12,8},{9,1... | collective-permute-start | bytes 319496 | tf_op jit(solution)/shard_map/ppermute | solution.py:14
  114.2 10.8 %collective-permute-start.3 = (f32[104,256]{1,0:T(8,128)}, f32[104,256]{1,0:T(8,128)S(1)}, u32[]{:S(2)}, u32[]{:S(2)}) collective-permute-start(f32[104,256]{1,0:T(8,128)} %reduce_sum.37), channel_id=1, source_target_pairs={{0,4},{4,0},{1,5},{5,1},{2,6},{6,2},{3,7},{7,3},{8,12},{12,8},{9,1... | collective-permute-start | bytes 319496 | tf_op jit(solution)/shard_map/ppermute | solution.py:14

commit v9 on v8

--- a/solution.py
+++ b/solution.py
@@ -22,27 +22,21 @@
     return jnp.concatenate([cut(got, source, 1, 0)[0] for source in sources], axis=1)
 
 
-def scatter_cores(right, left, owners):
+def half(right, left, side):
     rows_r, rows_l = right.shape[0] // C, left.shape[0] // C
-    own = jnp.concatenate([right[:rows_r], left[:rows_l], right[rows_r:], left[rows_l:]], axis=0)
+    return jnp.concatenate(
+        [cut(right, side * rows_r, rows_r, 0), cut(left, side * rows_l, rows_l, 0)], axis=0
+    )
+
+
+def scatter_cores(right, left, mine, owners):
+    own = jnp.concatenate([half(right, left, side) for side in range(C)], axis=0)
     own = own.reshape(Z * Y * C, -1, COLS)
     got = lax.all_to_all(own, ("c", "z", "y"), 0, 0, tiled=True)
     return pick(got, [(owner & 1) * (Z * Y) + (owner >> 1) for owner in owners])
 
 
-def scatter_chips(right, left, owners):
-    core, chip = lax.axis_index("c"), lax.axis_index(("z", "y"))
-    rows_r, rows_l = right.shape[0] // C, left.shape[0] // C
-
-    def half(side):
-        return (
-            cut(right, side * rows_r, rows_r, 0),
-            cut(left, side * rows_l, rows_l, 0),
-        )
-
-    far = swap(jnp.concatenate(half(1 - core), axis=0), "c")
-    wanted = jnp.where(chip == owners[0] >> 1, owners[0], owners[1]) & 1
-    mine = jnp.where(wanted == core, jnp.concatenate(half(core), axis=0), far)
+def scatter_chips(right, left, mine, owners):
     got = lax.all_to_all(mine.reshape(Z * Y, -1, COLS), ("z", "y"), 0, 0, tiled=True)
     return pick(got, [owner >> 1 for owner in owners])
 
@@ -61,12 +55,18 @@
 def shards(hidden_acts, out_grads, left_factors, right_factors, doc_tokens, owners):
     tok_rows = hidden_acts.shape[0]
     core, at_x = lax.axis_index("c"), lax.axis_index("x")
+    chip = lax.axis_index(("z", "y"))
     share = tok_rows // X
 
     right, left = right_factors[0], left_factors[0]
     rows_r = right.shape[0] // C
     owner = owners[0], owners[1]
-    picked = lax.cond(owner[0] ^ owner[1] == 1, scatter_cores, scatter_chips, right, left, owner)
+    far = swap(half(right, left, 1 - core), "c")
+    wanted = jnp.where(chip == owner[0] >> 1, owner[0], owner[1]) & 1
+    mine = jnp.where(wanted == core, half(right, left, core), far)
+    picked = lax.cond(
+        owner[0] ^ owner[1] == 1, scatter_cores, scatter_chips, right, left, mine, owner
+    )
 
     copies = jnp.broadcast_to(picked[None], (Z * Y, *picked.shape))
     mine = lax.all_to_all(copies, ("z", "y"), 0, 0, tiled=True).reshape(-1, 2 * COLS)
@@ -74,7 +74,6 @@
 
     near_g = dot(out_grads, mine[:rows_r], core)
     near_h = dot(hidden_acts, mine[rows_r:], core)
-    near_g, near_h, other = lax.optimization_barrier((near_g, near_h, other))
     proj_g = near_g + dot(out_grads, other[:rows_r], 1 - core)
     proj_h = near_h + dot(hidden_acts, other[rows_r:], 1 - core)
 

time: 137 us -> 135 us (0.985)
  other arithmetic: 8.04 us -> 6.51 us
    concatenate x1 -> x2, other arithmetic: 0.85 us -> 2.63 us  [half(): jnp.concatenate([cut(right, side * rows_r, rows_r, 0), cut(left, side * r...]
    add x2 -> x0, other arithmetic: 1.62 us -> none  [the longest x1 0.81 us: shards(): proj_g = near_g + dot(out_grads, other[:rows_r], 1 - core)]
    ppermute x4, waiting for transfers between devices: 6.55 us -> 8.09 us  [swap(): return lax.ppermute(block, axis, [(0, 1), (1, 0)])]
  transfers between devices with their start and end apart: 7 -> 7, of which waited for: 5 -> 5; matrix products, arithmetic and copies ran while one was open for 5% -> 6% of each run, Pallas kernels for 0% -> 0%
where the time goes in v9:
time: 135 us; the launch traced here: 133 us
  blocking collectives  43.4 us (32%)
  starting transfers between devices  35.4 us (26%)
  waiting for transfers between devices  34.5 us (26%)
  other arithmetic  6.51 us (5%)
  matrix products  5.48 us (4%)
  local copies, waits for them, and re-layouts  3.69 us (3%)
  loops' own time  2.5 us (2%)
  between operations  1.44 us (1%)
    all_to_all x1, blocking collectives, shards(): lax.all_to_all(copies, ('z', 'y'), 0, 0, tiled=True).reshape(-1, 2 * COLS)  35.7 us
    all_to_all x1, waiting for transfers between devices, scatter_chips(): lax.all_to_all(mine.reshape(Z * Y, -1, COLS), ('z', 'y'), 0, 0, tiled=True)  18.1 us
    all_to_all x1, starting transfers between devices, scatter_chips(): lax.all_to_all(mine.reshape(Z * Y, -1, COLS), ('z', 'y'), 0, 0, tiled=True)  13.8 us
    ppermute x4, starting transfers between devices, swap(): return lax.ppermute(block, axis, [(0, 1), (1, 0)])  13.3 us
    all_to_all x2, starting transfers between devices, sum_x(): parts = lax.all_to_all(proj, 'x', 0, 0, tiled=True)  8.41 us
    all_to_all x2, waiting for transfers between devices, sum_x(): parts = lax.all_to_all(proj, 'x', 0, 0, tiled=True)  8.22 us
    ppermute x4, waiting for transfers between devices, swap(): return lax.ppermute(block, axis, [(0, 1), (1, 0)])  8.09 us
    all_to_all x1, blocking collectives, shards(): summed = lax.all_to_all(copies, 'x', 0, 0, tiled=True).sum(axis=0)  7.71 us
  transfers between devices with their start and end apart: 7, of which 5 were waited for; matrix products, arithmetic and copies ran while one was open for 6% of the time, Pallas kernels for 0%

profile of v9, /device:TPU:56, one launch (start us, length us, event | category | flops | bytes accessed | tf_op | source)
XLA Modules:
  0.0 133.0 jit_solution(14084552159917785787)
XLA Ops:
  0.0 1.4 %dynamic-slice_bitcast_fusion.4 = (bf16[1792,128]{1,0:T(8,128)(2,1)S(1)}, bf16[1792,128]{1,0:T(8,128)(2,1)S(1)}) fusion(bf16[1,3584,128]{2,1,0:T(8,128)(2,1)} %param.10, s32[]{:T(128)S(6)} %mul.36, s32[]{:T(128)S(6)} %mul.33), kind=kLoop, calls=%fused_computation.22 | loop fusion | bytes 1835016 | tf_op jit(solution)/shard_map/dynamic_slice | solution.py:18
  2.1 0.9 pad_maximum_fusion.4
  2.9 1.9 %collective-permute-start = (bf16[2304,128]{1,0:T(8,128)(2,1)}, bf16[2304,128]{1,0:T(8,128)(2,1)}, u32[]{:S(2)}, u32[]{:S(2)}) collective-permute-start(bf16[2304,128]{1,0:T(8,128)(2,1)} %pad_maximum_fusion.4), channel_id=1, source_target_pairs={{0,8},{8,0},{1,9},{9,1},{2,10},{10,2},{3,11},{11,3},{4,12},{12,4},... | collective-permute-start | bytes 1769480 | tf_op jit(solution)/shard_map/ppermute | solution.py:14
  6.7 1.8 %pad_maximum_fusion.3 = bf16[2304,128]{1,0:T(8,128)(2,1)} fusion(bf16[1792,128]{1,0:T(8,128)(2,1)S(1)} %get-tuple-element.67, bf16[512,128]{1,0:T(8,128)(2,1)} %get-tuple-element.69), kind=kLoop, calls=%fused_computation.20 | loop fusion | flops 1179648 | bytes 1179648 | tf_op jit(solution)/shard_map/concatenate | solution.py:27
  8.5 37.2 %conditional.1 = (bf16[72,256]{1,0:T(8,128)(2,1)S(1)}) conditional(s32[]{:T(128)} %convert_element_type.4, (s32[]{:T(128)}, s32[]{:T(128)}, s32[]{:T(128)}, s32[]{:T(128)}, s32[]{:T(128)}, /*index=5*/bf16[2304,128]{1,0:T(8,128)(2,1)}, bf16[2304,128]{1,0:T(8,128)(2,1)}) %tuple.12, (bf16[1,1024,128]{2,1,0:T(8,128)(2,1)}, ...), branch_computations={%region_1.2_spmd, %region_2.3_spmd} | conditional | flops 4792328 | bytes 9453740 | solution.py:67
  10.4 2.0 %broadcast_select_fusion = bf16[2304,128]{1,0:T(8,128)(2,1)} fusion(bf16[2304,128]{1,0:T(8,128)(2,1)} %get-tuple-element.52, bf16[2304,128]{1,0:T(8,128)(2,1)} %get-tuple-element.53, pred[]{:T(512)S(6)} %eq.9), kind=kLoop, calls=%fused_computation | loop fusion | flops 294912 | bytes 1769473 | tf_op jit(solution)/shard_map/jit(_where)/select_n | solution.py:66
  12.3 13.8 %all-to-all-start = ((bf16[32,72,128]{2,1,0:T(8,128)(2,1)}), bf16[32,72,128]{2,1,0:T(8,128)(2,1)}, u32[]{:S(2)}, u32[]{:S(2)}) async-start(bf16[32,72,128]{2,1,0:T(8,128)(2,1)} %bitcast.40), calls=%async_computation | async-start | bytes 1179648 | tf_op jit(solution)/shard_map/cond/branch_0_fun/all_to_all | solution.py:40
  26.7 18.1 %all-to-all-done = bf16[32,72,128]{2,1,0:T(8,128)(2,1)} async-done(((bf16[32,72,128]{2,1,0:T(8,128)(2,1)}), bf16[32,72,128]{2,1,0:T(8,128)(2,1)}, u32[]{:S(2)}, u32[]{:S(2)}) %all-to-all-start) | async-done | bytes 589856 | tf_op jit(solution)/shard_map/cond/branch_0_fun/all_to_all | solution.py:40
  44.9 0.8 dynamic-slice_bitcast_fusion.1
  45.8 35.7 %all_to_all.36 = bf16[32,72,256]{2,1,0:T(8,128)(2,1)S(1)} all-to-all(bf16[32,72,256]{2,1,0:T(8,128)(2,1)S(1)} %broadcast_in_dim.4), channel_id=1, replica_groups=mesh['z'=8,'y'=4,'c'=2,'h'=2,'x'=4] {'z','y'}, dimensions={0} | all-to-all | bytes 2359296 | tf_op jit(solution)/shard_map/all_to_all | solution.py:72
  81.5 1.9 %collective-permute-start.1 = (bf16[2304,256]{1,0:T(8,128)(2,1)S(1)}, bf16[2304,256]{1,0:T(8,128)(2,1)S(1)}, u32[]{:S(2)}, u32[]{:S(2)}) collective-permute-start(bf16[2304,256]{1,0:T(8,128)(2,1)S(1)} %bitcast.41), channel_id=1, source_target_pairs={{0,8},{8,0},{1,9},{9,1},{2,10},{10,2},{3,11},{11,3},{4,12},{12,4},... | collective-permute-start | bytes 3538952 | tf_op jit(solution)/shard_map/ppermute | solution.py:14
  84.0 2.2 %collective-permute-done.1 = bf16[2304,256]{1,0:T(8,128)(2,1)S(1)} collective-permute-done((bf16[2304,256]{1,0:T(8,128)(2,1)S(1)}, bf16[2304,256]{1,0:T(8,128)(2,1)S(1)}, u32[]{:S(2)}, u32[]{:S(2)}) %collective-permute-start.1) | collective-permute-done | bytes 1179680 | tf_op jit(solution)/shard_map/ppermute | solution.py:14
  86.3 1.3 fusion.4
  87.6 4.3 %all-to-all-start.3 = ((f32[4,104,256]{2,1,0:T(8,128)}), f32[4,104,256]{2,1,0:T(8,128)S(1)}, u32[]{:S(2)}, u32[]{:S(2)}) async-start(f32[4,104,256]{2,1,0:T(8,128)} %bitcast.45), calls=%async_computation.3 | async-start | bytes 851968 | tf_op jit(solution)/shard_map/all_to_all | solution.py:51
  91.9 1.4 %fusion.10 = f32[416,256]{1,0:T(8,128)S(1)} fusion(bf16[416,1024]{1,0:T(8,128)(2,1)} %param.9, s32[]{:T(128)S(6)} %mul.34, bf16[2304,256]{1,0:T(8,128)(2,1)} %bitcast.43), kind=kOutput, calls=%fused_computation.25 | convolution fusion | flops 109051904 | bytes 1114116 | tf_op jit(solution)/shard_map/dot_general | solution.py:47
  93.3 2.0 %convolution_add_fusion = f32[416,256]{1,0:T(8,128)} fusion(f32[416,256]{1,0:T(8,128)S(1)} %fusion.10, bf16[416,1024]{1,0:T(8,128)(2,1)S(1)} %copy-done.4, s32[]{:T(128)S(6)} %mul.35, bf16[2304,256]{1,0:T(8,128)(2,1)} %copy-done.5), kind=kOutput, calls=%fused_computation.16 | convolution fusion | flops 109158400 | bytes 1540100 | tf_op jit(solution)/shard_map/dot_general | solution.py:47
  95.3 5.3 %all-to-all-done.3 = f32[4,104,256]{2,1,0:T(8,128)S(1)} async-done(((f32[4,104,256]{2,1,0:T(8,128)}), f32[4,104,256]{2,1,0:T(8,128)S(1)}, u32[]{:S(2)}, u32[]{:S(2)}) %all-to-all-start.3) | async-done | bytes 426016 | tf_op jit(solution)/shard_map/all_to_all | solution.py:51
  100.6 4.1 %all-to-all-start.4 = ((f32[4,104,256]{2,1,0:T(8,128)}), f32[4,104,256]{2,1,0:T(8,128)}, u32[]{:S(2)}, u32[]{:S(2)}) async-start(f32[4,104,256]{2,1,0:T(8,128)} %bitcast.44), calls=%async_computation.4 | async-start | bytes 851968 | tf_op jit(solution)/shard_map/all_to_all | solution.py:51
  105.0 4.7 %collective-permute-start.2 = (f32[104,256]{1,0:T(8,128)S(1)}, f32[104,256]{1,0:T(8,128)S(1)}, u32[]{:S(2)}, u32[]{:S(2)}) collective-permute-start(f32[104,256]{1,0:T(8,128)S(1)} %reduce_sum.36), channel_id=1, source_target_pairs={{0,4},{4,0},{1,5},{5,1},{2,6},{6,2},{3,7},{7,3},{8,12},{12,8},{9,1... | collective-permute-start | bytes 319496 | tf_op jit(solution)/shard_map/ppermute | solution.py:14
  109.7 2.9 %all-to-all-done.4 = f32[4,104,256]{2,1,0:T(8,128)} async-done(((f32[4,104,256]{2,1,0:T(8,128)}), f32[4,104,256]{2,1,0:T(8,128)}, u32[]{:S(2)}, u32[]{:S(2)}) %all-to-all-start.4) | async-done | bytes 426016 | tf_op jit(solution)/shard_map/all_to_all | solution.py:51
  112.6 1.0 reduce_sum.37
  113.7 4.7 %collective-permute-start.3 = (f32[104,256]{1,0:T(8,128)S(1)}, f32[104,256]{1,0:T(8,128)S(1)}, u32[]{:S(2)}, u32[]{:S(2)}) collective-permute-start(f32[104,256]{1,0:T(8,128)S(1)} %reduce_sum.37), channel_id=1, source_target_pairs={{0,4},{4,0},{1,5},{5,1},{2,6},{6,2},{3,7},{7,3},{8,12},{12,8},{9,1... | collective-permute-start | bytes 319496 | tf_op jit(solution)/shard_map/ppermute | solution.py:14
  118.4 5.9 %collective-permute-done.3 = f32[104,256]{1,0:T(8,128)S(1)} collective-permute-done((f32[104,256]{1,0:T(8,128)S(1)}, f32[104,256]{1,0:T(8,128)S(1)}, u32[]{:S(2)}, u32[]{:S(2)}) %collective-permute-start.3) | collective-permute-done | bytes 106528 | tf_op jit(solution)/shard_map/ppermute | solution.py:14
  124.6 7.7 %all_to_all.37 = f32[4,8,8]{2,1,0:T(8,128)S(1)} all-to-all(f32[4,8,8]{2,1,0:T(8,128)S(1)} %broadcast_in_dim.5), channel_id=1, replica_groups=mesh['z'=8,'y'=4,'c'=2,'h'=2,'x'=4] {'x'}, dimensions={0} | all-to-all | bytes 2048 | tf_op jit(solution)/shard_map/all_to_all | solution.py:97
  (32 shorter events, 3.1 us)
Async XLA Ops:
  0.0 83.4 %copy-start = (bf16[416,3584]{1,0:T(8,128)(2,1)S(1)}, bf16[416,3584]{1,0:T(8,128)(2,1)}, u32[]{:S(2)}) copy-start(bf16[416,3584]{1,0:T(8,128)(2,1)} %param.8) | copy-start | bytes 8945668
  0.0 1.4 %copy-start.2 = (bf16[1,1024,128]{2,1,0:T(8,128)(2,1)S(1)}, bf16[1,1024,128]{2,1,0:T(8,128)(2,1)}, u32[]{:S(2)}) copy-start(bf16[1,1024,128]{2,1,0:T(8,128)(2,1)} %param.11) | copy-start | bytes 786436
  1.4 3.5 %copy-start.6 = (s32[2]{0:T(128)S(1)}, s32[2]{0:T(128)}, u32[]{:S(2)}) copy-start(s32[2]{0:T(128)} %param.13) | copy-start | bytes 28
  2.9 5.6 %collective-permute-start = (bf16[2304,128]{1,0:T(8,128)(2,1)}, bf16[2304,128]{1,0:T(8,128)(2,1)}, u32[]{:S(2)}, u32[]{:S(2)}) collective-permute-start(bf16[2304,128]{1,0:T(8,128)(2,1)} %pad_maximum_fusion.4), channel_id=1, source_target_pairs={{0,8},{8,0},{1,9},{9,1},{2,10},{10,2},{3,11},{11,3},{4,12},{12,4},... | collective-permute-start | bytes 1769480 | tf_op jit(solution)/shard_map/ppermute | solution.py:14
  12.3 32.5 %all-to-all-start = ((bf16[32,72,128]{2,1,0:T(8,128)(2,1)}), bf16[32,72,128]{2,1,0:T(8,128)(2,1)}, u32[]{:S(2)}, u32[]{:S(2)}) async-start(bf16[32,72,128]{2,1,0:T(8,128)(2,1)} %bitcast.40), calls=%async_computation | async-start | bytes 1179648 | tf_op jit(solution)/shard_map/cond/branch_0_fun/all_to_all | solution.py:40
  81.5 2.5 %copy-start.1 = (bf16[32,72,256]{2,1,0:T(8,128)(2,1)}, bf16[32,72,256]{2,1,0:T(8,128)(2,1)S(1)}, u32[]{:S(2)}) copy-start(bf16[32,72,256]{2,1,0:T(8,128)(2,1)S(1)} %all_to_all.36) | copy-start | bytes 3538948
  81.5 4.7 %collective-permute-start.1 = (bf16[2304,256]{1,0:T(8,128)(2,1)S(1)}, bf16[2304,256]{1,0:T(8,128)(2,1)S(1)}, u32[]{:S(2)}, u32[]{:S(2)}) collective-permute-start(bf16[2304,256]{1,0:T(8,128)(2,1)S(1)} %bitcast.41), channel_id=1, source_target_pairs={{0,8},{8,0},{1,9},{9,1},{2,10},{10,2},{3,11},{11,3},{4,12},{12,4},... | collective-permute-start | bytes 3538952 | tf_op jit(solution)/shard_map/ppermute | solution.py:14
  86.3 1.3 copy-start.5
  87.6 13.0 %all-to-all-start.3 = ((f32[4,104,256]{2,1,0:T(8,128)}), f32[4,104,256]{2,1,0:T(8,128)S(1)}, u32[]{:S(2)}, u32[]{:S(2)}) async-start(f32[4,104,256]{2,1,0:T(8,128)} %bitcast.45), calls=%async_computation.3 | async-start | bytes 851968 | tf_op jit(solution)/shard_map/all_to_all | solution.py:51
  91.9 1.4 %copy-start.4 = (bf16[416,1024]{1,0:T(8,128)(2,1)S(1)}, bf16[416,1024]{1,0:T(8,128)(2,1)}, u32[]{:S(2)}) copy-start(bf16[416,1024]{1,0:T(8,128)(2,1)} %param.9) | copy-start | bytes 2555908
  93.3 11.4 %copy-start.7 = (s32[1,8]{1,0:T(1,128)S(1)}, s32[1,8]{1,0:T(1,128)}, u32[]{:S(2)}) copy-start(s32[1,8]{1,0:T(1,128)} %param.12) | copy-start | bytes 100
  100.6 12.0 %all-to-all-start.4 = ((f32[4,104,256]{2,1,0:T(8,128)}), f32[4,104,256]{2,1,0:T(8,128)}, u32[]{:S(2)}, u32[]{:S(2)}) async-start(f32[4,104,256]{2,1,0:T(8,128)} %bitcast.44), calls=%async_computation.4 | async-start | bytes 851968 | tf_op jit(solution)/shard_map/all_to_all | solution.py:51
  105.0 13.5 %collective-permute-start.2 = (f32[104,256]{1,0:T(8,128)S(1)}, f32[104,256]{1,0:T(8,128)S(1)}, u32[]{:S(2)}, u32[]{:S(2)}) collective-permute-start(f32[104,256]{1,0:T(8,128)S(1)} %reduce_sum.36), channel_id=1, source_target_pairs={{0,4},{4,0},{1,5},{5,1},{2,6},{6,2},{3,7},{7,3},{8,12},{12,8},{9,1... | collective-permute-start | bytes 319496 | tf_op jit(solution)/shard_map/ppermute | solution.py:14
  113.7 10.6 %collective-permute-start.3 = (f32[104,256]{1,0:T(8,128)S(1)}, f32[104,256]{1,0:T(8,128)S(1)}, u32[]{:S(2)}, u32[]{:S(2)}) collective-permute-start(f32[104,256]{1,0:T(8,128)S(1)} %reduce_sum.37), channel_id=1, source_target_pairs={{0,4},{4,0},{1,5},{5,1},{2,6},{6,2},{3,7},{7,3},{8,12},{12,8},{9,1... | collective-permute-start | bytes 319496 | tf_op jit(solution)/shard_map/ppermute | solution.py:14

commit v10 on v9

--- a/solution.py
+++ b/solution.py
@@ -1,6 +1,8 @@
 import jax
 import jax.numpy as jnp
 from jax import lax
+from jax.experimental import pallas as pl
+from jax.experimental.pallas import tpu as pltpu
 from jax.sharding import Mesh
 from jax.sharding import PartitionSpec as P
 
@@ -29,6 +31,82 @@
     )
 
 
+LEFT_CUTS = 4
+
+
+def half_copies(right, left, side, out, sems):
+    rows_r, rows_l = right.shape[0] // C, left.shape[0] // C
+    step = rows_l // LEFT_CUTS
+    copies = []
+    for i in range(LEFT_CUTS):
+        start = pl.multiple_of(side * rows_l + i * step, step)
+        copies.append(
+            pltpu.make_async_copy(
+                left.at[pl.ds(start, step)], out.at[pl.ds(rows_r + i * step, step)], sems.at[i]
+            )
+        )
+    start = pl.multiple_of(side * rows_r, rows_r)
+    copies.append(
+        pltpu.make_async_copy(
+            right.at[pl.ds(start, rows_r)], out.at[pl.ds(0, rows_r)], sems.at[LEFT_CUTS]
+        )
+    )
+    return copies
+
+
+def run(copies):
+    for copy in copies:
+        copy.start()
+    for copy in copies:
+        copy.wait()
+
+
+def send_kernel(right, left, out, sems):
+    run(half_copies(right, left, 1 - lax.axis_index("c"), out, sems))
+
+
+def keep_kernel(owners, right, left, far, out, sems):
+    core, chip = lax.axis_index("c"), lax.axis_index("z") * Y + lax.axis_index("y")
+    wanted = jnp.where(chip == owners[0] >> 1, owners[0], owners[1]) & 1
+
+    @pl.when(wanted == core)
+    def _():
+        run(half_copies(right, left, core, out, sems))
+
+    @pl.when(wanted != core)
+    def _():
+        count = LEFT_CUTS
+        step = out.shape[0] // count
+        run(
+            [
+                pltpu.make_async_copy(
+                    far.at[pl.ds(i * step, step)], out.at[pl.ds(i * step, step)], sems.at[i]
+                )
+                for i in range(count)
+            ]
+        )
+
+
+def local_copy(kernel, right, left, *more, owners=None):
+    rows = (right.shape[0] + left.shape[0]) // C
+    operands = (right, left, *more)
+    anywhere = pl.BlockSpec(memory_space=pl.ANY)
+    in_specs = [anywhere] * len(operands)
+    if owners is not None:
+        operands = (owners, *operands)
+        in_specs = [pl.BlockSpec(memory_space=pltpu.SMEM), *in_specs]
+    return pl.pallas_call(
+        kernel,
+        out_shape=jax.ShapeDtypeStruct((rows, right.shape[1]), right.dtype),
+        in_specs=in_specs,
+        out_specs=anywhere,
+        scratch_shapes=[pltpu.SemaphoreType.DMA((LEFT_CUTS + 1,))],
+        cost_estimate=pl.CostEstimate(
+            flops=0, bytes_accessed=4 * rows * right.shape[1], transcendentals=0
+        ),
+    )(*operands)
+
+
 def scatter_cores(right, left, mine, owners):
     own = jnp.concatenate([half(right, left, side) for side in range(C)], axis=0)
     own = own.reshape(Z * Y * C, -1, COLS)
@@ -55,15 +133,13 @@
 def shards(hidden_acts, out_grads, left_factors, right_factors, doc_tokens, owners):
     tok_rows = hidden_acts.shape[0]
     core, at_x = lax.axis_index("c"), lax.axis_index("x")
-    chip = lax.axis_index(("z", "y"))
     share = tok_rows // X
 
     right, left = right_factors[0], left_factors[0]
     rows_r = right.shape[0] // C
     owner = owners[0], owners[1]
-    far = swap(half(right, left, 1 - core), "c")
-    wanted = jnp.where(chip == owner[0] >> 1, owner[0], owner[1]) & 1
-    mine = jnp.where(wanted == core, half(right, left, core), far)
+    far = swap(local_copy(send_kernel, right, left), "c")
+    mine = local_copy(keep_kernel, right, left, far, owners=owners)
     picked = lax.cond(
         owner[0] ^ owner[1] == 1, scatter_cores, scatter_chips, right, left, mine, owner
     )

time: 135 us -> 165 us (1.22)
  Pallas kernels: 0 us -> 34.7 us
  other arithmetic: 6.51 us -> 1.93 us
  matrix products: 5.48 us -> 7.84 us
  local copies, waits for them, and re-layouts: 3.69 us -> 1.53 us
  blocking collectives: 43.4 us -> 45.3 us
  waiting for transfers between devices: 34.5 us -> 32.6 us
    pallas_call x0 -> x2, Pallas kernels: none -> 34.7 us  [local_copy(): pl.pallas_call(kernel, out_shape=jax.ShapeDtypeStruct((rows, right.shape[...]
    concatenate x2 -> x0, other arithmetic: 2.63 us -> none  [half(): jnp.concatenate([cut(right, side * rows_r, rows_r, 0), cut(left, side * r...]
    dot_general x4, matrix products: 5.3 us -> 7.66 us  [dot(): return jnp.dot(acts, part, preferred_element_type=jnp.float32)]
    dynamic_slice x2 -> x0, local copies, waits for them, and re-layouts: 2.05 us -> none  [cut(): lax.dynamic_slice_in_dim(block, start, size, axis, allow_negative_indices...]
    select_n x1 -> x0, other arithmetic: 1.95 us -> none  [shards(): mine = jnp.where(wanted == core, half(right, left, core), far)]
    all_to_all x1, blocking collectives: 35.7 us -> 37.6 us  [shards(): lax.all_to_all(copies, ('z', 'y'), 0, 0, tiled=True).reshape(-1, 2 * COLS)]
  transfers between devices with their start and end apart: 7 -> 7, of which waited for: 5 -> 6; matrix products, arithmetic and copies ran while one was open for 6% -> 4% of each run, Pallas kernels for 0% -> 0%
where the time goes in v10:
time: 165 us; the launch traced here: 162 us
  blocking collectives  45.3 us (27%)
  starting transfers between devices  35.5 us (22%)
  Pallas kernels  34.7 us (21%)
  waiting for transfers between devices  32.6 us (20%)
  matrix products  7.84 us (5%)
  other arithmetic  1.93 us (1%)
    all_to_all x1, blocking collectives, shards(): lax.all_to_all(copies, ('z', 'y'), 0, 0, tiled=True).reshape(-1, 2 * COLS)  37.6 us
    pallas_call x2, Pallas kernels, local_copy(): pl.pallas_call(kernel, out_shape=jax.ShapeDtypeStruct((rows, right.shape[...  34.7 us
    all_to_all x1, waiting for transfers between devices, scatter_chips(): lax.all_to_all(mine.reshape(Z * Y, -1, COLS), ('z', 'y'), 0, 0, tiled=True)  16.7 us
    all_to_all x1, starting transfers between devices, scatter_chips(): lax.all_to_all(mine.reshape(Z * Y, -1, COLS), ('z', 'y'), 0, 0, tiled=True)  13.8 us
    ppermute x4, starting transfers between devices, swap(): return lax.ppermute(block, axis, [(0, 1), (1, 0)])  13.3 us
    all_to_all x2, starting transfers between devices, sum_x(): parts = lax.all_to_all(proj, 'x', 0, 0, tiled=True)  8.41 us
    all_to_all x2, waiting for transfers between devices, sum_x(): parts = lax.all_to_all(proj, 'x', 0, 0, tiled=True)  8.2 us
    all_to_all x1, blocking collectives, shards(): summed = lax.all_to_all(copies, 'x', 0, 0, tiled=True).sum(axis=0)  7.71 us
  transfers between devices with their start and end apart: 7, of which 6 were waited for; matrix products, arithmetic and copies ran while one was open for 4% of the time, Pallas kernels for 0%

profile of v10, /device:TPU:56, one launch (start us, length us, event | category | flops | bytes accessed | tf_op | source)
XLA Modules:
  0.0 162.3 jit_solution(7308744222297060720)
XLA Ops:
  0.0 19.0 %shard_map.64 = bf16[2304,128]{1,0:T(8,128)(2,1)} custom-call(bf16[1024,128]{1,0:T(8,128)(2,1)} %bitcast.30, bf16[3584,128]{1,0:T(8,128)(2,1)} %bitcast.25), custom_call_target="tpu_custom_call" | custom-call | bytes 1179648 | tf_op jit(solution)/shard_map/pallas_call | solution.py:98
  19.0 1.9 %collective-permute-start = (bf16[2304,128]{1,0:T(8,128)(2,1)}, bf16[2304,128]{1,0:T(8,128)(2,1)}, u32[]{:S(2)}, u32[]{:S(2)}) collective-permute-start(bf16[2304,128]{1,0:T(8,128)(2,1)} %shard_map.64), channel_id=1, source_target_pairs={{0,8},{8,0},{1,9},{9,1},{2,10},{10,2},{3,11},{11,3},{4,12},{12,4},... | collective-permute-start | bytes 1769480 | tf_op jit(solution)/shard_map/ppermute | solution.py:16
  23.3 15.7 %shard_map.65 = bf16[2304,128]{1,0:T(8,128)(2,1)} custom-call(s32[2]{0:T(128)} %owners.1, bf16[1024,128]{1,0:T(8,128)(2,1)S(1)} %bitcast.31, bf16[3584,128]{1,0:T(8,128)(2,1)} %bitcast.26, bf16[2304,128]{1,0:T(8,128)(2,1)} %collective-permute-done.far), custom_call_target="tpu_custom_call" | custom-call | bytes 1179648 | tf_op jit(solution)/shard_map/pallas_call | solution.py:98
  39.0 32.6 %conditional.1 = (bf16[72,256]{1,0:T(8,128)(2,1)S(1)}) conditional(s32[]{:T(128)} %convert_element_type.4, (bf16[2304,128]{1,0:T(8,128)(2,1)}, s32[]{:T(128)}, s32[]{:T(128)}) %tuple.11, (bf16[1024,128]{1,0:T(8,128)(2,1)S(1)}, bf16[3584,128]{1,0:T(8,128)(2,1)}, s32[]{:T(128)}, s32[]{:T(128)}) %tuple.21), branch_computations={%region_1.0_spmd, %region_2.0_spmd} | conditional | flops 4792328 | bytes 8405136 | solution.py:143
  39.0 13.8 %all-to-all-start = ((bf16[32,72,128]{2,1,0:T(8,128)(2,1)}), bf16[32,72,128]{2,1,0:T(8,128)(2,1)}, u32[]{:S(2)}, u32[]{:S(2)}) async-start(bf16[32,72,128]{2,1,0:T(8,128)(2,1)} %bitcast.29), calls=%async_computation | async-start | bytes 1179648 | tf_op jit(solution)/shard_map/cond/branch_0_fun/all_to_all | solution.py:118
  54.2 16.7 %all-to-all-done = bf16[32,72,128]{2,1,0:T(8,128)(2,1)} async-done(((bf16[32,72,128]{2,1,0:T(8,128)(2,1)}), bf16[32,72,128]{2,1,0:T(8,128)(2,1)}, u32[]{:S(2)}, u32[]{:S(2)}) %all-to-all-start) | async-done | bytes 589856 | tf_op jit(solution)/shard_map/cond/branch_0_fun/all_to_all | solution.py:118
  70.9 0.7 dynamic-slice_bitcast_fusion.1
  71.7 37.6 %all_to_all.36 = bf16[32,72,256]{2,1,0:T(8,128)(2,1)} all-to-all(bf16[32,72,256]{2,1,0:T(8,128)(2,1)S(1)} %broadcast_in_dim.4), channel_id=1, replica_groups=mesh['z'=8,'y'=4,'c'=2,'h'=2,'x'=4] {'z','y'}, dimensions={0} | all-to-all | bytes 2359296 | tf_op jit(solution)/shard_map/all_to_all | solution.py:148
  109.4 1.9 %collective-permute-start.1 = (bf16[2304,256]{1,0:T(8,128)(2,1)}, bf16[2304,256]{1,0:T(8,128)(2,1)}, u32[]{:S(2)}, u32[]{:S(2)}) collective-permute-start(bf16[2304,256]{1,0:T(8,128)(2,1)} %bitcast.13), channel_id=1, source_target_pairs={{0,8},{8,0},{1,9},{9,1},{2,10},{10,2},{3,11},{11,3},{4,12},{12,4},... | collective-permute-start | bytes 3538952 | tf_op jit(solution)/shard_map/ppermute | solution.py:16
  111.3 1.7 %fusion.2 = f32[416,256]{1,0:T(8,128)S(1)} fusion(bf16[416,3584]{1,0:T(8,128)(2,1)S(1)} %copy-done, s32[]{:T(128)S(6)} %mul.25, bf16[2304,256]{1,0:T(8,128)(2,1)} %bitcast.13), kind=kOutput, calls=%fused_computation.9 | convolution fusion | flops 381681664 | bytes 2834436 | tf_op jit(solution)/shard_map/dot_general | solution.py:125
  113.1 1.4 collective-permute-done.1
  114.5 2.5 %fusion.4 = f32[416,256]{1,0:T(8,128)} fusion(f32[416,256]{1,0:T(8,128)S(1)} %fusion.2, bf16[416,3584]{1,0:T(8,128)(2,1)S(1)} %copy-done, s32[]{:T(128)S(6)} %mul.26, bf16[2304,256]{1,0:T(8,128)(2,1)} %collective-permute-done.1), kind=kOutput, calls=%fused_computation.12 | convolution fusion | flops 381788160 | bytes 3260420 | tf_op jit(solution)/shard_map/dot_general | solution.py:125
  117.0 4.3 %all-to-all-start.3 = ((f32[4,104,256]{2,1,0:T(8,128)}), f32[4,104,256]{2,1,0:T(8,128)S(1)}, u32[]{:S(2)}, u32[]{:S(2)}) async-start(f32[4,104,256]{2,1,0:T(8,128)} %bitcast.34), calls=%async_computation.3 | async-start | bytes 851968 | tf_op jit(solution)/shard_map/all_to_all | solution.py:129
  121.2 1.4 fusion.10
  122.7 2.0 %convolution_add_fusion = f32[416,256]{1,0:T(8,128)} fusion(f32[416,256]{1,0:T(8,128)S(1)} %fusion.10, bf16[416,1024]{1,0:T(8,128)(2,1)S(1)} %copy-done.2, s32[]{:T(128)S(6)} %mul.28, bf16[2304,256]{1,0:T(8,128)(2,1)} %collective-permute-done.1), kind=kOutput, calls=%fused_computation.11 | convolution fusion | flops 109158400 | bytes 1540100 | tf_op jit(solution)/shard_map/dot_general | solution.py:125
  124.7 5.3 %all-to-all-done.3 = f32[4,104,256]{2,1,0:T(8,128)S(1)} async-done(((f32[4,104,256]{2,1,0:T(8,128)}), f32[4,104,256]{2,1,0:T(8,128)S(1)}, u32[]{:S(2)}, u32[]{:S(2)}) %all-to-all-start.3) | async-done | bytes 426016 | tf_op jit(solution)/shard_map/all_to_all | solution.py:129
  130.0 4.1 %all-to-all-start.4 = ((f32[4,104,256]{2,1,0:T(8,128)}), f32[4,104,256]{2,1,0:T(8,128)}, u32[]{:S(2)}, u32[]{:S(2)}) async-start(f32[4,104,256]{2,1,0:T(8,128)} %bitcast.33), calls=%async_computation.4 | async-start | bytes 851968 | tf_op jit(solution)/shard_map/all_to_all | solution.py:129
  134.3 4.7 %collective-permute-start.2 = (f32[104,256]{1,0:T(8,128)S(1)}, f32[104,256]{1,0:T(8,128)S(1)}, u32[]{:S(2)}, u32[]{:S(2)}) collective-permute-start(f32[104,256]{1,0:T(8,128)S(1)} %reduce_sum.36), channel_id=1, source_target_pairs={{0,4},{4,0},{1,5},{5,1},{2,6},{6,2},{3,7},{7,3},{8,12},{12,8},{9,1... | collective-permute-start | bytes 319496 | tf_op jit(solution)/shard_map/ppermute | solution.py:16
  139.1 2.9 %all-to-all-done.4 = f32[4,104,256]{2,1,0:T(8,128)} async-done(((f32[4,104,256]{2,1,0:T(8,128)}), f32[4,104,256]{2,1,0:T(8,128)}, u32[]{:S(2)}, u32[]{:S(2)}) %all-to-all-start.4) | async-done | bytes 426016 | tf_op jit(solution)/shard_map/all_to_all | solution.py:129
  142.0 1.0 reduce_sum.37
  143.1 4.7 %collective-permute-start.3 = (f32[104,256]{1,0:T(8,128)S(1)}, f32[104,256]{1,0:T(8,128)S(1)}, u32[]{:S(2)}, u32[]{:S(2)}) collective-permute-start(f32[104,256]{1,0:T(8,128)S(1)} %reduce_sum.37), channel_id=1, source_target_pairs={{0,4},{4,0},{1,5},{5,1},{2,6},{6,2},{3,7},{7,3},{8,12},{12,8},{9,1... | collective-permute-start | bytes 319496 | tf_op jit(solution)/shard_map/ppermute | solution.py:16
  147.8 5.9 %collective-permute-done.3 = f32[104,256]{1,0:T(8,128)S(1)} collective-permute-done((f32[104,256]{1,0:T(8,128)S(1)}, f32[104,256]{1,0:T(8,128)S(1)}, u32[]{:S(2)}, u32[]{:S(2)}) %collective-permute-start.3) | collective-permute-done | bytes 106528 | tf_op jit(solution)/shard_map/ppermute | solution.py:16
  154.0 7.7 %all_to_all.37 = f32[4,8,8]{2,1,0:T(8,128)S(1)} all-to-all(f32[4,8,8]{2,1,0:T(8,128)S(1)} %broadcast_in_dim.5), channel_id=1, replica_groups=mesh['z'=8,'y'=4,'c'=2,'h'=2,'x'=4] {'x'}, dimensions={0} | all-to-all | bytes 2048 | tf_op jit(solution)/shard_map/all_to_all | solution.py:173
  161.7 0.6 broadcast_multiply_fusion
  (25 shorter events, 1.6 us)
Async XLA Ops:
  0.0 111.3 %copy-start = (bf16[416,3584]{1,0:T(8,128)(2,1)S(1)}, bf16[416,3584]{1,0:T(8,128)(2,1)}, u32[]{:S(2)}) copy-start(bf16[416,3584]{1,0:T(8,128)(2,1)} %param.8) | copy-start | bytes 8945668
  0.0 23.3 %copy-start.1 = (bf16[1,1024,128]{2,1,0:T(8,128)(2,1)S(1)}, bf16[1,1024,128]{2,1,0:T(8,128)(2,1)}, u32[]{:S(2)}) copy-start(bf16[1,1024,128]{2,1,0:T(8,128)(2,1)} %param.11) | copy-start | bytes 786436
  0.0 21.0 %copy-start.3 = (s32[2]{0:T(128)S(1)}, s32[2]{0:T(128)}, u32[]{:S(2)}) copy-start(s32[2]{0:T(128)} %owners.1) | copy-start | bytes 28
  19.0 4.2 %collective-permute-start = (bf16[2304,128]{1,0:T(8,128)(2,1)}, bf16[2304,128]{1,0:T(8,128)(2,1)}, u32[]{:S(2)}, u32[]{:S(2)}) collective-permute-start(bf16[2304,128]{1,0:T(8,128)(2,1)} %shard_map.64), channel_id=1, source_target_pairs={{0,8},{8,0},{1,9},{9,1},{2,10},{10,2},{3,11},{11,3},{4,12},{12,4},... | collective-permute-start | bytes 1769480 | tf_op jit(solution)/shard_map/ppermute | solution.py:16
  39.0 31.9 %all-to-all-start = ((bf16[32,72,128]{2,1,0:T(8,128)(2,1)}), bf16[32,72,128]{2,1,0:T(8,128)(2,1)}, u32[]{:S(2)}, u32[]{:S(2)}) async-start(bf16[32,72,128]{2,1,0:T(8,128)(2,1)} %bitcast.29), calls=%async_computation | async-start | bytes 1179648 | tf_op jit(solution)/shard_map/cond/branch_0_fun/all_to_all | solution.py:118
  109.4 5.1 %collective-permute-start.1 = (bf16[2304,256]{1,0:T(8,128)(2,1)}, bf16[2304,256]{1,0:T(8,128)(2,1)}, u32[]{:S(2)}, u32[]{:S(2)}) collective-permute-start(bf16[2304,256]{1,0:T(8,128)(2,1)} %bitcast.13), channel_id=1, source_target_pairs={{0,8},{8,0},{1,9},{9,1},{2,10},{10,2},{3,11},{11,3},{4,12},{12,4},... | collective-permute-start | bytes 3538952 | tf_op jit(solution)/shard_map/ppermute | solution.py:16
  117.0 13.0 %all-to-all-start.3 = ((f32[4,104,256]{2,1,0:T(8,128)}), f32[4,104,256]{2,1,0:T(8,128)S(1)}, u32[]{:S(2)}, u32[]{:S(2)}) async-start(f32[4,104,256]{2,1,0:T(8,128)} %bitcast.34), calls=%async_computation.3 | async-start | bytes 851968 | tf_op jit(solution)/shard_map/all_to_all | solution.py:129
  121.2 1.4 copy-start.2
  122.7 11.4 %copy-start.4 = (s32[1,8]{1,0:T(1,128)S(1)}, s32[1,8]{1,0:T(1,128)}, u32[]{:S(2)}) copy-start(s32[1,8]{1,0:T(1,128)} %param.12) | copy-start | bytes 100
  130.0 12.0 %all-to-all-start.4 = ((f32[4,104,256]{2,1,0:T(8,128)}), f32[4,104,256]{2,1,0:T(8,128)}, u32[]{:S(2)}, u32[]{:S(2)}) async-start(f32[4,104,256]{2,1,0:T(8,128)} %bitcast.33), calls=%async_computation.4 | async-start | bytes 851968 | tf_op jit(solution)/shard_map/all_to_all | solution.py:129
  134.3 13.5 %collective-permute-start.2 = (f32[104,256]{1,0:T(8,128)S(1)}, f32[104,256]{1,0:T(8,128)S(1)}, u32[]{:S(2)}, u32[]{:S(2)}) collective-permute-start(f32[104,256]{1,0:T(8,128)S(1)} %reduce_sum.36), channel_id=1, source_target_pairs={{0,4},{4,0},{1,5},{5,1},{2,6},{6,2},{3,7},{7,3},{8,12},{12,8},{9,1... | collective-permute-start | bytes 319496 | tf_op jit(solution)/shard_map/ppermute | solution.py:16
  143.1 10.6 %collective-permute-start.3 = (f32[104,256]{1,0:T(8,128)S(1)}, f32[104,256]{1,0:T(8,128)S(1)}, u32[]{:S(2)}, u32[]{:S(2)}) collective-permute-start(f32[104,256]{1,0:T(8,128)S(1)} %reduce_sum.37), channel_id=1, source_target_pairs={{0,4},{4,0},{1,5},{5,1},{2,6},{6,2},{3,7},{7,3},{8,12},{12,8},{9,1... | collective-permute-start | bytes 319496 | tf_op jit(solution)/shard_map/ppermute | solution.py:16

commit v11 on v9

--- a/solution.py
+++ b/solution.py
@@ -22,15 +22,15 @@
     return jnp.concatenate([cut(got, source, 1, 0)[0] for source in sources], axis=1)
 
 
-def half(right, left, side):
-    rows_r, rows_l = right.shape[0] // C, left.shape[0] // C
-    return jnp.concatenate(
-        [cut(right, side * rows_r, rows_r, 0), cut(left, side * rows_l, rows_l, 0)], axis=0
-    )
+def halves(factor, core):
+    rows = factor.shape[0] // C
+    low, high = factor[:rows], factor[rows:]
+    return jnp.where(core == 0, low, high), jnp.where(core == 0, high, low)
 
 
 def scatter_cores(right, left, mine, owners):
-    own = jnp.concatenate([half(right, left, side) for side in range(C)], axis=0)
+    rows_r, rows_l = right.shape[0] // C, left.shape[0] // C
+    own = jnp.concatenate([right[:rows_r], left[:rows_l], right[rows_r:], left[rows_l:]], axis=0)
     own = own.reshape(Z * Y * C, -1, COLS)
     got = lax.all_to_all(own, ("c", "z", "y"), 0, 0, tiled=True)
     return pick(got, [(owner & 1) * (Z * Y) + (owner >> 1) for owner in owners])
@@ -61,9 +61,13 @@
     right, left = right_factors[0], left_factors[0]
     rows_r = right.shape[0] // C
     owner = owners[0], owners[1]
-    far = swap(half(right, left, 1 - core), "c")
-    wanted = jnp.where(chip == owner[0] >> 1, owner[0], owner[1]) & 1
-    mine = jnp.where(wanted == core, half(right, left, core), far)
+    near_r, send_r = halves(right, core)
+    near_l, send_l = halves(left, core)
+    far = swap(jnp.concatenate([send_r, send_l], axis=0), "c")
+    wanted = (jnp.where(chip == owner[0] >> 1, owner[0], owner[1]) & 1) == core
+    mine = jnp.concatenate(
+        [jnp.where(wanted, near_r, far[:rows_r]), jnp.where(wanted, near_l, far[rows_r:])], axis=0
+    )
     picked = lax.cond(
         owner[0] ^ owner[1] == 1, scatter_cores, scatter_chips, right, left, mine, owner
     )

time: 135 us -> 136 us (level)
  matrix products: 5.48 us -> 7.86 us
  between operations: 1.44 us -> 3.35 us
  waiting for transfers between devices: 34.5 us -> 33 us
    dot_general x4, matrix products: 5.3 us -> 7.67 us  [dot(): return jnp.dot(acts, part, preferred_element_type=jnp.float32)]
    dynamic_slice x2 -> x0, local copies, waits for them, and re-layouts: 2.05 us -> none  [cut(): lax.dynamic_slice_in_dim(block, start, size, axis, allow_negative_indices...]
    concatenate x2, other arithmetic: 2.63 us -> 0.89 us  [the longest x1 0.85 us: shards(): far = swap(jnp.concatenate([send_r, send_l], axis=0), 'c')]
    select_n x1 -> x4, other arithmetic: 1.95 us -> 3.67 us  [the longest x2 1.38 us: halves(): return (jnp.where(core == 0, low, high), jnp.where(core == 0, high, low))]
  transfers between devices with their start and end apart: 7 -> 7, of which waited for: 5 -> 5; matrix products, arithmetic and copies ran while one was open for 6% -> 5% of each run, Pallas kernels for 0% -> 0%
where the time goes in v11:
time: 136 us; the launch traced here: 133 us
  blocking collectives  43.5 us (32%)
  starting transfers between devices  35.4 us (26%)
  waiting for transfers between devices  33 us (24%)
  matrix products  7.86 us (6%)
  other arithmetic  6.48 us (5%)
  between operations  3.35 us (2%)
  local copies, waits for them, and re-layouts  2.33 us (2%)
    all_to_all x1, blocking collectives, shards(): lax.all_to_all(copies, ('z', 'y'), 0, 0, tiled=True).reshape(-1, 2 * COLS)  35.8 us
    all_to_all x1, waiting for transfers between devices, scatter_chips(): lax.all_to_all(mine.reshape(Z * Y, -1, COLS), ('z', 'y'), 0, 0, tiled=True)  17.5 us
    all_to_all x1, starting transfers between devices, scatter_chips(): lax.all_to_all(mine.reshape(Z * Y, -1, COLS), ('z', 'y'), 0, 0, tiled=True)  13.8 us
    ppermute x4, starting transfers between devices, swap(): return lax.ppermute(block, axis, [(0, 1), (1, 0)])  13.3 us
    all_to_all x2, starting transfers between devices, sum_x(): parts = lax.all_to_all(proj, 'x', 0, 0, tiled=True)  8.41 us
    all_to_all x2, waiting for transfers between devices, sum_x(): parts = lax.all_to_all(proj, 'x', 0, 0, tiled=True)  8.21 us
    all_to_all x1, blocking collectives, shards(): summed = lax.all_to_all(copies, 'x', 0, 0, tiled=True).sum(axis=0)  7.71 us
    dot_general x4, matrix products, dot(): return jnp.dot(acts, part, preferred_element_type=jnp.float32)  7.67 us
  transfers between devices with their start and end apart: 7, of which 5 were waited for; matrix products, arithmetic and copies ran while one was open for 5% of the time, Pallas kernels for 0%

profile of v11, /device:TPU:56, one launch (start us, length us, event | category | flops | bytes accessed | tf_op | source)
XLA Modules:
  0.0 133.3 jit_solution(7022751575136347032)
XLA Ops:
  0.0 1.4 %select_bitcast_fusion = bf16[1792,128]{1,0:T(8,128)(2,1)S(1)} fusion(pred[]{:T(512)S(6)} %eq.18, bf16[1,3584,128]{2,1,0:T(8,128)(2,1)} %param.10), kind=kLoop, calls=%fused_computation.22 | loop fusion | flops 229376 | bytes 1376257 | tf_op jit(solution)/shard_map/jit(_where)/select_n | solution.py:28
  1.4 0.8 pad_maximum_fusion.3
  2.3 1.9 %collective-permute-start = (bf16[2304,128]{1,0:T(8,128)(2,1)}, bf16[2304,128]{1,0:T(8,128)(2,1)}, u32[]{:S(2)}, u32[]{:S(2)}) collective-permute-start(bf16[2304,128]{1,0:T(8,128)(2,1)} %pad_maximum_fusion.3), channel_id=1, source_target_pairs={{0,8},{8,0},{1,9},{9,1},{2,10},{10,2},{3,11},{11,3},{4,12},{12,4},... | collective-permute-start | bytes 1769480 | tf_op jit(solution)/shard_map/ppermute | solution.py:14
  7.9 1.4 %slice_select_fusion = bf16[1792,128]{1,0:T(8,128)(2,1)S(1)} fusion(bf16[2304,128]{1,0:T(8,128)(2,1)} %collective-permute-done, pred[]{:T(512)S(6)} %eq.17, pred[]{:T(512)S(6)} %eq.18, bf16[1,3584,128]{2,1,0:T(8,128)(2,1)} %param.10), kind=kLoop, calls=%fused_computation.21 | loop fusion | flops 458752 | bytes 1835010 | tf_op jit(solution)/shard_map/jit(_where)/select_n | solution.py:69
  9.3 0.9 slice_select_fusion.1
  10.3 34.1 %conditional.1 = (bf16[72,256]{1,0:T(8,128)(2,1)S(1)}) conditional(s32[]{:T(128)} %convert_element_type.4, (bf16[2304,128]{1,0:T(8,128)(2,1)S(1)}, s32[]{:T(128)}, s32[]{:T(128)}) %tuple.11, (bf16[1,1024,128]{2,1,0:T(8,128)(2,1)S(1)}, bf16[1,3584,128]{2,1,0:T(8,128)(2,1)}, s32[]{:T(128)}, s32[]{:T(128)}) %tuple.20), branch_computations={%region_1.2_spmd, %region_2.3_spmd} | conditional | flops 4792328 | bytes 8405136 | solution.py:71
  11.1 13.8 %all-to-all-start = ((bf16[32,72,128]{2,1,0:T(8,128)(2,1)}), bf16[32,72,128]{2,1,0:T(8,128)(2,1)}, u32[]{:S(2)}, u32[]{:S(2)}) async-start(bf16[32,72,128]{2,1,0:T(8,128)(2,1)} %bitcast.40), calls=%async_computation | async-start | bytes 1179648 | tf_op jit(solution)/shard_map/cond/branch_0_fun/all_to_all | solution.py:40
  26.1 17.5 %all-to-all-done = bf16[32,72,128]{2,1,0:T(8,128)(2,1)} async-done(((bf16[32,72,128]{2,1,0:T(8,128)(2,1)}), bf16[32,72,128]{2,1,0:T(8,128)(2,1)}, u32[]{:S(2)}, u32[]{:S(2)}) %all-to-all-start) | async-done | bytes 589856 | tf_op jit(solution)/shard_map/cond/branch_0_fun/all_to_all | solution.py:40
  44.5 35.8 %all_to_all.36 = bf16[32,72,256]{2,1,0:T(8,128)(2,1)} all-to-all(bf16[32,72,256]{2,1,0:T(8,128)(2,1)S(1)} %broadcast_in_dim.4), channel_id=1, replica_groups=mesh['z'=8,'y'=4,'c'=2,'h'=2,'x'=4] {'z','y'}, dimensions={0} | all-to-all | bytes 2359296 | tf_op jit(solution)/shard_map/all_to_all | solution.py:76
  80.3 1.9 %collective-permute-start.1 = (bf16[2304,256]{1,0:T(8,128)(2,1)}, bf16[2304,256]{1,0:T(8,128)(2,1)}, u32[]{:S(2)}, u32[]{:S(2)}) collective-permute-start(bf16[2304,256]{1,0:T(8,128)(2,1)} %bitcast.19), channel_id=1, source_target_pairs={{0,8},{8,0},{1,9},{9,1},{2,10},{10,2},{3,11},{11,3},{4,12},{12,4},... | collective-permute-start | bytes 3538952 | tf_op jit(solution)/shard_map/ppermute | solution.py:14
  82.3 1.7 %fusion.2 = f32[416,256]{1,0:T(8,128)S(1)} fusion(bf16[416,3584]{1,0:T(8,128)(2,1)S(1)} %copy-done, s32[]{:T(128)S(6)} %mul.28, bf16[2304,256]{1,0:T(8,128)(2,1)} %bitcast.19), kind=kOutput, calls=%fused_computation.13 | convolution fusion | flops 381681664 | bytes 2834436 | tf_op jit(solution)/shard_map/dot_general | solution.py:47
  84.0 1.4 %collective-permute-done.1 = bf16[2304,256]{1,0:T(8,128)(2,1)} collective-permute-done((bf16[2304,256]{1,0:T(8,128)(2,1)}, bf16[2304,256]{1,0:T(8,128)(2,1)}, u32[]{:S(2)}, u32[]{:S(2)}) %collective-permute-start.1) | collective-permute-done | bytes 1179680 | tf_op jit(solution)/shard_map/ppermute | solution.py:14
  85.4 2.5 %fusion.4 = f32[416,256]{1,0:T(8,128)} fusion(f32[416,256]{1,0:T(8,128)S(1)} %fusion.2, bf16[416,3584]{1,0:T(8,128)(2,1)S(1)} %copy-done, s32[]{:T(128)S(6)} %mul.30, bf16[2304,256]{1,0:T(8,128)(2,1)} %collective-permute-done.1), kind=kOutput, calls=%fused_computation.16 | convolution fusion | flops 381788160 | bytes 3260420 | tf_op jit(solution)/shard_map/dot_general | solution.py:47
  87.9 4.3 %all-to-all-start.3 = ((f32[4,104,256]{2,1,0:T(8,128)}), f32[4,104,256]{2,1,0:T(8,128)S(1)}, u32[]{:S(2)}, u32[]{:S(2)}) async-start(f32[4,104,256]{2,1,0:T(8,128)} %bitcast.42), calls=%async_computation.3 | async-start | bytes 851968 | tf_op jit(solution)/shard_map/all_to_all | solution.py:51
  92.2 1.4 %fusion.10 = f32[416,256]{1,0:T(8,128)S(1)} fusion(bf16[416,1024]{1,0:T(8,128)(2,1)} %param.9, s32[]{:T(128)S(6)} %mul.31, bf16[2304,256]{1,0:T(8,128)(2,1)} %bitcast.19), kind=kOutput, calls=%fused_computation.24 | convolution fusion | flops 109051904 | bytes 1114116 | tf_op jit(solution)/shard_map/dot_general | solution.py:47
  93.6 2.0 %convolution_add_fusion = f32[416,256]{1,0:T(8,128)} fusion(f32[416,256]{1,0:T(8,128)S(1)} %fusion.10, bf16[416,1024]{1,0:T(8,128)(2,1)S(1)} %copy-done.3, s32[]{:T(128)S(6)} %mul.32, bf16[2304,256]{1,0:T(8,128)(2,1)} %collective-permute-done.1), kind=kOutput, calls=%fused_computation.15 | convolution fusion | flops 109158400 | bytes 1540100 | tf_op jit(solution)/shard_map/dot_general | solution.py:47
  95.7 5.2 %all-to-all-done.3 = f32[4,104,256]{2,1,0:T(8,128)S(1)} async-done(((f32[4,104,256]{2,1,0:T(8,128)}), f32[4,104,256]{2,1,0:T(8,128)S(1)}, u32[]{:S(2)}, u32[]{:S(2)}) %all-to-all-start.3) | async-done | bytes 426016 | tf_op jit(solution)/shard_map/all_to_all | solution.py:51
  100.9 4.1 %all-to-all-start.4 = ((f32[4,104,256]{2,1,0:T(8,128)}), f32[4,104,256]{2,1,0:T(8,128)}, u32[]{:S(2)}, u32[]{:S(2)}) async-start(f32[4,104,256]{2,1,0:T(8,128)} %bitcast.41), calls=%async_computation.4 | async-start | bytes 851968 | tf_op jit(solution)/shard_map/all_to_all | solution.py:51
  105.3 4.7 %collective-permute-start.2 = (f32[104,256]{1,0:T(8,128)S(1)}, f32[104,256]{1,0:T(8,128)S(1)}, u32[]{:S(2)}, u32[]{:S(2)}) collective-permute-start(f32[104,256]{1,0:T(8,128)S(1)} %reduce_sum.36), channel_id=1, source_target_pairs={{0,4},{4,0},{1,5},{5,1},{2,6},{6,2},{3,7},{7,3},{8,12},{12,8},{9,1... | collective-permute-start | bytes 319496 | tf_op jit(solution)/shard_map/ppermute | solution.py:14
  110.0 3.0 %all-to-all-done.4 = f32[4,104,256]{2,1,0:T(8,128)} async-done(((f32[4,104,256]{2,1,0:T(8,128)}), f32[4,104,256]{2,1,0:T(8,128)}, u32[]{:S(2)}, u32[]{:S(2)}) %all-to-all-start.4) | async-done | bytes 426016 | tf_op jit(solution)/shard_map/all_to_all | solution.py:51
  112.9 1.0 reduce_sum.37
  114.0 4.7 %collective-permute-start.3 = (f32[104,256]{1,0:T(8,128)S(1)}, f32[104,256]{1,0:T(8,128)S(1)}, u32[]{:S(2)}, u32[]{:S(2)}) collective-permute-start(f32[104,256]{1,0:T(8,128)S(1)} %reduce_sum.37), channel_id=1, source_target_pairs={{0,4},{4,0},{1,5},{5,1},{2,6},{6,2},{3,7},{7,3},{8,12},{12,8},{9,1... | collective-permute-start | bytes 319496 | tf_op jit(solution)/shard_map/ppermute | solution.py:14
  118.7 5.9 %collective-permute-done.3 = f32[104,256]{1,0:T(8,128)S(1)} collective-permute-done((f32[104,256]{1,0:T(8,128)S(1)}, f32[104,256]{1,0:T(8,128)S(1)}, u32[]{:S(2)}, u32[]{:S(2)}) %collective-permute-start.3) | collective-permute-done | bytes 106528 | tf_op jit(solution)/shard_map/ppermute | solution.py:14
  125.0 7.7 %all_to_all.37 = f32[4,8,8]{2,1,0:T(8,128)S(1)} all-to-all(f32[4,8,8]{2,1,0:T(8,128)S(1)} %broadcast_in_dim.5), channel_id=1, replica_groups=mesh['z'=8,'y'=4,'c'=2,'h'=2,'x'=4] {'x'}, dimensions={0} | all-to-all | bytes 2048 | tf_op jit(solution)/shard_map/all_to_all | solution.py:101
  (31 shorter events, 3.5 us)
Async XLA Ops:
  0.0 82.3 %copy-start = (bf16[416,3584]{1,0:T(8,128)(2,1)S(1)}, bf16[416,3584]{1,0:T(8,128)(2,1)}, u32[]{:S(2)}) copy-start(bf16[416,3584]{1,0:T(8,128)(2,1)} %param.8) | copy-start | bytes 8945668
  0.0 1.4 %copy-start.2 = (bf16[1,1024,128]{2,1,0:T(8,128)(2,1)S(1)}, bf16[1,1024,128]{2,1,0:T(8,128)(2,1)}, u32[]{:S(2)}) copy-start(bf16[1,1024,128]{2,1,0:T(8,128)(2,1)} %param.11) | copy-start | bytes 786436
  0.0 4.2 %copy-start.4 = (s32[2]{0:T(128)S(1)}, s32[2]{0:T(128)}, u32[]{:S(2)}) copy-start(s32[2]{0:T(128)} %param.13) | copy-start | bytes 28
  2.3 5.7 %collective-permute-start = (bf16[2304,128]{1,0:T(8,128)(2,1)}, bf16[2304,128]{1,0:T(8,128)(2,1)}, u32[]{:S(2)}, u32[]{:S(2)}) collective-permute-start(bf16[2304,128]{1,0:T(8,128)(2,1)} %pad_maximum_fusion.3), channel_id=1, source_target_pairs={{0,8},{8,0},{1,9},{9,1},{2,10},{10,2},{3,11},{11,3},{4,12},{12,4},... | collective-permute-start | bytes 1769480 | tf_op jit(solution)/shard_map/ppermute | solution.py:14
  10.3 0.8 copy-start.1
  11.1 32.6 %all-to-all-start = ((bf16[32,72,128]{2,1,0:T(8,128)(2,1)}), bf16[32,72,128]{2,1,0:T(8,128)(2,1)}, u32[]{:S(2)}, u32[]{:S(2)}) async-start(bf16[32,72,128]{2,1,0:T(8,128)(2,1)} %bitcast.40), calls=%async_computation | async-start | bytes 1179648 | tf_op jit(solution)/shard_map/cond/branch_0_fun/all_to_all | solution.py:40
  80.3 5.1 %collective-permute-start.1 = (bf16[2304,256]{1,0:T(8,128)(2,1)}, bf16[2304,256]{1,0:T(8,128)(2,1)}, u32[]{:S(2)}, u32[]{:S(2)}) collective-permute-start(bf16[2304,256]{1,0:T(8,128)(2,1)} %bitcast.19), channel_id=1, source_target_pairs={{0,8},{8,0},{1,9},{9,1},{2,10},{10,2},{3,11},{11,3},{4,12},{12,4},... | collective-permute-start | bytes 3538952 | tf_op jit(solution)/shard_map/ppermute | solution.py:14
  87.9 13.0 %all-to-all-start.3 = ((f32[4,104,256]{2,1,0:T(8,128)}), f32[4,104,256]{2,1,0:T(8,128)S(1)}, u32[]{:S(2)}, u32[]{:S(2)}) async-start(f32[4,104,256]{2,1,0:T(8,128)} %bitcast.42), calls=%async_computation.3 | async-start | bytes 851968 | tf_op jit(solution)/shard_map/all_to_all | solution.py:51
  92.2 1.4 %copy-start.3 = (bf16[416,1024]{1,0:T(8,128)(2,1)S(1)}, bf16[416,1024]{1,0:T(8,128)(2,1)}, u32[]{:S(2)}) copy-start(bf16[416,1024]{1,0:T(8,128)(2,1)} %param.9) | copy-start | bytes 2555908
  93.6 11.4 %copy-start.5 = (s32[1,8]{1,0:T(1,128)S(1)}, s32[1,8]{1,0:T(1,128)}, u32[]{:S(2)}) copy-start(s32[1,8]{1,0:T(1,128)} %param.12) | copy-start | bytes 100
  100.9 12.0 %all-to-all-start.4 = ((f32[4,104,256]{2,1,0:T(8,128)}), f32[4,104,256]{2,1,0:T(8,128)}, u32[]{:S(2)}, u32[]{:S(2)}) async-start(f32[4,104,256]{2,1,0:T(8,128)} %bitcast.41), calls=%async_computation.4 | async-start | bytes 851968 | tf_op jit(solution)/shard_map/all_to_all | solution.py:51
  105.3 13.5 %collective-permute-start.2 = (f32[104,256]{1,0:T(8,128)S(1)}, f32[104,256]{1,0:T(8,128)S(1)}, u32[]{:S(2)}, u32[]{:S(2)}) collective-permute-start(f32[104,256]{1,0:T(8,128)S(1)} %reduce_sum.36), channel_id=1, source_target_pairs={{0,4},{4,0},{1,5},{5,1},{2,6},{6,2},{3,7},{7,3},{8,12},{12,8},{9,1... | collective-permute-start | bytes 319496 | tf_op jit(solution)/shard_map/ppermute | solution.py:14
  114.0 10.6 %collective-permute-start.3 = (f32[104,256]{1,0:T(8,128)S(1)}, f32[104,256]{1,0:T(8,128)S(1)}, u32[]{:S(2)}, u32[]{:S(2)}) collective-permute-start(f32[104,256]{1,0:T(8,128)S(1)} %reduce_sum.37), channel_id=1, source_target_pairs={{0,4},{4,0},{1,5},{5,1},{2,6},{6,2},{3,7},{7,3},{8,12},{12,8},{9,1... | collective-permute-start | bytes 319496 | tf_op jit(solution)/shard_map/ppermute | solution.py:14

commit v12 on v9

--- a/solution.py
+++ b/solution.py
@@ -55,15 +55,19 @@
 def shards(hidden_acts, out_grads, left_factors, right_factors, doc_tokens, owners):
     tok_rows = hidden_acts.shape[0]
     core, at_x = lax.axis_index("c"), lax.axis_index("x")
-    chip = lax.axis_index(("z", "y"))
+    device = lax.axis_index(("z", "y", "c"))
     share = tok_rows // X
 
     right, left = right_factors[0], left_factors[0]
     rows_r = right.shape[0] // C
     owner = owners[0], owners[1]
     far = swap(half(right, left, 1 - core), "c")
-    wanted = jnp.where(chip == owner[0] >> 1, owner[0], owner[1]) & 1
-    mine = jnp.where(wanted == core, half(right, left, core), far)
+    wanted = (owner[0] == device) | (owner[1] == device)
+    rows_l = left.shape[0] // C
+    near_r, near_l = cut(right, core * rows_r, rows_r, 0), cut(left, core * rows_l, rows_l, 0)
+    mine = jnp.concatenate(
+        [jnp.where(wanted, near_r, far[:rows_r]), jnp.where(wanted, near_l, far[rows_r:])], axis=0
+    )
     picked = lax.cond(
         owner[0] ^ owner[1] == 1, scatter_cores, scatter_chips, right, left, mine, owner
     )

time: 135 us -> 134 us (level)
  other arithmetic: 6.51 us -> 5.06 us
    concatenate x2 -> x1, other arithmetic: 2.63 us -> 0.85 us  [half(): jnp.concatenate([cut(right, side * rows_r, rows_r, 0), cut(left, side * r...]
  transfers between devices with their start and end apart: 7 -> 7, of which waited for: 5 -> 5; matrix products, arithmetic and copies ran while one was open for 6% -> 4% of each run, Pallas kernels for 0% -> 0%
where the time goes in v12:
time: 134 us; the launch traced here: 132 us
  blocking collectives  43.4 us (32%)
  starting transfers between devices  35.4 us (26%)
  waiting for transfers between devices  33.8 us (25%)
  matrix products  5.49 us (4%)
  other arithmetic  5.06 us (4%)
  local copies, waits for them, and re-layouts  4.47 us (3%)
  between operations  2.67 us (2%)
    all_to_all x1, blocking collectives, shards(): lax.all_to_all(copies, ('z', 'y'), 0, 0, tiled=True).reshape(-1, 2 * COLS)  35.7 us
    all_to_all x1, waiting for transfers between devices, scatter_chips(): lax.all_to_all(mine.reshape(Z * Y, -1, COLS), ('z', 'y'), 0, 0, tiled=True)  17.6 us
    all_to_all x1, starting transfers between devices, scatter_chips(): lax.all_to_all(mine.reshape(Z * Y, -1, COLS), ('z', 'y'), 0, 0, tiled=True)  13.8 us
    ppermute x4, starting transfers between devices, swap(): return lax.ppermute(block, axis, [(0, 1), (1, 0)])  13.3 us
    all_to_all x2, starting transfers between devices, sum_x(): parts = lax.all_to_all(proj, 'x', 0, 0, tiled=True)  8.4 us
    all_to_all x2, waiting for transfers between devices, sum_x(): parts = lax.all_to_all(proj, 'x', 0, 0, tiled=True)  8.2 us
    ppermute x4, waiting for transfers between devices, swap(): return lax.ppermute(block, axis, [(0, 1), (1, 0)])  8.09 us
    all_to_all x1, blocking collectives, shards(): summed = lax.all_to_all(copies, 'x', 0, 0, tiled=True).sum(axis=0)  7.71 us
  transfers between devices with their start and end apart: 7, of which 5 were waited for; matrix products, arithmetic and copies ran while one was open for 4% of the time, Pallas kernels for 0%

profile of v12, /device:TPU:56, one launch (start us, length us, event | category | flops | bytes accessed | tf_op | source)
XLA Modules:
  0.0 131.7 jit_solution(17284551413848001951)
XLA Ops:
  0.0 1.2 dynamic-slice_bitcast_fusion.4
  1.2 0.9 dynamic-slice_bitcast_fusion.5
  2.2 0.9 pad_maximum_fusion.3
  3.0 1.9 %collective-permute-start = (bf16[2304,128]{1,0:T(8,128)(2,1)}, bf16[2304,128]{1,0:T(8,128)(2,1)}, u32[]{:S(2)}, u32[]{:S(2)}) collective-permute-start(bf16[2304,128]{1,0:T(8,128)(2,1)} %pad_maximum_fusion.3), channel_id=1, source_target_pairs={{0,8},{8,0},{1,9},{9,1},{2,10},{10,2},{3,11},{11,3},{4,12},{12,4},... | collective-permute-start | bytes 1769480 | tf_op jit(solution)/shard_map/ppermute | solution.py:14
  8.0 1.3 slice_select_fusion
  9.3 0.9 slice_select_fusion.1
  10.3 34.1 %conditional.1 = (bf16[72,256]{1,0:T(8,128)(2,1)S(1)}) conditional(s32[]{:T(128)} %convert_element_type.4, (bf16[2304,128]{1,0:T(8,128)(2,1)S(1)}, s32[]{:T(128)}, s32[]{:T(128)}) %tuple.11, (bf16[1,1024,128]{2,1,0:T(8,128)(2,1)S(1)}, bf16[1,3584,128]{2,1,0:T(8,128)(2,1)}, s32[]{:T(128)}, s32[]{:T(128)}) %tuple.20), branch_computations={%region_1.2_spmd, %region_2.3_spmd} | conditional | flops 4792328 | bytes 8405136 | solution.py:71
  11.1 13.8 %all-to-all-start = ((bf16[32,72,128]{2,1,0:T(8,128)(2,1)}), bf16[32,72,128]{2,1,0:T(8,128)(2,1)}, u32[]{:S(2)}, u32[]{:S(2)}) async-start(bf16[32,72,128]{2,1,0:T(8,128)(2,1)} %bitcast.40), calls=%async_computation | async-start | bytes 1179648 | tf_op jit(solution)/shard_map/cond/branch_0_fun/all_to_all | solution.py:40
  26.1 17.6 %all-to-all-done = bf16[32,72,128]{2,1,0:T(8,128)(2,1)} async-done(((bf16[32,72,128]{2,1,0:T(8,128)(2,1)}), bf16[32,72,128]{2,1,0:T(8,128)(2,1)}, u32[]{:S(2)}, u32[]{:S(2)}) %all-to-all-start) | async-done | bytes 589856 | tf_op jit(solution)/shard_map/cond/branch_0_fun/all_to_all | solution.py:40
  44.5 35.7 %all_to_all.36 = bf16[32,72,256]{2,1,0:T(8,128)(2,1)S(1)} all-to-all(bf16[32,72,256]{2,1,0:T(8,128)(2,1)S(1)} %broadcast_in_dim.4), channel_id=1, replica_groups=mesh['z'=8,'y'=4,'c'=2,'h'=2,'x'=4] {'z','y'}, dimensions={0} | all-to-all | bytes 2359296 | tf_op jit(solution)/shard_map/all_to_all | solution.py:76
  80.2 1.9 %collective-permute-start.1 = (bf16[2304,256]{1,0:T(8,128)(2,1)S(1)}, bf16[2304,256]{1,0:T(8,128)(2,1)S(1)}, u32[]{:S(2)}, u32[]{:S(2)}) collective-permute-start(bf16[2304,256]{1,0:T(8,128)(2,1)S(1)} %bitcast.41), channel_id=1, source_target_pairs={{0,8},{8,0},{1,9},{9,1},{2,10},{10,2},{3,11},{11,3},{4,12},{12,4},... | collective-permute-start | bytes 3538952 | tf_op jit(solution)/shard_map/ppermute | solution.py:14
  82.7 2.2 %collective-permute-done.1 = bf16[2304,256]{1,0:T(8,128)(2,1)S(1)} collective-permute-done((bf16[2304,256]{1,0:T(8,128)(2,1)S(1)}, bf16[2304,256]{1,0:T(8,128)(2,1)S(1)}, u32[]{:S(2)}, u32[]{:S(2)}) %collective-permute-start.1) | collective-permute-done | bytes 1179680 | tf_op jit(solution)/shard_map/ppermute | solution.py:14
  85.0 1.3 fusion.4
  86.3 4.3 %all-to-all-start.3 = ((f32[4,104,256]{2,1,0:T(8,128)}), f32[4,104,256]{2,1,0:T(8,128)S(1)}, u32[]{:S(2)}, u32[]{:S(2)}) async-start(f32[4,104,256]{2,1,0:T(8,128)} %bitcast.45), calls=%async_computation.3 | async-start | bytes 851968 | tf_op jit(solution)/shard_map/all_to_all | solution.py:51
  90.6 1.4 %fusion.10 = f32[416,256]{1,0:T(8,128)S(1)} fusion(bf16[416,1024]{1,0:T(8,128)(2,1)} %param.9, s32[]{:T(128)S(6)} %mul.38, bf16[2304,256]{1,0:T(8,128)(2,1)} %bitcast.43), kind=kOutput, calls=%fused_computation.24 | convolution fusion | flops 109051904 | bytes 1114116 | tf_op jit(solution)/shard_map/dot_general | solution.py:47
  92.0 2.0 %convolution_add_fusion = f32[416,256]{1,0:T(8,128)} fusion(f32[416,256]{1,0:T(8,128)S(1)} %fusion.10, bf16[416,1024]{1,0:T(8,128)(2,1)S(1)} %copy-done.4, s32[]{:T(128)S(6)} %mul.39, bf16[2304,256]{1,0:T(8,128)(2,1)} %copy-done.5), kind=kOutput, calls=%fused_computation.15 | convolution fusion | flops 109158400 | bytes 1540100 | tf_op jit(solution)/shard_map/dot_general | solution.py:47
  94.1 5.3 %all-to-all-done.3 = f32[4,104,256]{2,1,0:T(8,128)S(1)} async-done(((f32[4,104,256]{2,1,0:T(8,128)}), f32[4,104,256]{2,1,0:T(8,128)S(1)}, u32[]{:S(2)}, u32[]{:S(2)}) %all-to-all-start.3) | async-done | bytes 426016 | tf_op jit(solution)/shard_map/all_to_all | solution.py:51
  99.3 4.1 %all-to-all-start.4 = ((f32[4,104,256]{2,1,0:T(8,128)}), f32[4,104,256]{2,1,0:T(8,128)}, u32[]{:S(2)}, u32[]{:S(2)}) async-start(f32[4,104,256]{2,1,0:T(8,128)} %bitcast.44), calls=%async_computation.4 | async-start | bytes 851968 | tf_op jit(solution)/shard_map/all_to_all | solution.py:51
  103.7 4.7 %collective-permute-start.2 = (f32[104,256]{1,0:T(8,128)S(1)}, f32[104,256]{1,0:T(8,128)S(1)}, u32[]{:S(2)}, u32[]{:S(2)}) collective-permute-start(f32[104,256]{1,0:T(8,128)S(1)} %reduce_sum.36), channel_id=1, source_target_pairs={{0,4},{4,0},{1,5},{5,1},{2,6},{6,2},{3,7},{7,3},{8,12},{12,8},{9,1... | collective-permute-start | bytes 319496 | tf_op jit(solution)/shard_map/ppermute | solution.py:14
  108.4 2.9 %all-to-all-done.4 = f32[4,104,256]{2,1,0:T(8,128)} async-done(((f32[4,104,256]{2,1,0:T(8,128)}), f32[4,104,256]{2,1,0:T(8,128)}, u32[]{:S(2)}, u32[]{:S(2)}) %all-to-all-start.4) | async-done | bytes 426016 | tf_op jit(solution)/shard_map/all_to_all | solution.py:51
  111.3 1.0 reduce_sum.37
  112.4 4.7 %collective-permute-start.3 = (f32[104,256]{1,0:T(8,128)S(1)}, f32[104,256]{1,0:T(8,128)S(1)}, u32[]{:S(2)}, u32[]{:S(2)}) collective-permute-start(f32[104,256]{1,0:T(8,128)S(1)} %reduce_sum.37), channel_id=1, source_target_pairs={{0,4},{4,0},{1,5},{5,1},{2,6},{6,2},{3,7},{7,3},{8,12},{12,8},{9,1... | collective-permute-start | bytes 319496 | tf_op jit(solution)/shard_map/ppermute | solution.py:14
  117.1 5.9 %collective-permute-done.3 = f32[104,256]{1,0:T(8,128)S(1)} collective-permute-done((f32[104,256]{1,0:T(8,128)S(1)}, f32[104,256]{1,0:T(8,128)S(1)}, u32[]{:S(2)}, u32[]{:S(2)}) %collective-permute-start.3) | collective-permute-done | bytes 106528 | tf_op jit(solution)/shard_map/ppermute | solution.py:14
  123.3 7.7 %all_to_all.37 = f32[4,8,8]{2,1,0:T(8,128)S(1)} all-to-all(f32[4,8,8]{2,1,0:T(8,128)S(1)} %broadcast_in_dim.5), channel_id=1, replica_groups=mesh['z'=8,'y'=4,'c'=2,'h'=2,'x'=4] {'x'}, dimensions={0} | all-to-all | bytes 2048 | tf_op jit(solution)/shard_map/all_to_all | solution.py:101
  (35 shorter events, 4.0 us)
Async XLA Ops:
  0.0 82.2 %copy-start = (bf16[416,3584]{1,0:T(8,128)(2,1)S(1)}, bf16[416,3584]{1,0:T(8,128)(2,1)}, u32[]{:S(2)}) copy-start(bf16[416,3584]{1,0:T(8,128)(2,1)} %param.8) | copy-start | bytes 8945668
  0.0 4.9 %copy-start.6 = (s32[2]{0:T(128)S(1)}, s32[2]{0:T(128)}, u32[]{:S(2)}) copy-start(s32[2]{0:T(128)} %param.13) | copy-start | bytes 28
  2.1 7.1 %copy-start.3 = (bf16[1,1024,128]{2,1,0:T(8,128)(2,1)S(1)}, bf16[1,1024,128]{2,1,0:T(8,128)(2,1)}, u32[]{:S(2)}) copy-start(bf16[1,1024,128]{2,1,0:T(8,128)(2,1)} %param.11) | copy-start | bytes 786436
  3.0 5.0 %collective-permute-start = (bf16[2304,128]{1,0:T(8,128)(2,1)}, bf16[2304,128]{1,0:T(8,128)(2,1)}, u32[]{:S(2)}, u32[]{:S(2)}) collective-permute-start(bf16[2304,128]{1,0:T(8,128)(2,1)} %pad_maximum_fusion.3), channel_id=1, source_target_pairs={{0,8},{8,0},{1,9},{9,1},{2,10},{10,2},{3,11},{11,3},{4,12},{12,4},... | collective-permute-start | bytes 1769480 | tf_op jit(solution)/shard_map/ppermute | solution.py:14
  10.3 0.8 copy-start.1
  11.1 32.6 %all-to-all-start = ((bf16[32,72,128]{2,1,0:T(8,128)(2,1)}), bf16[32,72,128]{2,1,0:T(8,128)(2,1)}, u32[]{:S(2)}, u32[]{:S(2)}) async-start(bf16[32,72,128]{2,1,0:T(8,128)(2,1)} %bitcast.40), calls=%async_computation | async-start | bytes 1179648 | tf_op jit(solution)/shard_map/cond/branch_0_fun/all_to_all | solution.py:40
  80.2 2.5 %copy-start.2 = (bf16[32,72,256]{2,1,0:T(8,128)(2,1)}, bf16[32,72,256]{2,1,0:T(8,128)(2,1)S(1)}, u32[]{:S(2)}) copy-start(bf16[32,72,256]{2,1,0:T(8,128)(2,1)S(1)} %all_to_all.36) | copy-start | bytes 3538948
  80.2 4.7 %collective-permute-start.1 = (bf16[2304,256]{1,0:T(8,128)(2,1)S(1)}, bf16[2304,256]{1,0:T(8,128)(2,1)S(1)}, u32[]{:S(2)}, u32[]{:S(2)}) collective-permute-start(bf16[2304,256]{1,0:T(8,128)(2,1)S(1)} %bitcast.41), channel_id=1, source_target_pairs={{0,8},{8,0},{1,9},{9,1},{2,10},{10,2},{3,11},{11,3},{4,12},{12,4},... | collective-permute-start | bytes 3538952 | tf_op jit(solution)/shard_map/ppermute | solution.py:14
  85.0 1.3 %copy-start.5 = (bf16[2304,256]{1,0:T(8,128)(2,1)}, bf16[2304,256]{1,0:T(8,128)(2,1)S(1)}, u32[]{:S(2)}) copy-start(bf16[2304,256]{1,0:T(8,128)(2,1)S(1)} %collective-permute-done.1) | copy-start | bytes 3538948
  86.3 13.0 %all-to-all-start.3 = ((f32[4,104,256]{2,1,0:T(8,128)}), f32[4,104,256]{2,1,0:T(8,128)S(1)}, u32[]{:S(2)}, u32[]{:S(2)}) async-start(f32[4,104,256]{2,1,0:T(8,128)} %bitcast.45), calls=%async_computation.3 | async-start | bytes 851968 | tf_op jit(solution)/shard_map/all_to_all | solution.py:51
  90.6 1.4 %copy-start.4 = (bf16[416,1024]{1,0:T(8,128)(2,1)S(1)}, bf16[416,1024]{1,0:T(8,128)(2,1)}, u32[]{:S(2)}) copy-start(bf16[416,1024]{1,0:T(8,128)(2,1)} %param.9) | copy-start | bytes 2555908
  92.0 11.4 %copy-start.7 = (s32[1,8]{1,0:T(1,128)S(1)}, s32[1,8]{1,0:T(1,128)}, u32[]{:S(2)}) copy-start(s32[1,8]{1,0:T(1,128)} %param.12) | copy-start | bytes 100
  99.3 12.0 %all-to-all-start.4 = ((f32[4,104,256]{2,1,0:T(8,128)}), f32[4,104,256]{2,1,0:T(8,128)}, u32[]{:S(2)}, u32[]{:S(2)}) async-start(f32[4,104,256]{2,1,0:T(8,128)} %bitcast.44), calls=%async_computation.4 | async-start | bytes 851968 | tf_op jit(solution)/shard_map/all_to_all | solution.py:51
  103.7 13.5 %collective-permute-start.2 = (f32[104,256]{1,0:T(8,128)S(1)}, f32[104,256]{1,0:T(8,128)S(1)}, u32[]{:S(2)}, u32[]{:S(2)}) collective-permute-start(f32[104,256]{1,0:T(8,128)S(1)} %reduce_sum.36), channel_id=1, source_target_pairs={{0,4},{4,0},{1,5},{5,1},{2,6},{6,2},{3,7},{7,3},{8,12},{12,8},{9,1... | collective-permute-start | bytes 319496 | tf_op jit(solution)/shard_map/ppermute | solution.py:14
  112.4 10.6 %collective-permute-start.3 = (f32[104,256]{1,0:T(8,128)S(1)}, f32[104,256]{1,0:T(8,128)S(1)}, u32[]{:S(2)}, u32[]{:S(2)}) collective-permute-start(f32[104,256]{1,0:T(8,128)S(1)} %reduce_sum.37), channel_id=1, source_target_pairs={{0,4},{4,0},{1,5},{5,1},{2,6},{6,2},{3,7},{7,3},{8,12},{12,8},{9,1... | collective-permute-start | bytes 319496 | tf_op jit(solution)/shard_map/ppermute | solution.py:14

commit v13 on v12

--- a/solution.py
+++ b/solution.py
@@ -22,15 +22,9 @@
     return jnp.concatenate([cut(got, source, 1, 0)[0] for source in sources], axis=1)
 
 
-def half(right, left, side):
+def scatter_cores(right, left, mine, owners):
     rows_r, rows_l = right.shape[0] // C, left.shape[0] // C
-    return jnp.concatenate(
-        [cut(right, side * rows_r, rows_r, 0), cut(left, side * rows_l, rows_l, 0)], axis=0
-    )
-
-
-def scatter_cores(right, left, mine, owners):
-    own = jnp.concatenate([half(right, left, side) for side in range(C)], axis=0)
+    own = jnp.concatenate([right[:rows_r], left[:rows_l], right[rows_r:], left[rows_l:]], axis=0)
     own = own.reshape(Z * Y * C, -1, COLS)
     got = lax.all_to_all(own, ("c", "z", "y"), 0, 0, tiled=True)
     return pick(got, [(owner & 1) * (Z * Y) + (owner >> 1) for owner in owners])
@@ -61,12 +55,13 @@
     right, left = right_factors[0], left_factors[0]
     rows_r = right.shape[0] // C
     owner = owners[0], owners[1]
-    far = swap(half(right, left, 1 - core), "c")
+    rows_l = left.shape[0] // C
+    far_l = swap(cut(left, (1 - core) * rows_l, rows_l, 0), "c")
+    far_r = swap(cut(right, (1 - core) * rows_r, rows_r, 0), "c")
     wanted = (owner[0] == device) | (owner[1] == device)
-    rows_l = left.shape[0] // C
     near_r, near_l = cut(right, core * rows_r, rows_r, 0), cut(left, core * rows_l, rows_l, 0)
     mine = jnp.concatenate(
-        [jnp.where(wanted, near_r, far[:rows_r]), jnp.where(wanted, near_l, far[rows_r:])], axis=0
+        [jnp.where(wanted, near_r, far_r), jnp.where(wanted, near_l, far_l)], axis=0
     )
     picked = lax.cond(
         owner[0] ^ owner[1] == 1, scatter_cores, scatter_chips, right, left, mine, owner

time: 134 us -> 136 us (1.015)
  the two profiles are of different devices: /device:TPU:56 before, /device:TPU:8 now
where the time goes in v13:
time: 136 us; the launch traced here: 135 us
  blocking collectives  44.3 us (33%)
  starting transfers between devices  38.7 us (28%)
  waiting for transfers between devices  33.5 us (25%)
  matrix products  5.49 us (4%)
  local copies, waits for them, and re-layouts  5.25 us (4%)
  other arithmetic  3.3 us (2%)
  between operations  2.94 us (2%)
  loops' own time  1.37 us (1%)
    all_to_all x1, blocking collectives, shards(): lax.all_to_all(copies, ('z', 'y'), 0, 0, tiled=True).reshape(-1, 2 * COLS)  36.6 us
    all_to_all x1, waiting for transfers between devices, scatter_chips(): lax.all_to_all(mine.reshape(Z * Y, -1, COLS), ('z', 'y'), 0, 0, tiled=True)  16.8 us
    ppermute x5, starting transfers between devices, swap(): return lax.ppermute(block, axis, [(0, 1), (1, 0)])  16.3 us
    all_to_all x1, starting transfers between devices, scatter_chips(): lax.all_to_all(mine.reshape(Z * Y, -1, COLS), ('z', 'y'), 0, 0, tiled=True)  14 us
    ppermute x5, waiting for transfers between devices, swap(): return lax.ppermute(block, axis, [(0, 1), (1, 0)])  8.82 us
    all_to_all x2, starting transfers between devices, sum_x(): parts = lax.all_to_all(proj, 'x', 0, 0, tiled=True)  8.42 us
    all_to_all x2, waiting for transfers between devices, sum_x(): parts = lax.all_to_all(proj, 'x', 0, 0, tiled=True)  7.9 us
    all_to_all x1, blocking collectives, shards(): summed = lax.all_to_all(copies, 'x', 0, 0, tiled=True).sum(axis=0)  7.71 us
  transfers between devices with their start and end apart: 8, of which 5 were waited for; matrix products, arithmetic and copies ran while one was open for 5% of the time, Pallas kernels for 0%

profile of v13, /device:TPU:8, one launch (start us, length us, event | category | flops | bytes accessed | tf_op | source)
XLA Modules:
  0.0 134.9 jit_solution(8335817600962479502)
XLA Ops:
  0.0 2.0 %dynamic-slice_bitcast_fusion.4 = bf16[1792,128]{1,0:T(8,128)(2,1)} fusion(bf16[1,3584,128]{2,1,0:T(8,128)(2,1)} %param.10, s32[]{:T(128)S(6)} %mul.40), kind=kLoop, calls=%fused_computation.21 | loop fusion | bytes 917508 | tf_op jit(solution)/shard_map/dynamic_slice | solution.py:18
  2.0 1.9 %collective-permute-start.1 = (bf16[1792,128]{1,0:T(8,128)(2,1)}, bf16[1792,128]{1,0:T(8,128)(2,1)}, u32[]{:S(2)}, u32[]{:S(2)}) collective-permute-start(bf16[1792,128]{1,0:T(8,128)(2,1)} %dynamic-slice_bitcast_fusion.4), channel_id=1, source_target_pairs={{0,8},{8,0},{1,9},{9,1},{2,10},{10,2},{3,11},{11,3},{4,12},{12,4},... | collective-permute-start | bytes 1376264 | tf_op jit(solution)/shard_map/ppermute | solution.py:14
  3.9 0.9 dynamic-slice_bitcast_fusion.5
  4.8 2.4 %collective-permute-start = (bf16[512,128]{1,0:T(8,128)(2,1)S(1)}, bf16[512,128]{1,0:T(8,128)(2,1)S(1)}, u32[]{:S(2)}, u32[]{:S(2)}) collective-permute-start(bf16[512,128]{1,0:T(8,128)(2,1)S(1)} %dynamic-slice_bitcast_fusion.5), channel_id=1, source_target_pairs={{0,8},{8,0},{1,9},{9,1},{2,10},{10,2},{3,11},{11,3},{4,12},{12,4},... | collective-permute-start | bytes 393224 | tf_op jit(solution)/shard_map/ppermute | solution.py:14
  10.6 1.3 bitcast_select_fusion
  12.0 33.8 %conditional.1 = (bf16[72,256]{1,0:T(8,128)(2,1)S(1)}) conditional(s32[]{:T(128)} %convert_element_type.4, (bf16[2304,128]{1,0:T(8,128)(2,1)S(1)}, s32[]{:T(128)}, s32[]{:T(128)}) %tuple.11, (bf16[1,1024,128]{2,1,0:T(8,128)(2,1)S(1)}, bf16[1,3584,128]{2,1,0:T(8,128)(2,1)}, s32[]{:T(128)}, s32[]{:T(128)}) %tuple.20), branch_computations={%region_1.2_spmd, %region_2.3_spmd} | conditional | flops 4792328 | bytes 8405136 | solution.py:66
  12.0 0.8 copy-done.1
  12.8 14.0 %all-to-all-start = ((bf16[32,72,128]{2,1,0:T(8,128)(2,1)}), bf16[32,72,128]{2,1,0:T(8,128)(2,1)}, u32[]{:S(2)}, u32[]{:S(2)}) async-start(bf16[32,72,128]{2,1,0:T(8,128)(2,1)} %bitcast.40), calls=%async_computation | async-start | bytes 1179648 | tf_op jit(solution)/shard_map/cond/branch_0_fun/all_to_all | solution.py:34
  28.2 16.8 %all-to-all-done = bf16[32,72,128]{2,1,0:T(8,128)(2,1)} async-done(((bf16[32,72,128]{2,1,0:T(8,128)(2,1)}), bf16[32,72,128]{2,1,0:T(8,128)(2,1)}, u32[]{:S(2)}, u32[]{:S(2)}) %all-to-all-start) | async-done | bytes 589856 | tf_op jit(solution)/shard_map/cond/branch_0_fun/all_to_all | solution.py:34
  45.8 36.6 %all_to_all.36 = bf16[32,72,256]{2,1,0:T(8,128)(2,1)S(1)} all-to-all(bf16[32,72,256]{2,1,0:T(8,128)(2,1)S(1)} %broadcast_in_dim.4), channel_id=1, replica_groups=mesh['z'=8,'y'=4,'c'=2,'h'=2,'x'=4] {'z','y'}, dimensions={0} | all-to-all | bytes 2359296 | tf_op jit(solution)/shard_map/all_to_all | solution.py:71
  82.4 1.9 %collective-permute-start.2 = (bf16[2304,256]{1,0:T(8,128)(2,1)S(1)}, bf16[2304,256]{1,0:T(8,128)(2,1)S(1)}, u32[]{:S(2)}, u32[]{:S(2)}) collective-permute-start(bf16[2304,256]{1,0:T(8,128)(2,1)S(1)} %bitcast.41), channel_id=1, source_target_pairs={{0,8},{8,0},{1,9},{9,1},{2,10},{10,2},{3,11},{11,3},{4,12},{12,4},... | collective-permute-start | bytes 3538952 | tf_op jit(solution)/shard_map/ppermute | solution.py:14
  84.9 2.2 %collective-permute-done.2 = bf16[2304,256]{1,0:T(8,128)(2,1)S(1)} collective-permute-done((bf16[2304,256]{1,0:T(8,128)(2,1)S(1)}, bf16[2304,256]{1,0:T(8,128)(2,1)S(1)}, u32[]{:S(2)}, u32[]{:S(2)}) %collective-permute-start.2) | collective-permute-done | bytes 1179680 | tf_op jit(solution)/shard_map/ppermute | solution.py:14
  87.2 1.3 fusion.4
  88.5 4.3 %all-to-all-start.3 = ((f32[4,104,256]{2,1,0:T(8,128)}), f32[4,104,256]{2,1,0:T(8,128)S(1)}, u32[]{:S(2)}, u32[]{:S(2)}) async-start(f32[4,104,256]{2,1,0:T(8,128)} %bitcast.45), calls=%async_computation.3 | async-start | bytes 851968 | tf_op jit(solution)/shard_map/all_to_all | solution.py:45
  92.8 1.4 %fusion.10 = f32[416,256]{1,0:T(8,128)S(1)} fusion(bf16[416,1024]{1,0:T(8,128)(2,1)} %param.9, s32[]{:T(128)S(6)} %mul.38, bf16[2304,256]{1,0:T(8,128)(2,1)} %bitcast.43), kind=kOutput, calls=%fused_computation.23 | convolution fusion | flops 109051904 | bytes 1114116 | tf_op jit(solution)/shard_map/dot_general | solution.py:41
  94.2 2.0 %convolution_add_fusion = f32[416,256]{1,0:T(8,128)} fusion(f32[416,256]{1,0:T(8,128)S(1)} %fusion.10, bf16[416,1024]{1,0:T(8,128)(2,1)S(1)} %copy-done.4, s32[]{:T(128)S(6)} %mul.39, bf16[2304,256]{1,0:T(8,128)(2,1)} %copy-done.5), kind=kOutput, calls=%fused_computation.15 | convolution fusion | flops 109158400 | bytes 1540100 | tf_op jit(solution)/shard_map/dot_general | solution.py:41
  96.3 5.3 %all-to-all-done.3 = f32[4,104,256]{2,1,0:T(8,128)S(1)} async-done(((f32[4,104,256]{2,1,0:T(8,128)}), f32[4,104,256]{2,1,0:T(8,128)S(1)}, u32[]{:S(2)}, u32[]{:S(2)}) %all-to-all-start.3) | async-done | bytes 426016 | tf_op jit(solution)/shard_map/all_to_all | solution.py:45
  101.5 4.1 %all-to-all-start.4 = ((f32[4,104,256]{2,1,0:T(8,128)}), f32[4,104,256]{2,1,0:T(8,128)}, u32[]{:S(2)}, u32[]{:S(2)}) async-start(f32[4,104,256]{2,1,0:T(8,128)} %bitcast.44), calls=%async_computation.4 | async-start | bytes 851968 | tf_op jit(solution)/shard_map/all_to_all | solution.py:45
  105.9 5.0 %collective-permute-start.3 = (f32[104,256]{1,0:T(8,128)S(1)}, f32[104,256]{1,0:T(8,128)S(1)}, u32[]{:S(2)}, u32[]{:S(2)}) collective-permute-start(f32[104,256]{1,0:T(8,128)S(1)} %reduce_sum.36), channel_id=1, source_target_pairs={{0,4},{4,0},{1,5},{5,1},{2,6},{6,2},{3,7},{7,3},{8,12},{12,8},{9,1... | collective-permute-start | bytes 319496 | tf_op jit(solution)/shard_map/ppermute | solution.py:14
  110.9 2.6 %all-to-all-done.4 = f32[4,104,256]{2,1,0:T(8,128)} async-done(((f32[4,104,256]{2,1,0:T(8,128)}), f32[4,104,256]{2,1,0:T(8,128)}, u32[]{:S(2)}, u32[]{:S(2)}) %all-to-all-start.4) | async-done | bytes 426016 | tf_op jit(solution)/shard_map/all_to_all | solution.py:45
  113.6 1.0 reduce_sum.37
  114.6 5.0 %collective-permute-start.4 = (f32[104,256]{1,0:T(8,128)S(1)}, f32[104,256]{1,0:T(8,128)S(1)}, u32[]{:S(2)}, u32[]{:S(2)}) collective-permute-start(f32[104,256]{1,0:T(8,128)S(1)} %reduce_sum.37), channel_id=1, source_target_pairs={{0,4},{4,0},{1,5},{5,1},{2,6},{6,2},{3,7},{7,3},{8,12},{12,8},{9,1... | collective-permute-start | bytes 319496 | tf_op jit(solution)/shard_map/ppermute | solution.py:14
  119.7 6.6 %collective-permute-done.4 = f32[104,256]{1,0:T(8,128)S(1)} collective-permute-done((f32[104,256]{1,0:T(8,128)S(1)}, f32[104,256]{1,0:T(8,128)S(1)}, u32[]{:S(2)}, u32[]{:S(2)}) %collective-permute-start.4) | collective-permute-done | bytes 106528 | tf_op jit(solution)/shard_map/ppermute | solution.py:14
  126.6 7.7 %all_to_all.37 = f32[4,8,8]{2,1,0:T(8,128)S(1)} all-to-all(f32[4,8,8]{2,1,0:T(8,128)S(1)} %broadcast_in_dim.5), channel_id=1, replica_groups=mesh['z'=8,'y'=4,'c'=2,'h'=2,'x'=4] {'x'}, dimensions={0} | all-to-all | bytes 2048 | tf_op jit(solution)/shard_map/all_to_all | solution.py:96
  (36 shorter events, 3.3 us)
Async XLA Ops:
  0.0 84.4 %copy-start = (bf16[416,3584]{1,0:T(8,128)(2,1)S(1)}, bf16[416,3584]{1,0:T(8,128)(2,1)}, u32[]{:S(2)}) copy-start(bf16[416,3584]{1,0:T(8,128)(2,1)} %param.8) | copy-start | bytes 8945668
  0.0 10.6 %copy-start.3 = (bf16[1,1024,128]{2,1,0:T(8,128)(2,1)S(1)}, bf16[1,1024,128]{2,1,0:T(8,128)(2,1)}, u32[]{:S(2)}) copy-start(bf16[1,1024,128]{2,1,0:T(8,128)(2,1)} %param.11) | copy-start | bytes 786436
  0.0 7.3 %copy-start.6 = (s32[2]{0:T(128)S(1)}, s32[2]{0:T(128)}, u32[]{:S(2)}) copy-start(s32[2]{0:T(128)} %param.13) | copy-start | bytes 28
  2.0 8.6 %collective-permute-start.1 = (bf16[1792,128]{1,0:T(8,128)(2,1)}, bf16[1792,128]{1,0:T(8,128)(2,1)}, u32[]{:S(2)}, u32[]{:S(2)}) collective-permute-start(bf16[1792,128]{1,0:T(8,128)(2,1)} %dynamic-slice_bitcast_fusion.4), channel_id=1, source_target_pairs={{0,8},{8,0},{1,9},{9,1},{2,10},{10,2},{3,11},{11,3},{4,12},{12,4},... | collective-permute-start | bytes 1376264 | tf_op jit(solution)/shard_map/ppermute | solution.py:14
  4.8 5.7 %collective-permute-start = (bf16[512,128]{1,0:T(8,128)(2,1)S(1)}, bf16[512,128]{1,0:T(8,128)(2,1)S(1)}, u32[]{:S(2)}, u32[]{:S(2)}) collective-permute-start(bf16[512,128]{1,0:T(8,128)(2,1)S(1)} %dynamic-slice_bitcast_fusion.5), channel_id=1, source_target_pairs={{0,8},{8,0},{1,9},{9,1},{2,10},{10,2},{3,11},{11,3},{4,12},{12,4},... | collective-permute-start | bytes 393224 | tf_op jit(solution)/shard_map/ppermute | solution.py:14
  12.0 0.8 copy-start.1
  12.8 32.2 %all-to-all-start = ((bf16[32,72,128]{2,1,0:T(8,128)(2,1)}), bf16[32,72,128]{2,1,0:T(8,128)(2,1)}, u32[]{:S(2)}, u32[]{:S(2)}) async-start(bf16[32,72,128]{2,1,0:T(8,128)(2,1)} %bitcast.40), calls=%async_computation | async-start | bytes 1179648 | tf_op jit(solution)/shard_map/cond/branch_0_fun/all_to_all | solution.py:34
  82.4 2.5 %copy-start.2 = (bf16[32,72,256]{2,1,0:T(8,128)(2,1)}, bf16[32,72,256]{2,1,0:T(8,128)(2,1)S(1)}, u32[]{:S(2)}) copy-start(bf16[32,72,256]{2,1,0:T(8,128)(2,1)S(1)} %all_to_all.36) | copy-start | bytes 3538948
  82.4 4.7 %collective-permute-start.2 = (bf16[2304,256]{1,0:T(8,128)(2,1)S(1)}, bf16[2304,256]{1,0:T(8,128)(2,1)S(1)}, u32[]{:S(2)}, u32[]{:S(2)}) collective-permute-start(bf16[2304,256]{1,0:T(8,128)(2,1)S(1)} %bitcast.41), channel_id=1, source_target_pairs={{0,8},{8,0},{1,9},{9,1},{2,10},{10,2},{3,11},{11,3},{4,12},{12,4},... | collective-permute-start | bytes 3538952 | tf_op jit(solution)/shard_map/ppermute | solution.py:14
  87.2 1.3 copy-start.5
  88.5 13.0 %all-to-all-start.3 = ((f32[4,104,256]{2,1,0:T(8,128)}), f32[4,104,256]{2,1,0:T(8,128)S(1)}, u32[]{:S(2)}, u32[]{:S(2)}) async-start(f32[4,104,256]{2,1,0:T(8,128)} %bitcast.45), calls=%async_computation.3 | async-start | bytes 851968 | tf_op jit(solution)/shard_map/all_to_all | solution.py:45
  92.8 1.4 %copy-start.4 = (bf16[416,1024]{1,0:T(8,128)(2,1)S(1)}, bf16[416,1024]{1,0:T(8,128)(2,1)}, u32[]{:S(2)}) copy-start(bf16[416,1024]{1,0:T(8,128)(2,1)} %param.9) | copy-start | bytes 2555908
  94.2 11.4 %copy-start.7 = (s32[1,8]{1,0:T(1,128)S(1)}, s32[1,8]{1,0:T(1,128)}, u32[]{:S(2)}) copy-start(s32[1,8]{1,0:T(1,128)} %param.12) | copy-start | bytes 100
  101.5 12.1 %all-to-all-start.4 = ((f32[4,104,256]{2,1,0:T(8,128)}), f32[4,104,256]{2,1,0:T(8,128)}, u32[]{:S(2)}, u32[]{:S(2)}) async-start(f32[4,104,256]{2,1,0:T(8,128)} %bitcast.44), calls=%async_computation.4 | async-start | bytes 851968 | tf_op jit(solution)/shard_map/all_to_all | solution.py:45
  105.9 13.8 %collective-permute-start.3 = (f32[104,256]{1,0:T(8,128)S(1)}, f32[104,256]{1,0:T(8,128)S(1)}, u32[]{:S(2)}, u32[]{:S(2)}) collective-permute-start(f32[104,256]{1,0:T(8,128)S(1)} %reduce_sum.36), channel_id=1, source_target_pairs={{0,4},{4,0},{1,5},{5,1},{2,6},{6,2},{3,7},{7,3},{8,12},{12,8},{9,1... | collective-permute-start | bytes 319496 | tf_op jit(solution)/shard_map/ppermute | solution.py:14
  114.6 11.6 %collective-permute-start.4 = (f32[104,256]{1,0:T(8,128)S(1)}, f32[104,256]{1,0:T(8,128)S(1)}, u32[]{:S(2)}, u32[]{:S(2)}) collective-permute-start(f32[104,256]{1,0:T(8,128)S(1)} %reduce_sum.37), channel_id=1, source_target_pairs={{0,4},{4,0},{1,5},{5,1},{2,6},{6,2},{3,7},{7,3},{8,12},{12,8},{9,1... | collective-permute-start | bytes 319496 | tf_op jit(solution)/shard_map/ppermute | solution.py:14
